TPU v7x, 32 devices: a whole 2x2x4 slice. The times are simulated.
32 devices in a mesh: dp: 4 (over y, core), seq: 8 (over z, x).
Axes of the slice: x: 2, y: 2, z: 4, core: 2. Of those that a mesh axis runs over, the one named last changes fastest.
Arguments:
- tokens: bfloat16 [4, 8192, 1152], P('dp', 'seq'), may hold values from -6 to 6
- segments: int32 [4, 8192], P('dp', 'seq'), may hold values from 0 to 63, as said below
- condition: bfloat16 [4, 64, 1152], P('dp'), may hold values from -6 to 6
- cotangent: bfloat16 [4, 8192, 1152], P('dp', 'seq'), may hold values from -6 to 6
- modulation_weight: bfloat16 [1152, 6912], P('dp'), may hold values from -0.1875 to 0.1875
- modulation_bias: bfloat16 [6912], replicated, may hold values from -1.796875 to 1.796875
- input_weight: bfloat16 [1152, 3456], P('dp'), may hold values from -0.1875 to 0.1875
- query_value_bias: bfloat16 [2304], replicated, may hold values from -1.796875 to 1.796875
- output_weight: bfloat16 [1152, 1152], P('dp'), may hold values from -2 to 2
- output_bias: bfloat16 [1152], replicated, may hold values from -1.796875 to 1.796875
- expand_weight: bfloat16 [1152, 4608], P('dp'), may hold values from -0.1875 to 0.1875
- expand_bias: bfloat16 [4608], replicated, may hold values from -1.796875 to 1.796875
- contract_weight: bfloat16 [4608, 1152], P('dp'), may hold values from -0.09375 to 0.09375
- contract_bias: bfloat16 [1152], replicated, may hold values from -1.796875 to 1.796875
Outputs:
- layer_out: bfloat16 [4, 8192, 1152], P('dp', 'seq')
- grad_tokens: float32 [4, 8192, 1152], P('dp', 'seq')
- grad_condition: float32 [4, 64, 1152], P('dp', 'seq')
- grad_modulation_weight: float32 [1152, 6912], P('dp', 'seq')
- grad_modulation_bias: float32 [6912], replicated
- grad_input_weight: float32 [1152, 3456], P('dp', 'seq')
- grad_query_value_bias: float32 [2304], replicated
- grad_output_weight: float32 [1152, 1152], P('dp', 'seq')
- grad_output_bias: float32 [1152], replicated
- grad_expand_weight: float32 [1152, 4608], P('dp', 'seq')
- grad_expand_bias: float32 [4608], replicated
- grad_contract_weight: float32 [4608, 1152], P('dp', 'seq')
- grad_contract_bias: float32 [1152], replicated
Inputs may be any that keep to these rules, and one draw needn't show every extreme that they name: `segments`: in each group the rows run through images 0 to 63 in order, each image one contiguous run of 64 to 192 rows; in every group some image has exactly 192 rows.
All inputs are finite; a program needn't handle non-finite values.
Results may differ from a plain program's by a relative error of at most 0.012.
The roundings to bfloat16 on the way count: a program that leaves them out, or rounds other values in their place, can miss the bound.
Values may be sent and summed in bfloat16 or wider, within the bound.
No kernel may reach another device: no remote copies, remote signals or barrier semaphores. Data moves between devices by JAX's collectives and lax.ppermute only.
A program may use at most 448 MiB of HBM per device.

v0:
```python
from functools import partial
import math

import jax
import jax.numpy as jnp
from jax import lax
from jax.sharding import PartitionSpec as P

HEADS = 16
MAXLEN = 192
WIN = 18


epsilon = 1e-06
highest = lax.Precision.HIGHEST


def padded(block, sides, width):
    for axis, dim in sides:
        count = lax.axis_size(axis)
        forward = [(i, i + 1) for i in range(count - 1)]
        backward = [(target, source) for source, target in forward]
        low = lax.ppermute(
            lax.slice_in_dim(block, block.shape[dim] - width, None, axis=dim), axis, forward
        )
        high = lax.ppermute(lax.slice_in_dim(block, 0, width, axis=dim), axis, backward)
        block = jnp.concatenate([low, block, high], axis=dim)
    return block


def from_behind(block, axis, distance):
    devices = range(lax.axis_size(axis))
    route = [(i - distance, i) for i in devices if i - distance in devices]
    return lax.ppermute(block, axis, route)


def layer_norm(token_rows):
    centred = token_rows - jnp.mean(token_rows, axis=-1, keepdims=True)
    inverse = lax.rsqrt(jnp.mean(centred * centred, axis=-1, keepdims=True) + epsilon)
    return (centred * inverse, inverse)


def norm_back(upstream, normed, inverse):
    return inverse * (
        upstream
        - jnp.mean(upstream, axis=-1, keepdims=True)
        - normed * jnp.mean(upstream * normed, axis=-1, keepdims=True)
    )


def outer_sum(first_matrix, second_matrix):
    return lax.dot_general(
        first_matrix, second_matrix, (((0,), (0,)), ((), ())), preferred_element_type=jnp.float32
    )


def back_dot(gradient, matrix):
    return lax.dot_general(
        gradient, matrix, (((1,), (1,)), ((), ())), preferred_element_type=jnp.float32
    )


def shards(
    tokens,
    segments,
    condition,
    cotangent,
    modulation_weight,
    modulation_bias,
    input_weight,
    query_value_bias,
    output_weight,
    output_bias,
    expand_weight,
    expand_bias,
    contract_weight,
    contract_bias,
):
    modulation_full, input_full, output_full, expand_full, contract_full = (
        lax.all_gather(modulation_weight, "dp", axis=0, tiled=True),
        lax.all_gather(input_weight, "dp", axis=0, tiled=True),
        lax.all_gather(output_weight, "dp", axis=0, tiled=True),
        lax.all_gather(expand_weight, "dp", axis=0, tiled=True),
        lax.all_gather(contract_weight, "dp", axis=0, tiled=True),
    )
    token_rows = tokens[0].astype(jnp.float32)
    segment = segments[0]
    conditions = condition[0]
    grad_out = cotangent[0].astype(jnp.float32)
    row_count, model_width = token_rows.shape
    images = conditions.shape[0]
    head_dim = model_width // HEADS
    score_scale = 1.0 / math.sqrt(head_dim)
    first_image = jnp.minimum(segment[0], images - WIN)
    window = lax.dynamic_slice_in_dim(conditions, first_image, WIN, 0).astype(jnp.float32)
    image_select = (
        (segment - first_image)[:, None] == jnp.arange(WIN, dtype=jnp.int32)[None, :]
    ).astype(jnp.float32)
    silu_window, silu_back = jax.vjp(jax.nn.silu, window)
    silu_low = silu_window.astype(jnp.bfloat16)
    modulation = jnp.dot(
        silu_low, modulation_full, preferred_element_type=jnp.float32
    ) + modulation_bias.astype(jnp.float32)
    per_row = jnp.dot(image_select, modulation, precision=highest)
    shift_mixer, scale_mixer, gate_mixer, shift_feed, scale_feed, gate_feed = jnp.split(
        per_row, 6, axis=1
    )
    normed_attn, inverse_attn = layer_norm(token_rows)
    input_attn = (normed_attn * (1.0 + scale_mixer) + shift_mixer).astype(jnp.bfloat16)
    packed = jnp.dot(input_attn, input_full, preferred_element_type=jnp.float32)
    bias_values = query_value_bias.astype(jnp.float32)
    queries = (packed[:, :model_width] + bias_values[:model_width]).astype(jnp.bfloat16)
    key_rows = packed[:, model_width : 2 * model_width].astype(jnp.bfloat16)
    values = (packed[:, 2 * model_width :] + bias_values[model_width:]).astype(jnp.bfloat16)
    key_value = jnp.concatenate([key_rows, values], axis=1)
    marker = segment + 1
    wide_pairs, wide_marker = (
        padded(key_value, (("seq", 0),), MAXLEN),
        padded(marker, (("seq", 0),), MAXLEN),
    )
    block_rows = min(512, row_count)
    block_count = row_count // block_rows
    window_rows = block_rows + 2 * MAXLEN
    query_heads = queries.reshape(block_count, block_rows, HEADS, head_dim)

    def block_scores(block_index):
        block_start = block_index * block_rows
        pair_window = lax.dynamic_slice_in_dim(wide_pairs, block_start, window_rows, 0)
        mark_window = lax.dynamic_slice_in_dim(wide_marker, block_start, window_rows, 0)
        own_marker = lax.dynamic_slice_in_dim(marker, block_start, block_rows, 0)
        key_heads = pair_window[:, :model_width].reshape(window_rows, HEADS, head_dim)
        value_heads = pair_window[:, model_width:].reshape(window_rows, HEADS, head_dim)
        raw_scores = (
            jnp.einsum(
                "qhd,khd->hqk",
                query_heads[block_index],
                key_heads,
                preferred_element_type=jnp.float32,
            )
            * score_scale
        )
        matching = (own_marker[:, None] == mark_window[None, :])[None]
        return (jnp.where(matching, raw_scores, -1e30), key_heads, value_heads)

    def forward_block(block_index):
        masked, key_heads, value_heads = block_scores(block_index)
        row_peak = jnp.max(masked, axis=-1, keepdims=True)
        exponent = jnp.exp(masked - row_peak)
        row_total = jnp.sum(exponent, axis=-1, keepdims=True)
        probability = (exponent / row_total).astype(jnp.bfloat16)
        mixed_block = jnp.einsum(
            "hqk,khd->qhd", probability, value_heads, preferred_element_type=jnp.float32
        )
        return (mixed_block.reshape(block_rows, model_width), row_peak, row_total)

    mixed_blocks, row_peaks, row_totals = lax.map(
        forward_block, jnp.arange(block_count, dtype=jnp.int32)
    )
    attn_mixed = mixed_blocks.reshape(row_count, model_width).astype(jnp.bfloat16)
    attn_out = jnp.dot(
        attn_mixed, output_full, preferred_element_type=jnp.float32
    ) + output_bias.astype(jnp.float32)
    middle = token_rows + gate_mixer * attn_out
    normed_feed, inverse_feed = layer_norm(middle)
    input_feed = (normed_feed * (1.0 + scale_feed) + shift_feed).astype(jnp.bfloat16)
    hidden = jnp.dot(
        input_feed, expand_full, preferred_element_type=jnp.float32
    ) + expand_bias.astype(jnp.float32)
    active, gelu_back = jax.vjp(partial(jax.nn.gelu, approximate=True), hidden)
    active_low = active.astype(jnp.bfloat16)
    feed_out = jnp.dot(
        active_low, contract_full, preferred_element_type=jnp.float32
    ) + contract_bias.astype(jnp.float32)
    layer_out = (middle + gate_feed * feed_out).astype(jnp.bfloat16)
    grad_feed = (grad_out * gate_feed).astype(jnp.bfloat16)
    grad_gate_feed = grad_out * feed_out
    grad_contract_weight = outer_sum(active_low, grad_feed)
    grad_contract_bias = jnp.sum(grad_feed.astype(jnp.float32), axis=0)
    grad_active = back_dot(grad_feed, contract_full)
    grad_hidden = gelu_back(grad_active)[0].astype(jnp.bfloat16)
    grad_expand_weight = outer_sum(input_feed, grad_hidden)
    grad_expand_bias = jnp.sum(grad_hidden.astype(jnp.float32), axis=0)
    grad_input_feed = back_dot(grad_hidden, expand_full)
    grad_scale_feed = grad_input_feed * normed_feed
    grad_middle = grad_out + norm_back(
        grad_input_feed * (1.0 + scale_feed), normed_feed, inverse_feed
    )
    grad_gate_mixer = grad_middle * attn_out
    grad_attn = (grad_middle * gate_mixer).astype(jnp.bfloat16)
    grad_output_weight = outer_sum(attn_mixed, grad_attn)
    grad_output_bias = jnp.sum(grad_attn.astype(jnp.float32), axis=0)
    grad_mixed = back_dot(grad_attn, output_full).astype(jnp.bfloat16)
    grad_mixed_heads = grad_mixed.reshape(block_count, block_rows, HEADS, head_dim)

    def backward_block(wide_carry, block_index):
        masked, key_heads, value_heads = block_scores(block_index)
        probability = jnp.exp(masked - row_peaks[block_index]) / row_totals[block_index]
        probability_low = probability.astype(jnp.bfloat16)
        grad_here = grad_mixed_heads[block_index]
        grad_probability = jnp.einsum(
            "qhd,khd->hqk", grad_here, value_heads, preferred_element_type=jnp.float32
        )
        grad_scores = (
            probability
            * (grad_probability - jnp.sum(probability * grad_probability, axis=-1, keepdims=True))
        ).astype(jnp.bfloat16)
        grad_query = (
            jnp.einsum("hqk,khd->qhd", grad_scores, key_heads, preferred_element_type=jnp.float32)
            * score_scale
        )
        grad_key = (
            jnp.einsum(
                "hqk,qhd->khd",
                grad_scores,
                query_heads[block_index],
                preferred_element_type=jnp.float32,
            )
            * score_scale
        )
        grad_value = jnp.einsum(
            "hqk,qhd->khd", probability_low, grad_here, preferred_element_type=jnp.float32
        )
        update = jnp.concatenate(
            [
                grad_key.reshape(window_rows, model_width),
                grad_value.reshape(window_rows, model_width),
            ],
            axis=1,
        )
        block_start = block_index * block_rows
        current = lax.dynamic_slice_in_dim(wide_carry, block_start, window_rows, 0)
        wide_carry = lax.dynamic_update_slice_in_dim(wide_carry, current + update, block_start, 0)
        return (wide_carry, grad_query.reshape(block_rows, model_width))

    wide_grad, grad_query_blocks = lax.scan(
        backward_block,
        jnp.zeros((row_count + 2 * MAXLEN, 2 * model_width), jnp.float32),
        jnp.arange(block_count, dtype=jnp.int32),
    )
    lower_rim = wide_grad[:MAXLEN]
    upper_rim = wide_grad[row_count + MAXLEN :]
    from_next = from_behind(lower_rim.astype(jnp.bfloat16), "seq", -1).astype(lower_rim.dtype)
    from_prev = from_behind(upper_rim, "seq", 1)
    own_grad = (
        wide_grad[MAXLEN : MAXLEN + row_count]
        + jnp.pad(from_prev, ((0, row_count - MAXLEN), (0, 0)))
        + jnp.pad(from_next, ((row_count - MAXLEN, 0), (0, 0)))
    )
    grad_packed = jnp.concatenate(
        [grad_query_blocks.reshape(row_count, model_width), own_grad], axis=1
    ).astype(jnp.bfloat16)
    grad_input_weight = outer_sum(input_attn, grad_packed)
    packed_sums = jnp.sum(grad_packed.astype(jnp.float32), axis=0)
    grad_query_value_bias = jnp.concatenate(
        [packed_sums[:model_width], packed_sums[2 * model_width :]]
    )
    grad_input_attn = back_dot(grad_packed, input_full)
    grad_scale_mixer = grad_input_attn * normed_attn
    grad_rows = grad_middle + norm_back(
        grad_input_attn * (1.0 + scale_mixer), normed_attn, inverse_attn
    )
    grad_per_row = jnp.concatenate(
        [
            grad_input_attn,
            grad_scale_mixer,
            grad_gate_mixer,
            grad_input_feed,
            grad_scale_feed,
            grad_gate_feed,
        ],
        axis=1,
    )
    grad_modulation = lax.dot_general(
        image_select, grad_per_row, (((0,), (0,)), ((), ())), precision=highest
    )
    grad_modulation_weight = jnp.dot(
        silu_low.astype(jnp.float32).T, grad_modulation, precision=highest
    )
    grad_modulation_bias = jnp.sum(grad_modulation, axis=0)
    grad_window = silu_back(jnp.dot(grad_modulation, modulation_full.T, precision=highest))[0]
    grad_condition_local = lax.dynamic_update_slice_in_dim(
        jnp.zeros((images, model_width), jnp.float32), grad_window, first_image, 0
    )
    condition_columns = grad_condition_local.T
    seq_modulation, seq_input, seq_output, seq_expand, seq_contract, condition_share = (
        lax.psum_scatter(grad_modulation_weight, "seq", scatter_dimension=1, tiled=True),
        lax.psum_scatter(grad_input_weight, "seq", scatter_dimension=1, tiled=True),
        lax.psum_scatter(grad_output_weight, "seq", scatter_dimension=1, tiled=True),
        lax.psum_scatter(grad_expand_weight, "seq", scatter_dimension=1, tiled=True),
        lax.psum_scatter(grad_contract_weight, "seq", scatter_dimension=1, tiled=True),
        lax.psum_scatter(condition_columns, "seq", scatter_dimension=1, tiled=True),
    )
    total_modulation, total_input, total_output, total_expand, total_contract = (
        lax.psum_scatter(seq_modulation, "dp", scatter_dimension=0, tiled=True),
        lax.psum_scatter(seq_input, "dp", scatter_dimension=0, tiled=True),
        lax.psum_scatter(seq_output, "dp", scatter_dimension=0, tiled=True),
        lax.psum_scatter(seq_expand, "dp", scatter_dimension=0, tiled=True),
        lax.psum_scatter(seq_contract, "dp", scatter_dimension=0, tiled=True),
    )
    grad_condition = condition_share.T
    bias_modulation, bias_query_value, bias_output, bias_expand, bias_contract = lax.psum(
        (
            grad_modulation_bias,
            grad_query_value_bias,
            grad_output_bias,
            grad_expand_bias,
            grad_contract_bias,
        ),
        ("dp", "seq"),
    )
    return (
        layer_out[None],
        grad_rows[None],
        grad_condition[None],
        total_modulation,
        bias_modulation,
        total_input,
        bias_query_value,
        total_output,
        bias_output,
        total_expand,
        bias_expand,
        total_contract,
        bias_contract,
    )


def solution(mesh):
    in_specs = (
        P("dp", "seq", None),
        P("dp", "seq"),
        P("dp", None, None),
        P("dp", "seq", None),
        P("dp", None),
        P(),
        P("dp", None),
        P(),
        P("dp", None),
        P(),
        P("dp", None),
        P(),
        P("dp", None),
        P(),
    )
    out_specs = (
        P("dp", "seq", None),
        P("dp", "seq", None),
        P("dp", "seq", None),
        P("dp", "seq"),
        P(),
        P("dp", "seq"),
        P(),
        P("dp", "seq"),
        P(),
        P("dp", "seq"),
        P(),
        P("dp", "seq"),
        P(),
    )
    return jax.shard_map(shards, mesh=mesh, in_specs=in_specs, out_specs=out_specs, check_vma=False)
```

profile of v0, /device:TPU:0, one launch (start us, length us, event | category | flops | bytes accessed | tf_op | source)
XLA Modules:
  0.0 2674.4 jit_solution(2236393778587409628)
XLA Ops:
  12.5 100.9 %all-gather.6.cloned.1.call-done = bf16[1152,6912]{1,0:T(8,128)(2,1)} async-done(((bf16[288,6912]{1,0:T(8,128)(2,1)}), bf16[1152,6912]{1,0:T(8,128)(2,1)}) %all-gather.6.cloned.1.call-update) | async-done | bytes 15925264 | tf_op jit(solution)/shard_map/all_gather | solution.py:80
  121.2 12.0 fusion.59
  133.3 9.4 copy-done.2
  145.2 25.7 all-gather.8.cloned.1.call-done
  170.9 13.0 fusion.85
  200.4 28.5 %collective-permute-done.2 = s32[192]{0:T(256)S(1)} collective-permute-done((s32[192]{0:T(256)S(1)}, s32[192]{0:T(256)S(1)}, u32[]{:S(2)}, u32[]{:S(2)}) %collective-permute-start.2) | collective-permute-done | bytes 800 | tf_op jit(solution)/shard_map/ppermute | solution.py:23
  229.0 8.8 reshape.203
  250.9 9.5 copy.49
  262.0 107.0 %while.26 = (s32[]{:T(128)}, bf16[2,512,1152]{2,1,0:T(8,128)(2,1)}, f32[2,16,512,1]{2,1,3,0:T(8,128)}, f32[2,16,512,1]{2,1,3,0:T(8,128)}, s32[2]{0:T(128)S(1)}, ...) while((s32[]{:T(128)}, bf16[2,512,1152]{2,1,0:T(8,128)(2,1)}, ...), condition=%wide.region_5.6_spmd, body=%wide.region_2.5_spmd.sunk | while | flops 2202451968 | bytes 109953912 | solution.py:156
  268.2 14.4 fusion.141
  282.6 15.1 fusion.142
  297.8 15.0 fusion.143
  323.2 12.8 fusion.141
  336.1 13.7 fusion.142
  349.8 14.8 fusion.143
  369.1 11.1 fusion.78
  383.5 7.9 convert_reduce_fusion.3
  391.5 19.6 fusion.86
  411.0 30.3 %convert_reduce_fusion = (f32[4608]{0:T(1024)}, bf16[1024,4608]{1,0:T(8,128)(2,1)}) fusion(f32[1024,4608]{1,0:T(8,128)} %fusion.86, f32[4608]{0:T(1024)S(1)} %copy-done.46, bf16[1024,1152]{1,0:T(8,128)(2,1)} %get-tuple-element.274, bf16[4608,1152]{1,0:T(8,128)(2,1)} %all-gather.14.cloned.1.call-done), kind=kOutput, calls=%fused_computation.54 | convolution fusion | flops 10980159488 | bytes 41324544 | tf_op jit(solution)/shard_map/dot_general | solution.py:58
  441.4 21.9 fusion.73
  463.3 22.5 convolution_add_fusion.1
  485.8 11.5 convert_reduce_fusion.4
  497.4 8.1 fusion.87
  512.0 9.6 reshape.193
  535.9 298.9 %while.27 = (s32[]{:T(128)}, f32[1408,2304]{1,0:T(8,128)}, bf16[2,512,1152]{2,1,0:T(8,128)(2,1)}, s32[2]{0:T(128)S(1)}, bf16[2,512,16,72]{1,3,2,0:T(8,128)(2,1)}...) while((s32[]{:T(128)}, f32[1408,2304]{1,0:T(8,128)}, ...), condition=%wide.region_12.13_spmd, body=%wide.region_10.12_spmd.sunk | while | flops 5365014528 | bytes 380945344 | solution.py:235
  550.8 9.0 copy.101
  559.8 15.5 fusion.154
  575.3 23.5 multiply_reduce_fusion.4
  598.8 24.7 multiply_convert_fusion.7
  623.5 14.3 fusion.155
  637.8 10.3 convolution_multiply_fusion.5
  648.1 10.0 convolution_multiply_fusion.4
  658.9 9.8 maximum_add_fusion.2
  668.7 8.9 copy.102
  700.6 8.8 copy.101
  709.4 15.1 fusion.154
  724.6 23.3 multiply_reduce_fusion.4
  747.9 24.4 multiply_convert_fusion.7
  772.3 14.1 fusion.155
  786.4 10.3 convolution_multiply_fusion.5
  796.7 10.0 convolution_multiply_fusion.4
  807.4 9.8 maximum_add_fusion.2
  817.2 8.9 copy.102
  844.8 22.0 collective-permute-done.5
  866.8 31.0 %collective-permute-done.4 = f32[192,2304]{1,0:T(8,128)S(1)} collective-permute-done((f32[192,2304]{1,0:T(8,128)S(1)}, f32[192,2304]{1,0:T(8,128)S(1)}, u32[]{:S(2)}, u32[]{:S(2)}) %collective-permute-start.4) | collective-permute-done | bytes 1769504 | tf_op jit(solution)/shard_map/ppermute | solution.py:34
  904.1 12.6 fusion.56
  918.4 19.6 fusion.75
  939.7 19.0 fusion.88
  958.8 16.0 constant_dynamic-update-slice_fusion.4
  978.7 7.9 fusion.46
  1000.9 14.1 fusion.84
  1015.0 17.2 fusion.70
  1032.3 15.3 fusion.63
  1052.0 136.4 %reduce-scatter.21.cloned.1.call-done = f32[1152,432]{0,1:T(8,128)} async-done(((f32[1152,3456]{0,1:T(8,128)}), f32[1152,432]{0,1:T(8,128)}) %reduce-scatter.21.cloned.1.call-update) | async-done | bytes 1990672 | tf_op jit(solution)/shard_map/reduce_scatter | solution.py:287
  1191.6 347.5 %reduce-scatter.27.cloned.1.call-done = f32[4608,144]{0,1:T(8,128)} async-done(((f32[4608,1152]{0,1:T(8,128)}), f32[4608,144]{0,1:T(8,128)}) %reduce-scatter.27.cloned.1.call-update) | async-done | bytes 2654224 | tf_op jit(solution)/shard_map/reduce_scatter | solution.py:290
  1539.2 350.2 %reduce-scatter.25.cloned.1.call-done = f32[1152,576]{0,1:T(8,128)} async-done(((f32[1152,4608]{0,1:T(8,128)}), f32[1152,576]{0,1:T(8,128)}) %reduce-scatter.25.cloned.1.call-update) | async-done | bytes 2654224 | tf_op jit(solution)/shard_map/reduce_scatter | solution.py:289
  1893.0 512.3 %reduce-scatter.19.cloned.1.call-done = f32[1152,864]{0,1:T(8,128)} async-done(((f32[1152,6912]{0,1:T(8,128)}), f32[1152,864]{0,1:T(8,128)}) %reduce-scatter.19.cloned.1.call-update) | async-done | bytes 3981328 | tf_op jit(solution)/shard_map/reduce_scatter | solution.py:286
  2415.6 41.5 %all-reduce.3 = (f32[6912]{0:T(1024)}, f32[2304]{0:T(1024)}, f32[1152]{0:T(1024)}, f32[4608]{0:T(1024)}, f32[1152]{0:T(1024)}) all-reduce(f32[6912]{0:T(1024)S(1)} %get-tuple-element.314, f32[2304]{0:T(1024)S(1)} %pad_maximum_fusion.6, f32[1152]{0:T(1024)S(1)} %copy-done.45, ...), channel_id=1, replica_groups=mesh['dp'=4,'seq'=8] {'dp','seq'}, use_global_device_ids=true, to_apply=%region_19.20 | all-reduce | flops 16128 | bytes 129024 | tf_op jit(solution)/shard_map/psum | solution.py:301
  2457.1 22.0 all-reduce.6.cloned.1.call-done
  2480.5 25.9 reduce-scatter.35.cloned.1.call-done
  2508.1 34.6 %reduce-scatter.33.cloned.1.call-done = f32[288,432]{1,0:T(8,128)} async-done(((f32[1152,432]{1,0:T(8,128)}), f32[288,432]{1,0:T(8,128)}) %reduce-scatter.33.cloned.1.call-update) | async-done | bytes 497680
  2542.7 37.9 %reduce-scatter.29.cloned.1.call-done = f32[1152,144]{0,1:T(8,128)} async-done(((f32[4608,144]{0,1:T(8,128)}), f32[1152,144]{0,1:T(8,128)}) %reduce-scatter.29.cloned.1.call-update) | async-done | bytes 663568 | tf_op jit(solution)/shard_map/reduce_scatter | solution.py:298
  2580.6 39.9 %reduce-scatter.37.cloned.1.call-done = f32[288,576]{1,0:T(8,128)} async-done(((f32[1152,576]{1,0:T(8,128)}), f32[288,576]{1,0:T(8,128)}) %reduce-scatter.37.cloned.1.call-update) | async-done | bytes 663568
  2620.5 47.2 %reduce-scatter.31.cloned.1.call-done = f32[288,864]{1,0:T(8,128)} async-done(((f32[1152,864]{1,0:T(8,128)}), f32[288,864]{1,0:T(8,128)}) %reduce-scatter.31.cloned.1.call-update) | async-done | bytes 995344
  (284 shorter events, 189.8 us)
Async XLA Ops:
  7.2 106.2 %all-gather.6.cloned.1.call-start = ((), (), s32[]{:S(2)}) async-start(), calls=%async_computation.10 | async-start | bytes 19906560 | tf_op jit(solution)/shard_map/all_gather | solution.py:80
  8.0 162.9 %all-gather.8.cloned.1.call-start = ((), (), s32[]{:S(2)}) async-start(), calls=%async_computation.11 | async-start | bytes 9953280 | tf_op jit(solution)/shard_map/all_gather | solution.py:81
  8.7 360.4 %all-gather.10.cloned.1.call-start = ((), (), s32[]{:S(2)}) async-start(), calls=%async_computation.12 | async-start | bytes 3317760 | tf_op jit(solution)/shard_map/all_gather | solution.py:82
  9.4 382.0 %all-gather.12.cloned.1.call-start = ((), (), s32[]{:S(2)}) async-start(), calls=%async_computation.13 | async-start | bytes 13271040 | tf_op jit(solution)/shard_map/all_gather | solution.py:83
  10.0 401.0 %all-gather.14.cloned.1.call-start = ((), (), s32[]{:S(2)}) async-start(), calls=%async_computation.14 | async-start | bytes 13271040 | tf_op jit(solution)/shard_map/all_gather | solution.py:84
  11.7 121.6 %copy-start.35 = (f32[1024]{0:T(1024)}, f32[1024]{0:T(1024)S(1)}, u32[]{:S(2)}) copy-start(f32[1024]{0:T(1024)S(1)} %broadcast_multiply_fusion.5) | copy-start | bytes 12292
  12.5 120.8 %copy-start.39 = (f32[1024]{0:T(1024)}, f32[1024]{0:T(1024)S(1)}, u32[]{:S(2)}) copy-start(f32[1024]{0:T(1024)S(1)} %add_rsqrt_fusion.1) | copy-start | bytes 12292
  12.5 108.7 %copy-start.26 = (s32[1,1024]{1,0:T(1,128)}, s32[1,1024]{1,0:T(1,128)S(1)}, u32[]{:S(2)}) copy-start(s32[1,1024]{1,0:T(1,128)S(1)} %get-tuple-element.309) | copy-start | bytes 12292
  185.0 13.6 copy-start.53
  185.0 14.2 copy-start.54
  185.0 14.8 copy-start.50
  186.9 56.7 %collective-permute-start = (bf16[192,2304]{1,0:T(8,128)(2,1)}, bf16[192,2304]{1,0:T(8,128)(2,1)}, u32[]{:S(2)}, u32[]{:S(2)}) collective-permute-start(bf16[192,2304]{1,0:T(8,128)(2,1)} %get-tuple-element.300), channel_id=1, source_target_pairs={{0,1},{1,2},{2,3},{3,4},{4,5},{5,6},{6,7},{8,9},{9,10},{10,11},{11... | collective-permute-start | bytes 2654216 | tf_op jit(solution)/shard_map/ppermute | solution.py:23
  191.3 52.4 %collective-permute-start.1 = (bf16[192,2304]{1,0:T(8,128)(2,1)}, bf16[192,2304]{1,0:T(8,128)(2,1)}, u32[]{:S(2)}, u32[]{:S(2)}) collective-permute-start(bf16[192,2304]{1,0:T(8,128)(2,1)} %get-tuple-element.301), channel_id=1, source_target_pairs={{1,0},{2,1},{3,2},{4,3},{5,4},{6,5},{7,6},{9,8},{10,9},{11,10},{12... | collective-permute-start | bytes 2654216 | tf_op jit(solution)/shard_map/ppermute | solution.py:26
  192.6 36.3 %collective-permute-start.2 = (s32[192]{0:T(256)S(1)}, s32[192]{0:T(256)S(1)}, u32[]{:S(2)}, u32[]{:S(2)}) collective-permute-start(s32[192]{0:T(256)S(1)} %bitcast.225), channel_id=1, source_target_pairs={{0,1},{1,2},{2,3},{3,4},{4,5},{5,6},{6,7},{8,9},{9,10},{10,11},{11... | collective-permute-start | bytes 2312 | tf_op jit(solution)/shard_map/ppermute | solution.py:23
  197.2 31.8 %collective-permute-start.3 = (s32[192]{0:T(256)S(1)}, s32[192]{0:T(256)S(1)}, u32[]{:S(2)}, u32[]{:S(2)}) collective-permute-start(s32[192]{0:T(256)S(1)} %bitcast.224), channel_id=1, source_target_pairs={{1,0},{2,1},{3,2},{4,3},{5,4},{6,5},{7,6},{9,8},{10,9},{11,10},{12... | collective-permute-start | bytes 2312 | tf_op jit(solution)/shard_map/ppermute | solution.py:26
  198.5 850.9 %reduce-scatter.23.cloned.1.call-start = ((), (), s32[]{:S(2)}) async-start(), calls=%async_computation.17 | async-start | bytes 5971968 | tf_op jit(solution)/shard_map/reduce_scatter | solution.py:288
  282.6 15.1 copy-start.18
  297.8 15.0 copy-start.19
  336.1 13.7 copy-start.18
  349.8 14.8 copy-start.19
  369.0 11.1 copy-start.3
  369.0 11.1 copy-start.30
  380.2 105.6 %copy-start.37 = (f32[1024]{0:T(1024)}, f32[1024]{0:T(1024)S(1)}, u32[]{:S(2)}) copy-start(f32[1024]{0:T(1024)S(1)} %broadcast_multiply_fusion.4) | copy-start | bytes 12292
  383.5 102.3 %copy-start.41 = (f32[1024]{0:T(1024)}, f32[1024]{0:T(1024)S(1)}, u32[]{:S(2)}) copy-start(f32[1024]{0:T(1024)S(1)} %add_rsqrt_fusion) | copy-start | bytes 12292
  391.4 19.6 copy-start.22
  391.5 19.6 copy-start.46
  441.3 21.9 copy-start.51
  441.4 44.5 %slice-start = ((s8[4718592]{0:T(1024)(128)(4,1)}), s8[524288]{0:T(1024)(128)(4,1)S(1)}, s32[]{:S(2)}) async-start(s8[4718592]{0:T(1024)(128)(4,1)} %bitcast.202), calls=%async_computation.26 | async-start | bytes 1048576
  463.2 22.6 slice-start.1
  463.2 22.6 copy-start.9
  463.2 22.6 copy-start.12
  528.7 659.7 %reduce-scatter.21.cloned.1.call-start = ((), (), s32[]{:S(2)}) async-start(), calls=%async_computation.16 | async-start | bytes 17915904 | tf_op jit(solution)/shard_map/reduce_scatter | solution.py:287
  559.8 15.5 copy-start
  559.8 15.5 copy-start.4
  598.8 24.8 copy-start.5
  623.5 14.3 copy-start.1
  709.4 15.2 copy-start
  709.4 15.2 copy-start.4
  747.9 24.4 copy-start.5
  772.3 14.1 copy-start.1
  836.4 61.4 %collective-permute-start.4 = (f32[192,2304]{1,0:T(8,128)S(1)}, f32[192,2304]{1,0:T(8,128)S(1)}, u32[]{:S(2)}, u32[]{:S(2)}) collective-permute-start(f32[192,2304]{1,0:T(8,128)S(1)} %slice.79), channel_id=1, source_target_pairs={{0,1},{1,2},{2,3},{3,4},{4,5},{5,6},{6,7},{8,9},{9,10},{10,11},{11... | collective-permute-start | bytes 5308424 | tf_op jit(solution)/shard_map/ppermute | solution.py:34
  843.2 60.8 %copy-start.16 = (bf16[2,512,1152]{2,1,0:T(8,128)(2,1)S(1)}, bf16[2,512,1152]{2,1,0:T(8,128)(2,1)}, u32[]{:S(2)}) copy-start(bf16[2,512,1152]{2,1,0:T(8,128)(2,1)} %get-tuple-element.123) | copy-start | bytes 7077892
  843.3 60.8 %copy-start.21 = (bf16[1024,1152]{1,0:T(8,128)(2,1)S(1)}, bf16[1024,1152]{1,0:T(8,128)(2,1)}, u32[]{:S(2)}) copy-start(bf16[1024,1152]{1,0:T(8,128)(2,1)} %fusion.40) | copy-start | bytes 7077892
  843.3 23.5 collective-permute-start.5
  916.7 622.4 %reduce-scatter.27.cloned.1.call-start = ((), (), s32[]{:S(2)}) async-start(), calls=%async_computation.19 | async-start | bytes 23887872 | tf_op jit(solution)/shard_map/reduce_scatter | solution.py:290
  938.0 951.4 %reduce-scatter.25.cloned.1.call-start = ((), (), s32[]{:S(2)}) async-start(), calls=%async_computation.18 | async-start | bytes 23887872 | tf_op jit(solution)/shard_map/reduce_scatter | solution.py:289
  958.7 16.1 copy-start.8
  958.7 16.0 copy-start.36
  958.7 16.0 copy-start.40
  958.7 1446.5 %reduce-scatter.19.cloned.1.call-start = ((), (), s32[]{:S(2)}) async-start(), calls=%async_computation.15 | async-start | bytes 35831808 | tf_op jit(solution)/shard_map/reduce_scatter | solution.py:286
  974.7 11.9 slice-start.6
  974.8 17.0 slice-start.4
  974.8 19.8 slice-start.2
  978.7 13.1 slice-start.5
  978.7 15.8 slice-start.3
  1000.9 14.1 copy-start.34
  1032.3 1446.8 %all-reduce.6.cloned.1.call-start = ((), (), s32[]{:S(2)}) async-start(), calls=%async_computation.25 | async-start | bytes 589824
  1049.4 1457.0 %reduce-scatter.35.cloned.1.call-start = ((), (), s32[]{:S(2)}) async-start(), calls=%async_computation.23 | async-start | bytes 1474560
  1051.9 1490.8 %reduce-scatter.33.cloned.1.call-start = ((), (), s32[]{:S(2)}) async-start(), calls=%async_computation.22 | async-start | bytes 2949120
  1191.6 1389.0 %reduce-scatter.29.cloned.1.call-start = ((), (), s32[]{:S(2)}) async-start(), calls=%async_computation.20 | async-start | bytes 3317760 | tf_op jit(solution)/shard_map/reduce_scatter | solution.py:298
  1539.2 1081.3 %reduce-scatter.37.cloned.1.call-start = ((), (), s32[]{:S(2)}) async-start(), calls=%async_computation.24 | async-start | bytes 3686400
  1892.9 518.0 %copy-start.55 = (u32[32]{0:T(128)S(1)}, u32[32]{0:T(128)}, u32[]{:S(2)}) copy-start(u32[32]{0:T(128)} %constant.106) | copy-start | bytes 388
  1892.9 519.2 %copy-start.17 = (bf16[2,512,1152]{2,1,0:T(8,128)(2,1)S(1)}, bf16[2,512,1152]{2,1,0:T(8,128)(2,1)}, u32[]{:S(2)}) copy-start(bf16[2,512,1152]{2,1,0:T(8,128)(2,1)} %get-tuple-element.123) | copy-start | bytes 7077892
  1892.9 774.7 %reduce-scatter.31.cloned.1.call-start = ((), (), s32[]{:S(2)}) async-start(), calls=%async_computation.21 | async-start | bytes 5160960
  (30 other events, 126.7 us)
Sparse Core Ops, SparseCore 0:
  9.6 103.7 all-gather.5
  115.0 55.8 all-gather.7
  172.5 25.7 all-gather.9
  199.6 70.9 all-gather.11
  272.0 70.9 all-gather.13
  528.9 105.0 reduce-scatter.22
  916.9 271.4 reduce-scatter.20
  1192.8 346.3 reduce-scatter.26
  1543.1 346.3 reduce-scatter.24
  1893.7 511.5 reduce-scatter.18
  2409.0 70.0 all-reduce.5
  2481.5 24.7 reduce-scatter.34
  2509.6 33.0 reduce-scatter.32
  2545.7 34.8 reduce-scatter.28
  2583.7 36.7 reduce-scatter.36
  2623.5 44.0 reduce-scatter.30
where the time goes:
time: 2680 us; the launch traced here: 2670 us
  waiting for transfers between devices  1760 us (66%)
  matrix products  470 us (18%)
  local copies, waits for them, and re-layouts  188 us (7%)
  other arithmetic  164 us (6%)
  blocking collectives  41.5 us (2%)
    reduce_scatter x1, waiting for transfers between devices, shards(): lax.psum_scatter(grad_modulation_weight, 'seq', scatter_dimension=1, tile...  512 us
    reduce_scatter x1, waiting for transfers between devices, shards(): lax.psum_scatter(grad_expand_weight, 'seq', scatter_dimension=1, tiled=True)  350 us
    reduce_scatter x1, waiting for transfers between devices, shards(): lax.psum_scatter(grad_contract_weight, 'seq', scatter_dimension=1, tiled=...  348 us
    unnamed x21, waiting for transfers between devices  172 us
    reduce_scatter x1, waiting for transfers between devices, shards(): lax.psum_scatter(grad_input_weight, 'seq', scatter_dimension=1, tiled=True)  136 us
    all_gather x1, waiting for transfers between devices, shards(): lax.all_gather(modulation_weight, 'dp', axis=0, tiled=True)  101 us
    dot_general x4, matrix products, back_dot(): lax.dot_general(gradient, matrix, (((1,), (1,)), ((), ())), preferred_ele...  74.7 us
    dot_general x4, matrix products, block_scores(): jnp.einsum('qhd,khd->hqk', query_heads[block_index], key_heads, preferred...  74 us
  transfers between devices with their start and end apart: 22, of which 15 were waited for; matrix products, arithmetic and copies ran while one was open for 26% of the time, Pallas kernels for 0%

commit v1 on v0

v1 whole, which is shorter than its diff:
```python
import functools
from functools import partial
import math

import jax
import jax.numpy as jnp
from jax import lax
from jax.experimental import pallas as pl
from jax.experimental.pallas import tpu as pltpu
from jax.sharding import PartitionSpec as P

WIN = 18
HEADS = 16
MAXLEN = 192
HEAD = 72
BLOCK = 256
SPAN = BLOCK + 2 * MAXLEN
CHUNK = 128
BF, F32 = jnp.bfloat16, jnp.float32
SCORE_SCALE = 1.0 / math.sqrt(HEAD)
LOG2E = 1.4426950408889634
VMEM = 60 * 1024 * 1024


def dot_rows(left, right):
    return lax.dot_general(left, right, (((1,), (1,)), ((), ())), preferred_element_type=F32)


def dot_plain(left, right):
    return jnp.dot(left, right, preferred_element_type=F32)


def fill_mask(key_mark_ref, query_mark_ref, bias):
    marks = jnp.broadcast_to(key_mark_ref[0].astype(F32), (CHUNK, SPAN))
    columns = marks.T
    query = query_mark_ref[0].astype(F32)
    for lane in range(0, BLOCK, CHUNK):
        bias[:, lane : lane + CHUNK] = jnp.where(
            columns == query[:, lane : lane + CHUNK], 0.0, -1e30
        )


def head_lanes(head, width):
    first = jnp.minimum((head * HEAD) // 128 * 128, width - 256)
    lanes = lax.broadcasted_iota(jnp.int32, (1, 256), 1) + first
    inside = (lanes >= head * HEAD) & (lanes < (head + 1) * HEAD)
    return pl.multiple_of(first, 128), inside


def masked(ref, first, inside):
    block = ref[:, pl.ds(first, 256)]
    return jnp.where(inside, block, jnp.zeros_like(block))


def take_window(edge, step, prev_ref, own_ref, next_ref, window):
    rows = own_ref.shape[0]
    inner = SPAN - MAXLEN
    if not edge:
        return own_ref.at[pl.ds(pl.multiple_of(step * BLOCK + BLOCK - MAXLEN, 64), SPAN)]

    @pl.when(step == 0)
    def _():
        window[0:MAXLEN, :] = prev_ref[...]
        window[MAXLEN:SPAN, :] = own_ref[0:inner, :]

    @pl.when(step == 1)
    def _():
        window[0:inner, :] = own_ref[rows - inner : rows, :]
        window[inner:SPAN, :] = next_ref[...]

    return window


def forward_kernel(edge, *refs):
    if edge:
        (query_ref, own_ref, prev_ref, next_ref, key_mark_ref, query_mark_ref, _, _,
         out_ref, peak_ref, bias, turned, scores, weights, mixed, window) = refs
    else:
        (query_ref, own_ref, key_mark_ref, query_mark_ref,
         out_ref, peak_ref, bias, turned, scores, weights, mixed) = refs
        prev_ref = next_ref = window = None
    width = query_ref.shape[1]
    view = take_window(edge, pl.program_id(0), prev_ref, own_ref, next_ref, window)
    fill_mask(key_mark_ref, query_mark_ref, bias)
    turned[...] = view[:, width : 2 * width].T
    factor = SCORE_SCALE * LOG2E

    def pair(index, carry):
        for odd in range(2):
            head = 2 * index + odd
            first, inside = head_lanes(head, width)
            query = masked(query_ref, first, inside)
            peak = jnp.full((8, BLOCK), -3e38, F32)
            for start in range(0, SPAN, CHUNK):
                rows = slice(start, start + CHUNK)
                score = dot_rows(view[rows, pl.ds(first, 256)], query) * factor + bias[rows, :]
                scores[odd, rows, :] = score
                peak = jnp.maximum(peak, jnp.max(score.reshape(CHUNK // 8, 8, BLOCK), axis=0))
            peak = jnp.max(peak, axis=0, keepdims=True)
            total = jnp.zeros((8, BLOCK), F32)
            for start in range(0, SPAN, CHUNK):
                rows = slice(start, start + CHUNK)
                power = jnp.exp2(scores[odd, rows, :] - peak)
                total = total + jnp.sum(power.reshape(CHUNK // 8, 8, BLOCK), axis=0)
                weights[odd, rows, :] = power.astype(BF)
            total = jnp.sum(total, axis=0, keepdims=True)
            base = pl.multiple_of(index * 2 * HEAD, 16)
            value = turned[pl.ds(pl.multiple_of(base + 64 * odd, 16), 80), :]
            part = dot_plain(value, weights[odd]) * (1.0 / total)
            mixed[pl.ds(pl.multiple_of(base + HEAD * odd, 8), HEAD), :] = part[8 * odd : 8 * odd + HEAD]
            peak_ref[pl.ds(head, 1), :] = peak + jnp.log2(total)
        return carry

    lax.fori_loop(0, HEADS // 2, pair, 0)
    out_ref[...] = mixed[...].T.astype(BF)


def backward_kernel(edge, *refs):
    if edge:
        (query_ref, out_ref, grad_ref, peak_ref, own_ref, prev_ref, next_ref, key_mark_ref, query_mark_ref,
         grad_query_ref, rim_low_ref, rim_high_ref, grad_own_ref,
         bias, turned, weights, signals, mixed, delta, window, total) = refs
    else:
        (query_ref, out_ref, grad_ref, peak_ref, own_ref, key_mark_ref, query_mark_ref, edge_ref, _,
         grad_query_ref, grad_own_ref,
         bias, turned, weights, signals, mixed, delta, sem) = refs
        prev_ref = next_ref = window = None
    width = query_ref.shape[1]
    step = pl.program_id(0)
    view = take_window(edge, step, prev_ref, own_ref, next_ref, window)
    inner = SPAN - MAXLEN
    if edge:
        total[...] = jnp.zeros_like(total)
        sums = total
    else:
        rows = grad_own_ref.shape[0]

        @pl.when(step == 0)
        def _():
            low = pltpu.make_async_copy(edge_ref.at[0], grad_own_ref.at[pl.ds(0, inner)], sem.at[0])
            high = pltpu.make_async_copy(
                edge_ref.at[1], grad_own_ref.at[pl.ds(rows - inner, inner)], sem.at[1]
            )
            low.start()
            high.start()
            grad_own_ref[inner : rows - inner, :] = jnp.zeros((rows - 2 * inner, 2 * width), F32)
            low.wait()
            high.wait()

        sums = grad_own_ref.at[pl.ds(pl.multiple_of(step * BLOCK + BLOCK - MAXLEN, 64), SPAN)]
    fill_mask(key_mark_ref, query_mark_ref, bias)
    turned[...] = view[:, 0:width].T
    product = out_ref[...].astype(F32) * grad_ref[...].astype(F32)
    high = product.astype(BF)
    low = (product - high.astype(F32)).astype(BF)
    of_head = (
        lax.broadcasted_iota(jnp.int32, (HEADS, width), 1) // HEAD
        == lax.broadcasted_iota(jnp.int32, (HEADS, width), 0)
    ).astype(BF)
    delta[...] = dot_rows(of_head, high) + dot_rows(of_head, low)
    factor = SCORE_SCALE * LOG2E

    def pair(index, carry):
        for odd in range(2):
            head = 2 * index + odd
            first, inside = head_lanes(head, width)
            query = masked(query_ref, first, inside)
            grad = masked(grad_ref, first, inside)
            peak = peak_ref[pl.ds(head, 1), :]
            mean = delta[pl.ds(head, 1), :]
            for start in range(0, SPAN, CHUNK):
                rows = slice(start, start + CHUNK)
                score = dot_rows(view[rows, pl.ds(first, 256)], query) * factor
                power = jnp.exp2(score + (bias[rows, :] - peak))
                slope = dot_rows(view[rows, pl.ds(first + width, 256)], grad)
                low = power.astype(BF)
                signal = (power * (slope - mean)).astype(BF)
                signals[odd, rows, :] = signal
                sums[rows, pl.ds(first, 256)] += dot_plain(signal, query)
                sums[rows, pl.ds(first + width, 256)] += dot_plain(low, grad)
            base = pl.multiple_of(index * 2 * HEAD, 16)
            key = turned[pl.ds(pl.multiple_of(base + 64 * odd, 16), 80), :]
            part = dot_plain(key, signals[odd]) * SCORE_SCALE
            mixed[pl.ds(pl.multiple_of(base + HEAD * odd, 8), HEAD), :] = part[8 * odd : 8 * odd + HEAD]
        return carry

    lax.fori_loop(0, HEADS // 2, pair, 0)
    grad_query_ref[...] = mixed[...].T.astype(BF)
    if edge:

        @pl.when(step == 0)
        def _():
            rim_low_ref[:, :width] = (total[0:MAXLEN, :width] * SCORE_SCALE).astype(BF)
            rim_low_ref[:, width:] = total[0:MAXLEN, width:].astype(BF)
            grad_own_ref[0] = total[MAXLEN:SPAN, :]

        @pl.when(step == 1)
        def _():
            rim_high_ref[:, :width] = (total[inner:SPAN, :width] * SCORE_SCALE).astype(BF)
            rim_high_ref[:, width:] = total[inner:SPAN, width:].astype(BF)
            grad_own_ref[0] = total[0:inner, :]
    else:

        @pl.when(step == pl.num_programs(0) - 1)
        def _():
            grad_own_ref[:, :width] = grad_own_ref[:, :width] * SCORE_SCALE


def mark_windows(marker, marker_prev, marker_next):
    wide = jnp.concatenate([marker_prev, marker, marker_next])
    count = marker.shape[0] // BLOCK
    keys = jnp.stack([wide[i * BLOCK : i * BLOCK + SPAN] for i in range(count)])[:, None, :]
    return keys, marker.reshape(count, 1, BLOCK)


def whole(shape):
    return pl.BlockSpec(shape, lambda i: (0,) * len(shape))


def attention_calls(rows, width):
    count = rows // BLOCK
    last = count - 1
    inner = SPAN - MAXLEN
    scratch = [
        pltpu.VMEM((SPAN, BLOCK), F32),
        pltpu.VMEM((width, SPAN), BF),
    ]
    elements = SPAN * BLOCK * HEADS

    def block_specs(edge):
        at = (lambda i: i * last) if edge else (lambda i: i + 1)
        row_block = pl.BlockSpec((BLOCK, width), lambda i: (at(i), 0))
        lane_block = pl.BlockSpec((HEADS, BLOCK), lambda i: (0, at(i)))
        key_mark = pl.BlockSpec((1, 1, SPAN), lambda i: (at(i), 0, 0))
        query_mark = pl.BlockSpec((1, 1, BLOCK), lambda i: (at(i), 0, 0))
        return row_block, lane_block, key_mark, query_mark

    any_spec = pl.BlockSpec(memory_space=pl.ANY)
    params = pltpu.CompilerParams(vmem_limit_bytes=VMEM, dimension_semantics=("arbitrary",))

    def forward(edge, queries, key_value, marks, halo=(), before=()):
        row_block, lane_block, key_mark, query_mark = block_specs(edge)
        steps = 2 if edge else count - 2
        in_specs = [row_block, whole((rows, 2 * width))]
        in_specs += [whole((MAXLEN, 2 * width))] * len(halo)
        in_specs += [key_mark, query_mark] + [any_spec] * len(before)
        extra = [pltpu.VMEM((SPAN, 2 * width), BF)] if edge else []
        return pl.pallas_call(
            functools.partial(forward_kernel, edge),
            grid=(steps,),
            in_specs=in_specs,
            out_specs=[row_block, lane_block],
            out_shape=[
                jax.ShapeDtypeStruct((rows, width), BF),
                jax.ShapeDtypeStruct((HEADS, rows), F32),
            ],
            scratch_shapes=scratch
            + [
                pltpu.VMEM((2, SPAN, BLOCK), F32),
                pltpu.VMEM((2, SPAN, BLOCK), BF),
                pltpu.VMEM((width, BLOCK), F32),
            ]
            + extra,
            input_output_aliases={6: 0, 7: 1} if edge else {},
            compiler_params=params,
            cost_estimate=pl.CostEstimate(
                flops=steps * elements * 1024, bytes_accessed=rows * width * 6, transcendentals=steps * elements
            ),
            name="attend_edge" if edge else "attend_inner",
        )(queries, key_value, *halo, *marks, *before)

    def backward(edge, queries, mixed, grad, peaks, key_value, marks, halo=(), before=()):
        row_block, lane_block, key_mark, query_mark = block_specs(edge)
        steps = 2 if edge else count - 2
        in_specs = [row_block, row_block, row_block, lane_block, whole((rows, 2 * width))]
        in_specs += [whole((MAXLEN, 2 * width))] * len(halo)
        in_specs += [key_mark, query_mark] + [any_spec] * len(before)
        rim = jax.ShapeDtypeStruct((MAXLEN, 2 * width), BF)
        if edge:
            out_specs = [row_block, whole(rim.shape), whole(rim.shape),
                         pl.BlockSpec((1, inner, 2 * width), lambda i: (i, 0, 0))]
            out_shape = [jax.ShapeDtypeStruct((rows, width), BF), rim, rim,
                         jax.ShapeDtypeStruct((2, inner, 2 * width), F32)]
            extra = [pltpu.VMEM((SPAN, 2 * width), BF), pltpu.VMEM((SPAN, 2 * width), F32)]
        else:
            out_specs = [row_block, whole((rows, 2 * width))]
            out_shape = [jax.ShapeDtypeStruct((rows, width), BF),
                         jax.ShapeDtypeStruct((rows, 2 * width), F32)]
            extra = [pltpu.SemaphoreType.DMA((2,))]
        return pl.pallas_call(
            functools.partial(backward_kernel, edge),
            grid=(steps,),
            in_specs=in_specs,
            out_specs=out_specs,
            out_shape=out_shape,
            scratch_shapes=scratch
            + [
                pltpu.VMEM((2, SPAN, BLOCK), BF),
                pltpu.VMEM((2, SPAN, BLOCK), BF),
                pltpu.VMEM((width, BLOCK), F32),
                pltpu.VMEM((HEADS, BLOCK), F32),
            ]
            + extra,
            input_output_aliases={} if edge else {8: 0},
            compiler_params=params,
            cost_estimate=pl.CostEstimate(
                flops=steps * elements * 2560, bytes_accessed=rows * width * 16, transcendentals=steps * elements
            ),
            name="attend_back_edge" if edge else "attend_back_inner",
        )(queries, mixed, grad, peaks, key_value, *halo, *marks, *before)

    return forward, backward


epsilon = 1e-06
highest = lax.Precision.HIGHEST


def partners(axis, bit):
    return [(i, i ^ bit) for i in range(lax.axis_size(axis))]


def halve(blocks, axis, bit):
    mine = (lax.axis_index(axis) // bit) % 2
    kept = lax.dynamic_index_in_dim(blocks, mine, 0, keepdims=False)
    sent = lax.dynamic_index_in_dim(blocks, 1 - mine, 0, keepdims=False)
    got = lax.ppermute(sent.astype(jnp.bfloat16), axis, partners(axis, bit))
    return kept.astype(jnp.float32) + got.astype(jnp.float32)


def share_of_sum(partial_sum):
    rows, columns = partial_sum.shape
    count, seq_count = lax.axis_size("dp"), lax.axis_size("seq")
    total = partial_sum.reshape(count, rows // count, columns)
    bit = 1
    while bit < count:
        total = total.reshape(-1, 2, *total.shape[1:]).swapaxes(0, 1)
        total = halve(total, "dp", bit)
        bit *= 2
    total = total.reshape(rows // count, seq_count, columns // seq_count).astype(jnp.bfloat16).swapaxes(0, 1)
    bit = 1
    while bit < seq_count:
        total = total.reshape(-1, 2, *total.shape[1:]).swapaxes(0, 1)
        total = halve(total, "seq", bit)
        bit *= 2
    return total[0]


def layer_norm(token_rows):
    centred = token_rows - jnp.mean(token_rows, axis=-1, keepdims=True)
    inverse = lax.rsqrt(jnp.mean(centred * centred, axis=-1, keepdims=True) + epsilon)
    return (centred * inverse, inverse)


def norm_back(upstream, normed, inverse):
    return inverse * (
        upstream
        - jnp.mean(upstream, axis=-1, keepdims=True)
        - normed * jnp.mean(upstream * normed, axis=-1, keepdims=True)
    )


def outer_sum(first_matrix, second_matrix):
    return lax.dot_general(
        first_matrix, second_matrix, (((0,), (0,)), ((), ())), preferred_element_type=jnp.float32
    )


def back_dot(gradient, matrix):
    return lax.dot_general(
        gradient, matrix, (((1,), (1,)), ((), ())), preferred_element_type=jnp.float32
    )


def shards(
    tokens,
    segments,
    condition,
    cotangent,
    modulation_weight,
    modulation_bias,
    input_weight,
    query_value_bias,
    output_weight,
    output_bias,
    expand_weight,
    expand_bias,
    contract_weight,
    contract_bias,
):
    modulation_full, input_full, output_full, expand_full, contract_full = (
        lax.all_gather(modulation_weight, "dp", axis=0, tiled=True),
        lax.all_gather(input_weight, "dp", axis=0, tiled=True),
        lax.all_gather(output_weight, "dp", axis=0, tiled=True),
        lax.all_gather(expand_weight, "dp", axis=0, tiled=True),
        lax.all_gather(contract_weight, "dp", axis=0, tiled=True),
    )
    token_rows = tokens[0].astype(jnp.float32)
    segment = segments[0]
    conditions = condition[0]
    grad_out = cotangent[0].astype(jnp.float32)
    row_count, model_width = token_rows.shape
    images = conditions.shape[0]
    first_image = jnp.minimum(segment[0], images - WIN)
    window = lax.dynamic_slice_in_dim(conditions, first_image, WIN, 0).astype(jnp.float32)
    image_select = (
        (segment - first_image)[:, None] == jnp.arange(WIN, dtype=jnp.int32)[None, :]
    ).astype(jnp.float32)
    silu_low = jax.nn.silu(window).astype(jnp.bfloat16)
    modulation = jnp.dot(
        silu_low, modulation_full, preferred_element_type=jnp.float32
    ) + modulation_bias.astype(jnp.float32)
    per_row = jnp.dot(image_select, modulation, precision=highest)
    shift_mixer, scale_mixer, gate_mixer, shift_feed, scale_feed, gate_feed = jnp.split(
        per_row, 6, axis=1
    )
    normed_attn, inverse_attn = layer_norm(token_rows)
    input_attn = (normed_attn * (1.0 + scale_mixer) + shift_mixer).astype(jnp.bfloat16)
    packed = jnp.dot(input_attn, input_full, preferred_element_type=jnp.float32)
    bias_values = query_value_bias.astype(jnp.float32)
    queries = (packed[:, :model_width] + bias_values[:model_width]).astype(jnp.bfloat16)
    key_rows = packed[:, model_width : 2 * model_width].astype(jnp.bfloat16)
    values = (packed[:, 2 * model_width :] + bias_values[model_width:]).astype(jnp.bfloat16)
    key_value = jnp.concatenate([key_rows, values], axis=1)
    marker = segment + 1
    seq_count = lax.axis_size("seq")
    onward = [(i, i + 1) for i in range(seq_count - 1)]
    back = [(i + 1, i) for i in range(seq_count - 1)]
    marks = mark_windows(
        marker,
        lax.ppermute(marker[row_count - MAXLEN :], "seq", onward),
        lax.ppermute(marker[:MAXLEN], "seq", back),
    )
    halo = (
        lax.ppermute(key_value[row_count - MAXLEN :], "seq", onward),
        lax.ppermute(key_value[:MAXLEN], "seq", back),
    )
    attend, attend_back = attention_calls(row_count, model_width)
    inner_part = attend(False, queries, key_value, marks)
    attn_mixed, row_peaks = attend(True, queries, key_value, marks, halo, inner_part)
    attn_out = jnp.dot(
        attn_mixed, output_full, preferred_element_type=jnp.float32
    ) + output_bias.astype(jnp.float32)
    middle = token_rows + gate_mixer * attn_out
    normed_feed, inverse_feed = layer_norm(middle)
    input_feed = (normed_feed * (1.0 + scale_feed) + shift_feed).astype(jnp.bfloat16)
    hidden = jnp.dot(
        input_feed, expand_full, preferred_element_type=jnp.float32
    ) + expand_bias.astype(jnp.float32)
    active, gelu_back = jax.vjp(partial(jax.nn.gelu, approximate=True), hidden)
    active_low = active.astype(jnp.bfloat16)
    feed_out = jnp.dot(
        active_low, contract_full, preferred_element_type=jnp.float32
    ) + contract_bias.astype(jnp.float32)
    layer_out = (middle + gate_feed * feed_out).astype(jnp.bfloat16)
    grad_feed = (grad_out * gate_feed).astype(jnp.bfloat16)
    grad_gate_feed = grad_out * feed_out
    grad_contract_weight = outer_sum(active_low, grad_feed)
    grad_contract_bias = jnp.sum(grad_feed.astype(jnp.float32), axis=0)
    grad_active = back_dot(grad_feed, contract_full)
    grad_hidden = gelu_back(grad_active)[0].astype(jnp.bfloat16)
    grad_expand_weight = outer_sum(input_feed, grad_hidden)
    grad_expand_bias = jnp.sum(grad_hidden.astype(jnp.float32), axis=0)
    grad_input_feed = back_dot(grad_hidden, expand_full)
    grad_scale_feed = grad_input_feed * normed_feed
    grad_middle = grad_out + norm_back(
        grad_input_feed * (1.0 + scale_feed), normed_feed, inverse_feed
    )
    grad_gate_mixer = grad_middle * attn_out
    grad_attn = (grad_middle * gate_mixer).astype(jnp.bfloat16)
    grad_output_weight = outer_sum(attn_mixed, grad_attn)
    grad_output_bias = jnp.sum(grad_attn.astype(jnp.float32), axis=0)
    grad_mixed = back_dot(grad_attn, output_full).astype(jnp.bfloat16)
    grad_query_edge, rim_low, rim_high, grad_edge = attend_back(
        True, queries, attn_mixed, grad_mixed, row_peaks, key_value, marks, halo
    )
    from_next = lax.ppermute(rim_low, "seq", back)
    from_prev = lax.ppermute(rim_high, "seq", onward)
    grad_query, own_grad = attend_back(
        False, queries, attn_mixed, grad_mixed, row_peaks, key_value, marks, (), (grad_edge, grad_query_edge)
    )
    own_grad = own_grad.at[:MAXLEN].add(from_prev.astype(jnp.float32))
    own_grad = own_grad.at[row_count - MAXLEN :].add(from_next.astype(jnp.float32))
    grad_packed = jnp.concatenate([grad_query, own_grad.astype(jnp.bfloat16)], axis=1)
    grad_input_weight = outer_sum(input_attn, grad_packed)
    packed_sums = jnp.sum(grad_packed.astype(jnp.float32), axis=0)
    grad_query_value_bias = jnp.concatenate(
        [packed_sums[:model_width], packed_sums[2 * model_width :]]
    )
    grad_input_attn = back_dot(grad_packed, input_full)
    grad_scale_mixer = grad_input_attn * normed_attn
    grad_rows = grad_middle + norm_back(
        grad_input_attn * (1.0 + scale_mixer), normed_attn, inverse_attn
    )
    grad_per_row = jnp.concatenate(
        [
            grad_input_attn,
            grad_scale_mixer,
            grad_gate_mixer,
            grad_input_feed,
            grad_scale_feed,
            grad_gate_feed,
        ],
        axis=1,
    )
    window_grads = lax.dot_general(
        image_select, grad_per_row, (((0,), (0,)), ((), ())), precision=highest
    )
    image_grads = lax.dynamic_update_slice_in_dim(
        jnp.zeros((images, window_grads.shape[1]), jnp.float32), window_grads, first_image, 0
    )
    column_grads = lax.psum_scatter(image_grads, "seq", scatter_dimension=1, tiled=True)
    columns = column_grads.shape[1]
    silu_all, silu_all_back = jax.vjp(jax.nn.silu, conditions.astype(jnp.float32))
    cond_act = silu_all.astype(jnp.bfloat16)
    all_grads = lax.all_gather(column_grads, "dp", axis=0, tiled=True)
    all_act = lax.all_gather(cond_act, "dp", axis=0, tiled=True)
    share_rows = modulation_weight.shape[0]
    own_act = lax.dynamic_slice_in_dim(all_act, lax.axis_index("dp") * share_rows, share_rows, 1)
    total_modulation = lax.dot_general(
        own_act.astype(jnp.float32), all_grads, (((0,), (0,)), ((), ())), precision=highest
    )
    own_columns = lax.dynamic_slice_in_dim(
        modulation_full, lax.axis_index("seq") * columns, columns, 1
    )
    grad_condition = silu_all_back(lax.dot_general(
        column_grads, own_columns.astype(jnp.float32), (((1,), (1,)), ((), ())), precision=highest
    ))[0]
    grad_condition = lax.psum_scatter(grad_condition, "seq", scatter_dimension=0, tiled=True)
    grad_modulation_bias = jnp.sum(window_grads, axis=0)
    total_contract = share_of_sum(grad_contract_weight)
    total_expand = share_of_sum(grad_expand_weight)
    total_output = share_of_sum(grad_output_weight)
    total_input = share_of_sum(grad_input_weight)
    bias_modulation, bias_query_value, bias_output, bias_expand, bias_contract = lax.psum(
        (
            grad_modulation_bias,
            grad_query_value_bias,
            grad_output_bias,
            grad_expand_bias,
            grad_contract_bias,
        ),
        ("dp", "seq"),
    )
    return (
        layer_out[None],
        grad_rows[None],
        grad_condition[None],
        total_modulation,
        bias_modulation,
        total_input,
        bias_query_value,
        total_output,
        bias_output,
        total_expand,
        bias_expand,
        total_contract,
        bias_contract,
    )


def solution(mesh):
    in_specs = (
        P("dp", "seq", None),
        P("dp", "seq"),
        P("dp", None, None),
        P("dp", "seq", None),
        P("dp", None),
        P(),
        P("dp", None),
        P(),
        P("dp", None),
        P(),
        P("dp", None),
        P(),
        P("dp", None),
        P(),
    )
    out_specs = (
        P("dp", "seq", None),
        P("dp", "seq", None),
        P("dp", "seq", None),
        P("dp", "seq"),
        P(),
        P("dp", "seq"),
        P(),
        P("dp", "seq"),
        P(),
        P("dp", "seq"),
        P(),
        P("dp", "seq"),
        P(),
    )
    return jax.shard_map(shards, mesh=mesh, in_specs=in_specs, out_specs=out_specs, check_vma=False)
```

time: 2680 us -> 1080 us (0.40)
  waiting for transfers between devices: 1760 us -> 248 us
  matrix products: 470 us -> 233 us
  Pallas kernels: 0 us -> 149 us
  blocking collectives: 41.5 us -> 149 us
  local copies, waits for them, and re-layouts: 188 us -> 112 us
  other arithmetic: 164 us -> 116 us
    reduce_scatter x6 -> x0, waiting for transfers between devices: 1380 us -> none  [the longest x1 512 us: shards(): lax.psum_scatter(grad_modulation_weight, 'seq', scatter_dimension=1, tile...]
    dot_general x16 -> x2, matrix products: 236 us -> 7.77 us  [the longest x1 5.1 us: shards(): lax.dot_general(column_grads, own_columns.astype(jnp.float32), (((1,), (1...]
    unnamed x21 -> x9, waiting for transfers between devices: 172 us -> 2.63 us
    pallas_call x0 -> x4, Pallas kernels: none -> 149 us  [the longest x2 103 us: backward(): pl.pallas_call(functools.partial(backward_kernel, edge), grid=(steps,), i...]
    all_gather x0 -> x2, blocking collectives: none -> 106 us  [the longest x1 96 us: shards(): all_grads = lax.all_gather(column_grads, 'dp', axis=0, tiled=True)]
    ppermute x6 -> x26, waiting for transfers between devices: 81.5 us -> 137 us  [the longest x20 126 us: halve(): got = lax.ppermute(sent.astype(jnp.bfloat16), axis, partners(axis, bit))]
    dynamic_update_slice x15 -> x1, local copies, waits for them, and re-layouts: 45.1 us -> 1.54 us  [shards(): lax.dynamic_update_slice_in_dim(jnp.zeros((images, window_grads.shape[1])...]
    dynamic_slice x16 -> x0, local copies, waits for them, and re-layouts: 35 us -> none  [the longest x4 32.1 us: backward_block(): current = lax.dynamic_slice_in_dim(wide_carry, block_start, window_rows, 0)]
  transfers between devices with their start and end apart: 22 -> 33, of which waited for: 15 -> 11; matrix products, arithmetic and copies ran while one was open for 26% -> 41% of each run, Pallas kernels for 0% -> 14%
where the time goes in v1:
time: 1080 us; the launch traced here: 1070 us
  waiting for transfers between devices  248 us (23%)
  matrix products  233 us (22%)
  blocking collectives  149 us (14%)
  Pallas kernels  149 us (14%)
  other arithmetic  116 us (11%)
  local copies, waits for them, and re-layouts  112 us (10%)
  starting transfers between devices  45.2 us (4%)
  between operations  16.8 us (2%)
    ppermute x20, waiting for transfers between devices, halve(): got = lax.ppermute(sent.astype(jnp.bfloat16), axis, partners(axis, bit))  126 us
    pallas_call x2, Pallas kernels, backward(): pl.pallas_call(functools.partial(backward_kernel, edge), grid=(steps,), i...  103 us
    all_gather x1, blocking collectives, shards(): all_grads = lax.all_gather(column_grads, 'dp', axis=0, tiled=True)  96 us
    all_gather x1, waiting for transfers between devices, shards(): lax.all_gather(modulation_weight, 'dp', axis=0, tiled=True)  82.3 us
    dot_general x4, matrix products, back_dot(): lax.dot_general(gradient, matrix, (((1,), (1,)), ((), ())), preferred_ele...  72.5 us
    dot_general x4, matrix products, outer_sum(): lax.dot_general(first_matrix, second_matrix, (((0,), (0,)), ((), ())), pr...  56.3 us
    pallas_call x2, Pallas kernels, forward(): pl.pallas_call(functools.partial(forward_kernel, edge), grid=(steps,), in...  46.4 us
    psum x1, blocking collectives, shards(): lax.psum((grad_modulation_bias, grad_query_value_bias, grad_output_bias,...  42.2 us
  transfers between devices with their start and end apart: 33, of which 11 were waited for; matrix products, arithmetic and copies ran while one was open for 41% of the time, Pallas kernels for 14%

profile of v1, /device:TPU:0, one launch (start us, length us, event | category | flops | bytes accessed | tf_op | source)
XLA Modules:
  0.0 1069.3 jit_solution(12930239136911191345)
XLA Ops:
  12.7 5.5 collective-permute-start.2
  20.4 10.4 all_gather.26
  32.8 82.3 %all-gather.6.cloned.1.call-done = bf16[1152,6912]{1,0:T(8,128)(2,1)} async-done(((bf16[288,6912]{1,0:T(8,128)(2,1)}), bf16[1152,6912]{1,0:T(8,128)(2,1)}) %all-gather.6.cloned.1.call-update) | async-done | bytes 15925264 | tf_op jit(solution)/shard_map/all_gather | solution.py:392
  115.1 7.7 convolution_add_fusion
  122.9 11.7 %fusion.46 = f32[1024,6912]{1,0:T(8,128)S(1)} fusion(f32[18,6912]{1,0:T(8,128)S(1)} %convolution_add_fusion, s32[1024]{0:T(1024)S(1)} %bitcast.235), kind=kOutput, calls=%fused_computation.119 | convolution fusion | flops 1528842240 | bytes 28813312 | tf_op jit(solution)/shard_map/dot_general | solution.py:413
  134.6 9.4 copy-done
  146.5 26.3 %all-gather.8.cloned.1.call-done = bf16[1152,3456]{1,0:T(8,128)(2,1)} async-done(((bf16[288,3456]{1,0:T(8,128)(2,1)}), bf16[1152,3456]{1,0:T(8,128)(2,1)}) %all-gather.8.cloned.1.call-update) | async-done | bytes 7962640 | tf_op jit(solution)/shard_map/all_gather | solution.py:393
  172.7 13.0 %fusion.87 = f32[1024,3456]{1,0:T(8,128)S(1)} fusion(bf16[1024,1152]{1,0:T(8,128)(2,1)} %fusion.17, bf16[1152,3456]{1,0:T(8,128)(2,1)} %all-gather.8.cloned.1.call-done), kind=kOutput, calls=%fused_computation.184 | convolution fusion | flops 8153726976 | bytes 24477696 | tf_op jit(solution)/shard_map/dot_general | solution.py:419
  190.9 5.5 collective-permute-start
  198.9 22.7 %attend_inner.1 = (bf16[1024,1152]{1,0:T(8,128)(2,1)}, f32[16,1024]{1,0:T(8,128)}) custom-call(bf16[1024,1152]{1,0:T(8,128)(2,1)} %get-tuple-element.78.refs_0_, bf16[1024,2304]{1,0:T(8,128)(2,1)} %pad_maximum_fusion.1.refs_1_.refs_4_, s32[4,1,640]{2,1,0:T(1,128)} %broadcast_in_dim.10.refs_2_.refs_4_.refs_7_.refs_5_, s32[4,1,256]{2,1,0:T(1,128)} %bitcast.238), custom_call_target="tpu_custom_call" | custom-call | flops 5368709120 | bytes 7077888 | tf_op jit(solution)/shard_map/attend_inner/pallas_call | solution.py:248
  221.6 10.8 %collective-permute-done.refs_2_.refs_5_ = bf16[192,2304]{1,0:T(8,128)(2,1)} collective-permute-done((bf16[192,2304]{1,0:T(8,128)(2,1)S(1)}, bf16[192,2304]{1,0:T(8,128)(2,1)}, u32[]{:S(2)}, u32[]{:S(2)}) %collective-permute-start) | collective-permute-done | bytes 884768 | tf_op jit(solution)/shard_map/ppermute | solution.py:435
  232.4 23.6 %attend_edge.1 = (bf16[1024,1152]{1,0:T(8,128)(2,1)}, f32[16,1024]{1,0:T(8,128)}) custom-call(bf16[1024,1152]{1,0:T(8,128)(2,1)} %get-tuple-element.78.refs_0_, bf16[1024,2304]{1,0:T(8,128)(2,1)} %pad_maximum_fusion.1.refs_1_.refs_4_, bf16[192,2304]{1,0:T(8,128)(2,1)} %collective-permute-done.refs_2_.refs_5_, ...), custom_call_target="tpu_custom_call", output_to_operand_aliasing={{0}: (6, {}), {1}: (7, {})} | custom-call | flops 5368709120 | bytes 7077888 | tf_op jit(solution)/shard_map/attend_edge/pallas_call | solution.py:248
  256.0 9.6 fusion.80
  269.0 8.2 convert_reduce_fusion.3
  277.1 18.9 %fusion.88 = f32[1024,4608]{1,0:T(8,128)} fusion(bf16[1024,1152]{1,0:T(8,128)(2,1)S(1)} %get-tuple-element.76, bf16[1152,4608]{1,0:T(8,128)(2,1)} %all-gather.12.cloned.1.call-done), kind=kOutput, calls=%fused_computation.185 | convolution fusion | flops 10871635968 | bytes 31850496 | tf_op jit(solution)/shard_map/dot_general | solution.py:447
  296.0 24.0 %fusion.77 = f32[4608,1152]{1,0:T(8,128)} fusion(bf16[1024,1152]{1,0:T(8,128)(2,1)S(1)} %copy-done.18, f32[1024,4608]{1,0:T(8,128)} %fusion.88, f32[4608]{0:T(1024)S(1)} %convert_element_type.308), kind=kOutput, calls=%fused_computation.177 | convolution fusion | flops 10918821888 | bytes 42485760 | tf_op jit(solution)/shard_map/dot_general | solution.py:364
  320.0 8.8 constant_dynamic-slice_fusion.1
  328.8 12.7 %copy.64 = f32[2,1,1152,1152]{2,3,0,1:T(8,128)} copy(f32[2,1,1152,1152]{3,2,1,0:T(8,128)} %constant_dynamic-slice_fusion.1) | data formatting | bytes 21233664 | tf_op jit(solution)/shard_map/dynamic-slice.47
  341.5 7.0 constant_dynamic-slice_fusion
  348.6 8.6 copy.72
  357.1 28.6 %convert_reduce_fusion = (f32[4608]{0:T(1024)}, bf16[1024,4608]{1,0:T(8,128)(2,1)S(1)}) fusion(f32[1024,4608]{1,0:T(8,128)} %fusion.88, f32[4608]{0:T(1024)S(1)} %convert_element_type.308, bf16[1024,1152]{1,0:T(8,128)(2,1)} %get-tuple-element.67, bf16[4608,1152]{1,0:T(8,128)(2,1)} %all-gather.14.cloned.1.call-done), kind=kOutput, calls=%fused_computation.9 | convolution fusion | flops 10980159488 | bytes 41324544 | tf_op jit(solution)/shard_map/dot_general | solution.py:370
  385.8 3.6 copy-done.44
  389.3 14.6 %fusion.90 = f32[1152,4608]{1,0:T(8,128)} fusion(bf16[1024,1152]{1,0:T(8,128)(2,1)S(1)} %get-tuple-element.76, bf16[1024,4608]{1,0:T(8,128)(2,1)S(1)} %get-tuple-element.69), kind=kOutput, calls=%fused_computation.187 | convolution fusion | flops 10871635968 | bytes 33030144 | tf_op jit(solution)/shard_map/dot_general | solution.py:364
  403.9 22.6 %fusion.75 = (f32[1024]{0:T(1024)S(1)}, f32[1024]{0:T(1024)S(1)}, f32[1024,1152]{1,0:T(8,128)}) fusion(f32[1024,6912]{1,0:T(8,128)} %copy-done, f32[1024]{0:T(1024)S(1)} %copy-done.31, f32[1024,1152]{1,0:T(8,128)} %copy-done.1, f32[1024]{0:T(1024)S(1)} %copy-done.27, bf16[1024,4608]{1,0:T(8,128)(2,1)} %copy-done.44, ...), kind=kOutput, calls=%fused_computation.175 | convolution fusion | flops 10879891456 | bytes 34226176 | tf_op jit(solution)/shard_map/dot_general | solution.py:370
  426.5 21.9 %convolution_add_fusion.1 = f32[1024,1152]{1,0:T(8,128)} fusion(bf16[4608,1152]{1,0:T(8,128)(2,1)} %all-gather.14.cloned.1.call-done, f32[1152]{0:T(1024)S(1)} %copy-done.38, f32[1024,4608]{1,0:T(8,128)} %fusion.88, f32[4608]{0:T(1024)S(1)} %convert_element_type.308), kind=kOutput, calls=%fused_computation.43 | convolution fusion | flops 10920001536 | bytes 34232832 | tf_op jit(solution)/shard_map/dot_general | solution.py:452
  448.5 10.9 %convert_reduce_fusion.4 = (f32[1152]{0:T(1024)S(1)}, bf16[1024,1152]{1,0:T(8,128)(2,1)}, f32[1024,1152]{1,0:T(8,128)}, bf16[1,1024,1152]{2,1,0:T(8,128)(2,1)}) fusion(f32[1024,6912]{1,0:T(8,128)} %copy-done, f32[1024]{0:T(1024)S(1)} %get-tuple-element.101, f32[1024,1152]{1,0:T(8,128)S(1)} %bitcast.193, f32[1024]{0:T(1024)S(1)} %copy-done.27, ...), kind=kLoop, calls=%fused_computation.65 | loop fusion | flops 20052864 | bytes 40129024 | tf_op jit(solution)/shard_map/reduce_sum | solution.py:472
  459.4 5.8 fusion.89
  469.3 4.8 convolution_convert_fusion.refs_2_
  474.0 50.6 %attend_back_edge.1 = (bf16[1024,1152]{1,0:T(8,128)(2,1)}, bf16[192,2304]{1,0:T(8,128)(2,1)}, bf16[192,2304]{1,0:T(8,128)(2,1)}, f32[2,448,2304]{2,1,0:T(8,128)}) custom-call(bf16[1024,1152]{1,0:T(8,128)(2,1)} %get-tuple-element.78.refs_0_, bf16[1024,1152]{1,0:T(8,128)(2,1)} %get-tuple-element.49.refs_1_, ...), custom_call_target="tpu_custom_call" | custom-call | flops 13421772800 | bytes 18874368 | tf_op jit(solution)/shard_map/attend_back_edge/pallas_call | solution.py:290
  524.7 5.4 collective-permute-start.4
  531.4 52.4 %attend_back_inner.1 = (bf16[1024,1152]{1,0:T(8,128)(2,1)}, f32[1024,2304]{1,0:T(8,128)}) custom-call(bf16[1024,1152]{1,0:T(8,128)(2,1)} %get-tuple-element.78.refs_0_, bf16[1024,1152]{1,0:T(8,128)(2,1)} %get-tuple-element.49.refs_1_, bf16[1024,1152]{1,0:T(8,128)(2,1)} %convolution_convert_fusion.refs_2_, ...), custom_call_target="tpu_custom_call", output_to_operand_aliasing={{0}: (8, {})} | custom-call | flops 13421772800 | bytes 18874368 | tf_op jit(solution)/shard_map/attend_back_inner/pallas_call | solution.py:290
  583.8 3.1 add_dynamic-update-slice_fusion
  589.8 4.3 convert_element_type.320
  594.8 11.9 %fusion.36 = f32[1152,3456]{1,0:T(8,128)} fusion(bf16[1024,1152]{1,0:T(8,128)(2,1)S(1)} %copy-done.17, bf16[1024,2304]{1,0:T(8,128)(2,1)S(1)} %convert_element_type.320, bf16[1024,1152]{1,0:T(8,128)(2,1)S(1)} %copy-done.16), kind=kOutput, calls=%fused_computation.88 | convolution fusion | flops 8167882752 | bytes 25362432 | tf_op jit(solution)/shard_map/dot_general | solution.py:364
  606.8 5.7 fusion.32
  612.6 16.5 %constant_dynamic-update-slice_fusion.1 = (f32[1024,6912]{1,0:T(8,128)}, f32[1024,1152]{1,0:T(8,128)}) fusion(bf16[1152,3456]{1,0:T(8,128)(2,1)} %all-gather.8.cloned.1.call-done, bf16[1024,2304]{1,0:T(8,128)(2,1)} %copy-done.8, bf16[1024,1152]{1,0:T(8,128)(2,1)} %get-tuple-element.53), kind=kOutput, calls=%fused_computation.151 | convolution fusion | flops 8167882752 | bytes 24477696 | tf_op jit(solution)/shard_map/dot_general | solution.py:370
  629.1 4.9 fusion.76
  634.1 8.2 fusion.23
  642.3 2.9 multiply_dynamic-update-slice_fusion.1
  653.4 13.9 %fusion.86 = (f32[6912]{0:T(1024)S(1)}, f32[18,6912]{1,0:T(8,128)S(1)}) fusion(f32[1024,6912]{1,0:T(8,128)} %fusion.26, s32[1024]{0:T(1024)S(1)} %bitcast.236), kind=kOutput, calls=%fused_computation.183 | convolution fusion | flops 1528959744 | bytes 28840960 | tf_op jit(solution)/shard_map/dot_general | solution.py:506
  674.5 7.2 fusion.15
  681.7 9.7 collective-permute-done.12
  694.7 4.3 convert_reduce_fusion.1
  699.0 9.6 collective-permute-done.13
  710.5 6.0 collective-permute-done.14
  718.6 42.2 %all-reduce.1 = (f32[6912]{0:T(1024)}, f32[2304]{0:T(1024)}, f32[1152]{0:T(1024)}, f32[4608]{0:T(1024)}, f32[1152]{0:T(1024)}) all-reduce(f32[6912]{0:T(1024)S(1)} %get-tuple-element.99, f32[2304]{0:T(1024)S(1)} %pad_maximum_fusion.4, f32[1152]{0:T(1024)S(1)} %get-tuple-element.70, ...), channel_id=1, replica_groups=mesh['dp'=4,'seq'=8] {'dp','seq'}, use_global_device_ids=true, to_apply=%region_11.12 | all-reduce | flops 16128 | bytes 129024 | tf_op jit(solution)/shard_map/psum | solution.py:535
  763.3 5.1 fusion.48
  768.4 5.2 bitcast_add_fusion.2
  773.6 3.1 copy-done.5
  779.2 10.4 bitcast_add_fusion
  789.6 4.3 dynamic-slice_convert_fusion
  793.9 11.2 %bitcast_add_fusion.1 = f32[2,288,4608]{2,1,0:T(8,128)} fusion(bf16[2,288,4608]{2,1,0:T(8,128)(2,1)} %collective-permute-done.16, f32[2,2,288,4608]{3,2,1,0:T(8,128)} %bitcast.208, s32[]{:T(128)S(6)} %select_n.174), kind=kLoop, calls=%fused_computation.14 | loop fusion | flops 5308416 | bytes 26542084 | tf_op jit(solution)/shard_map/add | solution.py:328
  805.2 18.4 %collective-permute-done.7 = bf16[1,288,3456]{2,1,0:T(8,128)(2,1)} collective-permute-done((bf16[1,288,3456]{2,1,0:T(8,128)(2,1)S(1)}, bf16[1,288,3456]{2,1,0:T(8,128)(2,1)}, u32[]{:S(2)}, u32[]{:S(2)}) %collective-permute-start.7) | collective-permute-done | bytes 1990688 | tf_op jit(solution)/shard_map/ppermute | solution.py:327
  823.6 4.4 add_convert_fusion.3
  828.0 6.2 convert_element_type.330
  839.4 4.3 dynamic-slice_convert_fusion.1
  845.3 96.0 %all_gather.27 = f32[256,864]{1,0:T(8,128)S(1)} all-gather(f32[64,864]{1,0:T(8,128)S(1)} %copy-done.19), channel_id=1, replica_groups=mesh['dp'=4,'seq'=8] {'dp'}, dimensions={0}, use_global_device_ids=true | all-gather | bytes 1105920 | tf_op jit(solution)/shard_map/all_gather | solution.py:516
  949.2 3.8 add_convert_fusion
  955.9 3.9 add_convert_fusion.1
  959.8 4.8 convert_element_type.362
  968.9 17.7 %collective-permute-done.23 = bf16[4,1152,144]{1,2,0:T(8,128)(2,1)} collective-permute-done((bf16[4,1152,144]{1,2,0:T(8,128)(2,1)}, bf16[4,1152,144]{1,2,0:T(8,128)(2,1)}, u32[]{:S(2)}, u32[]{:S(2)}) %collective-permute-start.23) | collective-permute-done | bytes 1327136 | tf_op jit(solution)/shard_map/ppermute | solution.py:327
  991.1 26.4 %collective-permute-done.18 = bf16[4,288,576]{2,1,0:T(8,128)(2,1)S(1)} collective-permute-done((bf16[4,288,576]{2,1,0:T(8,128)(2,1)S(1)}, bf16[4,288,576]{2,1,0:T(8,128)(2,1)S(1)}, u32[]{:S(2)}, u32[]{:S(2)}) %collective-permute-start.18) | collective-permute-done | bytes 1327136 | tf_op jit(solution)/shard_map/ppermute | solution.py:327
  1021.3 21.9 %collective-permute-done.19 = bf16[2,288,576]{2,1,0:T(8,128)(2,1)S(1)} collective-permute-done((bf16[2,288,576]{2,1,0:T(8,128)(2,1)S(1)}, bf16[2,288,576]{2,1,0:T(8,128)(2,1)S(1)}, u32[]{:S(2)}, u32[]{:S(2)}) %collective-permute-start.19) | collective-permute-done | bytes 663584 | tf_op jit(solution)/shard_map/ppermute | solution.py:327
  1044.8 16.5 %collective-permute-done.20 = bf16[1,288,576]{2,1,0:T(8,128)(2,1)S(1)} collective-permute-done((bf16[1,288,576]{2,1,0:T(8,128)(2,1)S(1)}, bf16[1,288,576]{2,1,0:T(8,128)(2,1)S(1)}, u32[]{:S(2)}, u32[]{:S(2)}) %collective-permute-start.20) | collective-permute-done | bytes 331808 | tf_op jit(solution)/shard_map/ppermute | solution.py:327
  (258 shorter events, 90.8 us)
Async XLA Ops:
  7.2 107.9 %all-gather.6.cloned.1.call-start = ((), (), s32[]{:S(2)}) async-start(), calls=%async_computation.1 | async-start | bytes 19906560 | tf_op jit(solution)/shard_map/all_gather | solution.py:392
  7.9 164.8 %all-gather.8.cloned.1.call-start = ((), (), s32[]{:S(2)}) async-start(), calls=%async_computation.2 | async-start | bytes 9953280 | tf_op jit(solution)/shard_map/all_gather | solution.py:393
  8.7 247.3 %all-gather.10.cloned.1.call-start = ((), (), s32[]{:S(2)}) async-start(), calls=%async_computation.3 | async-start | bytes 3317760 | tf_op jit(solution)/shard_map/all_gather | solution.py:394
  9.5 10.8 %copy-start.36 = (bf16[6912]{0:T(1024)(128)(2,1)S(1)}, bf16[6912]{0:T(1024)(128)(2,1)}, u32[]{:S(2)}) copy-start(bf16[6912]{0:T(1024)(128)(2,1)} %param.23) | copy-start | bytes 41476
  9.5 10.9 %copy-start.22 = (bf16[1,64,1152]{2,1,0:T(8,128)(2,1)S(1)}, bf16[1,64,1152]{2,1,0:T(8,128)(2,1)}, u32[]{:S(2)}) copy-start(bf16[1,64,1152]{2,1,0:T(8,128)(2,1)} %param.20) | copy-start | bytes 442372
  9.5 267.7 %all-gather.12.cloned.1.call-start = ((), (), s32[]{:S(2)}) async-start(), calls=%async_computation.4 | async-start | bytes 13271040 | tf_op jit(solution)/shard_map/all_gather | solution.py:395
  10.1 20.8 %copy-start.43 = (u32[32]{0:T(128)S(1)}, u32[32]{0:T(128)}, u32[]{:S(2)}) copy-start(u32[32]{0:T(128)} %constant.375) | copy-start | bytes 388
  10.1 347.1 %all-gather.14.cloned.1.call-start = ((), (), s32[]{:S(2)}) async-start(), calls=%async_computation.5 | async-start | bytes 13271040 | tf_op jit(solution)/shard_map/all_gather | solution.py:396
  11.3 111.5 %copy-start.32 = (s32[1,1024]{1,0:T(1,128)}, s32[1,1024]{1,0:T(1,128)S(1)}, u32[]{:S(2)}) copy-start(s32[1,1024]{1,0:T(1,128)S(1)} %get-tuple-element.93) | copy-start | bytes 12292
  11.3 111.5 %copy-start.20 = (s32[1,1024]{1,0:T(1,128)}, s32[1,1024]{1,0:T(1,128)S(1)}, u32[]{:S(2)}) copy-start(s32[1,1024]{1,0:T(1,128)S(1)} %get-tuple-element.94) | copy-start | bytes 12292
  11.4 20.6 %collective-permute-start.3 = (s32[192]{0:T(256)S(1)}, s32[192]{0:T(256)S(1)}, u32[]{:S(2)}, u32[]{:S(2)}) collective-permute-start(s32[192]{0:T(256)S(1)} %bitcast.243), channel_id=1, source_target_pairs={{1,0},{2,1},{3,2},{4,3},{5,4},{6,5},{7,6},{9,8},{10,9},{11,10},{12... | collective-permute-start | bytes 2312 | tf_op jit(solution)/shard_map/ppermute | solution.py:432
  12.7 19.4 %collective-permute-start.2 = (s32[192]{0:T(256)S(1)}, s32[192]{0:T(256)S(1)}, u32[]{:S(2)}, u32[]{:S(2)}) collective-permute-start(s32[192]{0:T(256)S(1)} %bitcast.242), channel_id=1, source_target_pairs={{0,1},{1,2},{2,3},{3,4},{4,5},{5,6},{6,7},{8,9},{9,10},{10,11},{11... | collective-permute-start | bytes 2312 | tf_op jit(solution)/shard_map/ppermute | solution.py:431
  18.2 743.2 %reduce-scatter.4.cloned.1.call-start = ((), (), s32[]{:S(2)}) async-start(), calls=%async_computation.6 | async-start | bytes 3981312
  18.9 115.7 %copy-start.24 = (f32[1024]{0:T(1024)}, f32[1024]{0:T(1024)S(1)}, u32[]{:S(2)}) copy-start(f32[1024]{0:T(1024)S(1)} %broadcast_multiply_fusion.5) | copy-start | bytes 12292
  19.6 114.9 %copy-start.28 = (f32[1024]{0:T(1024)}, f32[1024]{0:T(1024)S(1)}, u32[]{:S(2)}) copy-start(f32[1024]{0:T(1024)S(1)} %add_rsqrt_fusion.1) | copy-start | bytes 12292
  189.3 32.3 %collective-permute-start.1 = (bf16[192,2304]{1,0:T(8,128)(2,1)}, bf16[192,2304]{1,0:T(8,128)(2,1)}, u32[]{:S(2)}, u32[]{:S(2)}) collective-permute-start(bf16[192,2304]{1,0:T(8,128)(2,1)} %get-tuple-element.81), channel_id=1, source_target_pairs={{1,0},{2,1},{3,2},{4,3},{5,4},{6,5},{7,6},{9,8},{10,9},{11,10},{12... | collective-permute-start | bytes 2654216 | tf_op jit(solution)/shard_map/ppermute | solution.py:436
  190.9 41.5 %collective-permute-start = (bf16[192,2304]{1,0:T(8,128)(2,1)S(1)}, bf16[192,2304]{1,0:T(8,128)(2,1)}, u32[]{:S(2)}, u32[]{:S(2)}) collective-permute-start(bf16[192,2304]{1,0:T(8,128)(2,1)S(1)} %get-tuple-element.82), channel_id=1, source_target_pairs={{0,1},{1,2},{2,3},{3,4},{4,5},{5,6},{6,7},{8,9},{9,10},{10,11},{11... | collective-permute-start | bytes 2654216 | tf_op jit(solution)/shard_map/ppermute | solution.py:435
  277.1 18.9 %copy-start.18 = (bf16[1024,1152]{1,0:T(8,128)(2,1)S(1)}, bf16[1024,1152]{1,0:T(8,128)(2,1)}, u32[]{:S(2)}) copy-start(bf16[1024,1152]{1,0:T(8,128)(2,1)} %get-tuple-element.67) | copy-start | bytes 7077892
  357.1 422.1 %collective-permute-start.21 = (bf16[2,1152,1152]{1,2,0:T(8,128)(2,1)}, bf16[2,1152,1152]{1,2,0:T(8,128)(2,1)}, u32[]{:S(2)}, u32[]{:S(2)}) collective-permute-start(bf16[2,1152,1152]{1,2,0:T(8,128)(2,1)} %bitcast.225), channel_id=1, source_target_pairs={{0,8},{8,0},{16,24},{24,16},{1,9},{9,1},{17,25},{25,17},{2,10},{10... | collective-permute-start | bytes 15925256 | tf_op jit(solution)/shard_map/ppermute | solution.py:327
  389.3 14.6 %copy-start.27 = (f32[1024]{0:T(1024)S(1)}, f32[1024]{0:T(1024)}, u32[]{:S(2)}) copy-start(f32[1024]{0:T(1024)} %copy-done.26) | copy-start | bytes 12292
  389.3 14.6 %copy-start.31 = (f32[1024]{0:T(1024)S(1)}, f32[1024]{0:T(1024)}, u32[]{:S(2)}) copy-start(f32[1024]{0:T(1024)} %copy-done.30) | copy-start | bytes 12292
  403.9 22.6 %copy-start.38 = (f32[1152]{0:T(1024)S(1)}, f32[1152]{0:T(1024)}, u32[]{:S(2)}) copy-start(f32[1152]{0:T(1024)} %convert_element_type.310) | copy-start | bytes 13828
  403.9 44.6 %slice-start = ((s8[4718592]{0:T(1024)(128)(4,1)}), s8[524288]{0:T(1024)(128)(4,1)S(1)}, s32[]{:S(2)}) async-start(s8[4718592]{0:T(1024)(128)(4,1)} %bitcast.192), calls=%async_computation.8 | async-start | bytes 1048576
  426.5 22.0 %slice-start.1 = ((s8[4718592]{0:T(1024)(128)(4,1)}), s8[4194304]{0:T(1024)(128)(4,1)S(1)}, s32[]{:S(2)}) async-start(s8[4718592]{0:T(1024)(128)(4,1)} %bitcast.192), calls=%async_computation.9 | async-start | bytes 8388608
  426.5 22.0 %copy-start.4 = (f32[1024,1152]{1,0:T(8,128)S(1)}, f32[1024,1152]{1,0:T(8,128)}, u32[]{:S(2)}) copy-start(f32[1024,1152]{1,0:T(8,128)} %get-tuple-element.96) | copy-start | bytes 14155780
  426.5 22.0 %copy-start.7 = (bf16[1,1024,1152]{2,1,0:T(8,128)(2,1)S(1)}, bf16[1,1024,1152]{2,1,0:T(8,128)(2,1)}, u32[]{:S(2)}) copy-start(bf16[1,1024,1152]{2,1,0:T(8,128)(2,1)} %param.21) | copy-start | bytes 7077892
  468.8 202.8 %collective-permute-start.11 = (bf16[2,288,1152]{2,1,0:T(8,128)(2,1)}, bf16[2,288,1152]{2,1,0:T(8,128)(2,1)}, u32[]{:S(2)}, u32[]{:S(2)}) collective-permute-start(bf16[2,288,1152]{2,1,0:T(8,128)(2,1)} %fusion.39), channel_id=1, source_target_pairs={{0,8},{8,0},{16,24},{24,16},{1,9},{9,1},{17,25},{25,17},{2,10},{10... | collective-permute-start | bytes 3981320 | tf_op jit(solution)/shard_map/ppermute | solution.py:327
  524.7 59.2 %collective-permute-start.4 = (bf16[192,2304]{1,0:T(8,128)(2,1)}, bf16[192,2304]{1,0:T(8,128)(2,1)}, u32[]{:S(2)}, u32[]{:S(2)}) collective-permute-start(bf16[192,2304]{1,0:T(8,128)(2,1)} %get-tuple-element.55), channel_id=1, source_target_pairs={{0,1},{1,2},{2,3},{3,4},{4,5},{5,6},{6,7},{8,9},{9,10},{10,11},{11... | collective-permute-start | bytes 2654216 | tf_op jit(solution)/shard_map/ppermute | solution.py:478
  530.1 56.8 %collective-permute-start.5 = (bf16[192,2304]{1,0:T(8,128)(2,1)}, bf16[192,2304]{1,0:T(8,128)(2,1)S(1)}, u32[]{:S(2)}, u32[]{:S(2)}) collective-permute-start(bf16[192,2304]{1,0:T(8,128)(2,1)} %get-tuple-element.56), channel_id=1, source_target_pairs={{1,0},{2,1},{3,2},{4,3},{5,4},{6,5},{7,6},{9,8},{10,9},{11,10},{12... | collective-permute-start | bytes 2654216 | tf_op jit(solution)/shard_map/ppermute | solution.py:477
  594.1 12.7 %copy-start.8 = (bf16[1024,2304]{1,0:T(8,128)(2,1)}, bf16[1024,2304]{1,0:T(8,128)(2,1)S(1)}, u32[]{:S(2)}) copy-start(bf16[1024,2304]{1,0:T(8,128)(2,1)S(1)} %convert_element_type.320) | copy-start | bytes 14155780
  606.8 27.2 %slice-start.6 = ((s8[4718592]{0:T(1024)(128)(4,1)}), s8[4194304]{0:T(1024)(128)(4,1)S(1)}, s32[]{:S(2)}) async-start(s8[4718592]{0:T(1024)(128)(4,1)} %bitcast.198), calls=%async_computation.14 | async-start | bytes 8388608
  612.5 16.6 %copy-start.3 = (bf16[1,1024,1152]{2,1,0:T(8,128)(2,1)S(1)}, bf16[1,1024,1152]{2,1,0:T(8,128)(2,1)}, u32[]{:S(2)}) copy-start(bf16[1,1024,1152]{2,1,0:T(8,128)(2,1)} %param.18) | copy-start | bytes 7077892
  612.5 16.6 %copy-start.25 = (f32[1024]{0:T(1024)S(1)}, f32[1024]{0:T(1024)}, u32[]{:S(2)}) copy-start(f32[1024]{0:T(1024)} %copy-done.24) | copy-start | bytes 12292
  612.5 16.6 %copy-start.29 = (f32[1024]{0:T(1024)S(1)}, f32[1024]{0:T(1024)}, u32[]{:S(2)}) copy-start(f32[1024]{0:T(1024)} %copy-done.28) | copy-start | bytes 12292
  612.5 21.5 %slice-start.7 = ((s8[4718592]{0:T(1024)(128)(4,1)}), s8[524288]{0:T(1024)(128)(4,1)S(1)}, s32[]{:S(2)}) async-start(s8[4718592]{0:T(1024)(128)(4,1)} %bitcast.198), calls=%async_computation.15 | async-start | bytes 1048576
  612.5 156.0 %collective-permute-start.6 = (bf16[2,288,3456]{2,1,0:T(8,128)(2,1)}, bf16[2,288,3456]{2,1,0:T(8,128)(2,1)}, u32[]{:S(2)}, u32[]{:S(2)}) collective-permute-start(bf16[2,288,3456]{2,1,0:T(8,128)(2,1)} %fusion.32), channel_id=1, source_target_pairs={{0,8},{8,0},{16,24},{24,16},{1,9},{9,1},{17,25},{25,17},{2,10},{10... | collective-permute-start | bytes 11943944 | tf_op jit(solution)/shard_map/ppermute | solution.py:327
  629.1 13.2 %slice-start.13 = ((s8[4718592]{0:T(1024)(128)(4,1)}), s8[4194304]{0:T(1024)(128)(4,1)S(1)}, s32[]{:S(2)}) async-start(s8[4718592]{0:T(1024)(128)(4,1)} %bitcast.226), calls=%async_computation.21 | async-start | bytes 8388608
  629.1 16.1 %slice-start.4 = ((s8[4718592]{0:T(1024)(128)(4,1)}), s8[4194304]{0:T(1024)(128)(4,1)S(1)}, s32[]{:S(2)}) async-start(s8[4718592]{0:T(1024)(128)(4,1)} %bitcast.196), calls=%async_computation.12 | async-start | bytes 8388608
  629.1 18.8 %slice-start.2 = ((s8[4718592]{0:T(1024)(128)(4,1)}), s8[4194304]{0:T(1024)(128)(4,1)S(1)}, s32[]{:S(2)}) async-start(s8[4718592]{0:T(1024)(128)(4,1)} %bitcast.194), calls=%async_computation.10 | async-start | bytes 8388608
  634.0 11.2 %slice-start.5 = ((s8[4718592]{0:T(1024)(128)(4,1)}), s8[524288]{0:T(1024)(128)(4,1)S(1)}, s32[]{:S(2)}) async-start(s8[4718592]{0:T(1024)(128)(4,1)} %bitcast.196), calls=%async_computation.13 | async-start | bytes 1048576
  634.0 13.9 %slice-start.3 = ((s8[4718592]{0:T(1024)(128)(4,1)}), s8[524288]{0:T(1024)(128)(4,1)S(1)}, s32[]{:S(2)}) async-start(s8[4718592]{0:T(1024)(128)(4,1)} %bitcast.194), calls=%async_computation.11 | async-start | bytes 1048576
  671.5 272.4 %all-reduce.4.cloned.1.call-start = ((), (), s32[]{:S(2)}) async-start(), calls=%async_computation.7 | async-start | bytes 589824
  674.1 17.3 %collective-permute-start.12 = (bf16[1,288,1152]{2,1,0:T(8,128)(2,1)S(1)}, bf16[1,288,1152]{2,1,0:T(8,128)(2,1)S(1)}, u32[]{:S(2)}, u32[]{:S(2)}) collective-permute-start(bf16[1,288,1152]{2,1,0:T(8,128)(2,1)S(1)} %dynamic-slice_convert_fusion.5), channel_id=1, source_target_pairs={{0,16},{8,24},{16,0},{24,8},{1,17},{9,25},{17,1},{25,9},{2,18},{10... | collective-permute-start | bytes 1990664 | tf_op jit(solution)/shard_map/ppermute | solution.py:327
  681.7 112.2 %collective-permute-start.16 = (bf16[2,288,4608]{2,1,0:T(8,128)(2,1)}, bf16[2,288,4608]{2,1,0:T(8,128)(2,1)}, u32[]{:S(2)}, u32[]{:S(2)}) collective-permute-start(bf16[2,288,4608]{2,1,0:T(8,128)(2,1)} %fusion.15), channel_id=1, source_target_pairs={{0,8},{8,0},{16,24},{24,16},{1,9},{9,1},{17,25},{25,17},{2,10},{10... | collective-permute-start | bytes 15925256 | tf_op jit(solution)/shard_map/ppermute | solution.py:327
  692.0 26.5 %copy-start.34 = (f32[1152]{0:T(1024)S(1)}, f32[1152]{0:T(1024)}, u32[]{:S(2)}) copy-start(f32[1152]{0:T(1024)} %get-tuple-element.66) | copy-start | bytes 13828
  692.0 26.5 %copy-start.35 = (f32[4608]{0:T(1024)S(1)}, f32[4608]{0:T(1024)}, u32[]{:S(2)}) copy-start(f32[4608]{0:T(1024)} %get-tuple-element.68) | copy-start | bytes 55300
  692.1 71.3 %copy-start.23 = (bf16[1,64,1152]{2,1,0:T(8,128)(2,1)S(1)}, bf16[1,64,1152]{2,1,0:T(8,128)(2,1)}, u32[]{:S(2)}) copy-start(bf16[1,64,1152]{2,1,0:T(8,128)(2,1)} %param.20) | copy-start | bytes 442372
  692.1 16.5 %collective-permute-start.13 = (bf16[4,288,144]{1,2,0:T(8,128)(2,1)S(1)}, bf16[4,288,144]{1,2,0:T(8,128)(2,1)S(1)}, u32[]{:S(2)}, u32[]{:S(2)}) collective-permute-start(bf16[4,288,144]{1,2,0:T(8,128)(2,1)S(1)} %dynamic-slice_bitcast_fusion.3), channel_id=1, source_target_pairs={{0,1},{1,0},{2,3},{3,2},{4,5},{5,4},{6,7},{7,6},{8,9},{9,8},{10,11... | collective-permute-start | bytes 995336 | tf_op jit(solution)/shard_map/ppermute | solution.py:327
  708.7 7.7 collective-permute-start.14
  716.5 44.2 %collective-permute-start.15 = (bf16[1,288,144]{1,2,0:T(8,128)(2,1)S(1)}, bf16[1,288,144]{1,2,0:T(8,128)(2,1)S(1)}, u32[]{:S(2)}, u32[]{:S(2)}) collective-permute-start(bf16[1,288,144]{1,2,0:T(8,128)(2,1)S(1)} %dynamic-slice_convert_fusion.11), channel_id=1, source_target_pairs={{0,4},{1,5},{2,6},{3,7},{4,0},{5,1},{6,2},{7,3},{8,12},{9,13},{10,... | collective-permute-start | bytes 248840 | tf_op jit(solution)/shard_map/ppermute | solution.py:327
  776.9 46.6 %collective-permute-start.7 = (bf16[1,288,3456]{2,1,0:T(8,128)(2,1)S(1)}, bf16[1,288,3456]{2,1,0:T(8,128)(2,1)}, u32[]{:S(2)}, u32[]{:S(2)}) collective-permute-start(bf16[1,288,3456]{2,1,0:T(8,128)(2,1)S(1)} %dynamic-slice_convert_fusion.2), channel_id=1, source_target_pairs={{0,16},{8,24},{16,0},{24,8},{1,17},{9,25},{17,1},{25,9},{2,18},{10... | collective-permute-start | bytes 5971976 | tf_op jit(solution)/shard_map/ppermute | solution.py:327
  793.9 155.3 %collective-permute-start.22 = (bf16[1,1152,1152]{1,2,0:T(8,128)(2,1)}, bf16[1,1152,1152]{1,2,0:T(8,128)(2,1)}, u32[]{:S(2)}, u32[]{:S(2)}) collective-permute-start(bf16[1,1152,1152]{1,2,0:T(8,128)(2,1)} %dynamic-slice_convert_fusion), channel_id=1, source_target_pairs={{0,16},{8,24},{16,0},{24,8},{1,17},{9,25},{17,1},{25,9},{2,18},{10... | collective-permute-start | bytes 7962632 | tf_op jit(solution)/shard_map/ppermute | solution.py:327
  837.5 107.8 %collective-permute-start.8 = (bf16[4,288,432]{2,1,0:T(8,128)(2,1)}, bf16[4,288,432]{2,1,0:T(8,128)(2,1)S(1)}, u32[]{:S(2)}, u32[]{:S(2)}) collective-permute-start(bf16[4,288,432]{2,1,0:T(8,128)(2,1)} %dynamic-slice_bitcast_fusion.2), channel_id=1, source_target_pairs={{0,1},{1,0},{2,3},{3,2},{4,5},{5,4},{6,7},{7,6},{8,9},{9,8},{10,11... | collective-permute-start | bytes 2985992 | tf_op jit(solution)/shard_map/ppermute | solution.py:327
  843.7 112.2 %collective-permute-start.17 = (bf16[1,288,4608]{2,1,0:T(8,128)(2,1)}, bf16[1,288,4608]{2,1,0:T(8,128)(2,1)}, u32[]{:S(2)}, u32[]{:S(2)}) collective-permute-start(bf16[1,288,4608]{2,1,0:T(8,128)(2,1)} %dynamic-slice_convert_fusion.1), channel_id=1, source_target_pairs={{0,16},{8,24},{16,0},{24,8},{1,17},{9,25},{17,1},{25,9},{2,18},{10... | collective-permute-start | bytes 7962632 | tf_op jit(solution)/shard_map/ppermute | solution.py:327
  845.3 110.6 %slice-start.8 = ((s8[10616832]{0:T(1024)(128)(4,1)}), s8[2228224]{0:T(1024)(128)(4,1)S(1)}, s32[]{:S(2)}) async-start(s8[10616832]{0:T(1024)(128)(4,1)} %bitcast.200), calls=%async_computation.16 | async-start | bytes 4456448
  947.2 18.6 %collective-permute-start.9 = (bf16[2,288,432]{2,1,0:T(8,128)(2,1)S(1)}, bf16[2,288,432]{2,1,0:T(8,128)(2,1)}, u32[]{:S(2)}, u32[]{:S(2)}) collective-permute-start(bf16[2,288,432]{2,1,0:T(8,128)(2,1)S(1)} %fusion.44), channel_id=1, source_target_pairs={{0,2},{1,3},{2,0},{3,1},{4,6},{5,7},{6,4},{7,5},{8,10},{9,11},{10,... | collective-permute-start | bytes 1493000 | tf_op jit(solution)/shard_map/ppermute | solution.py:327
  954.4 32.3 %collective-permute-start.23 = (bf16[4,1152,144]{1,2,0:T(8,128)(2,1)}, bf16[4,1152,144]{1,2,0:T(8,128)(2,1)}, u32[]{:S(2)}, u32[]{:S(2)}) collective-permute-start(bf16[4,1152,144]{1,2,0:T(8,128)(2,1)} %dynamic-slice_bitcast_fusion.1), channel_id=1, source_target_pairs={{0,1},{1,0},{2,3},{3,2},{4,5},{5,4},{6,7},{7,6},{8,9},{9,8},{10,11... | collective-permute-start | bytes 3981320 | tf_op jit(solution)/shard_map/ppermute | solution.py:327
  965.0 21.7 %copy-start.10 = (bf16[1,1152,1152]{1,2,0:T(8,128)(2,1)S(1)}, bf16[1,1152,1152]{1,2,0:T(8,128)(2,1)}, u32[]{:S(2)}) copy-start(bf16[1,1152,1152]{1,2,0:T(8,128)(2,1)} %copy-done.9) | copy-start | bytes 7962628
  965.1 52.3 %collective-permute-start.18 = (bf16[4,288,576]{2,1,0:T(8,128)(2,1)S(1)}, bf16[4,288,576]{2,1,0:T(8,128)(2,1)S(1)}, u32[]{:S(2)}, u32[]{:S(2)}) collective-permute-start(bf16[4,288,576]{2,1,0:T(8,128)(2,1)S(1)} %dynamic-slice_bitcast_fusion), channel_id=1, source_target_pairs={{0,1},{1,0},{2,3},{3,2},{4,5},{5,4},{6,7},{7,6},{8,9},{9,8},{10,11... | collective-permute-start | bytes 3981320 | tf_op jit(solution)/shard_map/ppermute | solution.py:327
  967.5 22.7 %collective-permute-start.10 = (bf16[1,288,432]{2,1,0:T(8,128)(2,1)S(1)}, bf16[1,288,432]{2,1,0:T(8,128)(2,1)S(1)}, u32[]{:S(2)}, u32[]{:S(2)}) collective-permute-start(bf16[1,288,432]{2,1,0:T(8,128)(2,1)S(1)} %dynamic-slice_convert_fusion.9), channel_id=1, source_target_pairs={{0,4},{1,5},{2,6},{3,7},{4,0},{5,1},{6,2},{7,3},{8,12},{9,13},{10,... | collective-permute-start | bytes 746504 | tf_op jit(solution)/shard_map/ppermute | solution.py:327
  988.3 31.6 %collective-permute-start.24 = (bf16[2,1152,144]{1,2,0:T(8,128)(2,1)S(1)}, bf16[2,1152,144]{1,2,0:T(8,128)(2,1)S(1)}, u32[]{:S(2)}, u32[]{:S(2)}) collective-permute-start(bf16[2,1152,144]{1,2,0:T(8,128)(2,1)S(1)} %fusion.43), channel_id=1, source_target_pairs={{0,2},{1,3},{2,0},{3,1},{4,6},{5,7},{6,4},{7,5},{8,10},{9,11},{10,... | collective-permute-start | bytes 1990664 | tf_op jit(solution)/shard_map/ppermute | solution.py:327
  1017.9 25.3 %collective-permute-start.19 = (bf16[2,288,576]{2,1,0:T(8,128)(2,1)S(1)}, bf16[2,288,576]{2,1,0:T(8,128)(2,1)S(1)}, u32[]{:S(2)}, u32[]{:S(2)}) collective-permute-start(bf16[2,288,576]{2,1,0:T(8,128)(2,1)S(1)} %fusion.42), channel_id=1, source_target_pairs={{0,2},{1,3},{2,0},{3,1},{4,6},{5,7},{6,4},{7,5},{8,10},{9,11},{10,... | collective-permute-start | bytes 1990664 | tf_op jit(solution)/shard_map/ppermute | solution.py:327
  1020.1 23.9 %collective-permute-start.25 = (bf16[1,1152,144]{1,2,0:T(8,128)(2,1)S(1)}, bf16[1,1152,144]{1,2,0:T(8,128)(2,1)S(1)}, u32[]{:S(2)}, u32[]{:S(2)}) collective-permute-start(bf16[1,1152,144]{1,2,0:T(8,128)(2,1)S(1)} %dynamic-slice_convert_fusion.8), channel_id=1, source_target_pairs={{0,4},{1,5},{2,6},{3,7},{4,0},{5,1},{6,2},{7,3},{8,12},{9,13},{10,... | collective-permute-start | bytes 995336 | tf_op jit(solution)/shard_map/ppermute | solution.py:327
  1043.4 17.9 %collective-permute-start.20 = (bf16[1,288,576]{2,1,0:T(8,128)(2,1)S(1)}, bf16[1,288,576]{2,1,0:T(8,128)(2,1)S(1)}, u32[]{:S(2)}, u32[]{:S(2)}) collective-permute-start(bf16[1,288,576]{2,1,0:T(8,128)(2,1)S(1)} %dynamic-slice_convert_fusion.7), channel_id=1, source_target_pairs={{0,4},{1,5},{2,6},{3,7},{4,0},{5,1},{6,2},{7,3},{8,12},{9,13},{10,... | collective-permute-start | bytes 995336 | tf_op jit(solution)/shard_map/ppermute | solution.py:327
  (29 other events, 168.8 us)
Sparse Core Ops, SparseCore 0:
  9.6 105.4 all-gather.5
  116.7 56.0 all-gather.7
  174.3 25.7 all-gather.9
  201.5 70.9 all-gather.11
  273.9 70.8 all-gather.13
  671.7 80.6 reduce-scatter.3
  768.6 71.6 all-reduce.3

commit v2 on v1

v2 whole, which is shorter than its diff:
```python
import functools
import math

import jax
import jax.numpy as jnp
from jax import lax
from jax.experimental import pallas as pl
from jax.experimental.pallas import tpu as pltpu
from jax.sharding import PartitionSpec as P

WIN = 24
WIN_PAD = 32
BEFORE = 3
TERMS = 128
HEADS = 16
MAXLEN = 192
HEAD = 72
BLOCK = 256
SPAN = BLOCK + 2 * MAXLEN
CHUNK = 128
BF, F32 = jnp.bfloat16, jnp.float32
SCORE_SCALE = 1.0 / math.sqrt(HEAD)
LOG2E = 1.4426950408889634
VMEM = 60 * 1024 * 1024


def dot_rows(left, right):
    return lax.dot_general(left, right, (((1,), (1,)), ((), ())), preferred_element_type=F32)


def dot_plain(left, right):
    return jnp.dot(left, right, preferred_element_type=F32)


def fill_mask(key_mark_ref, query_mark_ref, bias):
    marks = jnp.broadcast_to(key_mark_ref[0].astype(F32), (CHUNK, SPAN))
    columns = marks.T
    query = query_mark_ref[0].astype(F32)
    for lane in range(0, BLOCK, CHUNK):
        bias[:, lane : lane + CHUNK] = jnp.where(
            columns == query[:, lane : lane + CHUNK], 0.0, -1e30
        )


def head_lanes(head, width):
    first = jnp.minimum((head * HEAD) // 128 * 128, width - 256)
    lanes = lax.broadcasted_iota(jnp.int32, (1, 256), 1) + first
    inside = (lanes >= head * HEAD) & (lanes < (head + 1) * HEAD)
    return pl.multiple_of(first, 128), inside


def masked(ref, first, inside):
    block = ref[:, pl.ds(first, 256)]
    return jnp.where(inside, block, jnp.zeros_like(block))


def fill_window(block, last, pair_ref, window):
    rows = pair_ref.shape[0] - 2 * MAXLEN
    inner = SPAN - MAXLEN

    @pl.when(block == 0)
    def _():
        window[0:MAXLEN, :] = pair_ref[rows : rows + MAXLEN, :]
        window[MAXLEN:SPAN, :] = pair_ref[0:inner, :]

    @pl.when((block > 0) & (block < last))
    def _():
        window[...] = pair_ref[pl.ds(pl.multiple_of(block * BLOCK - MAXLEN, 64), SPAN), :]

    @pl.when(block == last)
    def _():
        window[0:inner, :] = pair_ref[rows - inner : rows, :]
        window[inner:SPAN, :] = pair_ref[rows + MAXLEN : rows + 2 * MAXLEN, :]


def forward_kernel(query_ref, pair_ref, key_mark_ref, query_mark_ref,
                   out_ref, peak_ref, bias, turned, scores, weights, mixed, view):
    width = query_ref.shape[1]
    fill_window(pl.program_id(0), pl.num_programs(0) - 1, pair_ref, view)
    fill_mask(key_mark_ref, query_mark_ref, bias)
    turned[...] = view[:, width : 2 * width].T
    factor = SCORE_SCALE * LOG2E

    def pair(index, carry):
        for odd in range(2):
            head = 2 * index + odd
            first, inside = head_lanes(head, width)
            query = masked(query_ref, first, inside)
            peak = jnp.full((8, BLOCK), -3e38, F32)
            for start in range(0, SPAN, CHUNK):
                rows = slice(start, start + CHUNK)
                score = dot_rows(view[rows, pl.ds(first, 256)], query) * factor + bias[rows, :]
                scores[odd, rows, :] = score
                peak = jnp.maximum(peak, jnp.max(score.reshape(CHUNK // 8, 8, BLOCK), axis=0))
            peak = jnp.max(peak, axis=0, keepdims=True)
            total = jnp.zeros((8, BLOCK), F32)
            for start in range(0, SPAN, CHUNK):
                rows = slice(start, start + CHUNK)
                power = jnp.exp2(scores[odd, rows, :] - peak)
                total = total + jnp.sum(power.reshape(CHUNK // 8, 8, BLOCK), axis=0)
                weights[odd, rows, :] = power.astype(BF)
            total = jnp.sum(total, axis=0, keepdims=True)
            base = pl.multiple_of(index * 2 * HEAD, 16)
            value = turned[pl.ds(pl.multiple_of(base + 64 * odd, 16), 80), :]
            part = dot_plain(value, weights[odd]) * (1.0 / total)
            mixed[pl.ds(pl.multiple_of(base + HEAD * odd, 8), HEAD), :] = part[8 * odd : 8 * odd + HEAD]
            peak_ref[pl.ds(head, 1), :] = peak + jnp.log2(total)
        return carry

    lax.fori_loop(0, HEADS // 2, pair, 0)
    out_ref[...] = mixed[...].T.astype(BF)


def backward_kernel(edge, *refs):
    if edge:
        (query_ref, out_ref, grad_ref, peak_ref, pair_ref, key_mark_ref, query_mark_ref,
         grad_query_ref, rim_low_ref, rim_high_ref, grad_own_ref,
         bias, turned, weights, signals, mixed, delta, view, total) = refs
    else:
        (query_ref, out_ref, grad_ref, peak_ref, pair_ref, key_mark_ref, query_mark_ref, edge_ref, _,
         grad_query_ref, grad_own_ref,
         bias, turned, weights, signals, mixed, delta, view, sem) = refs
    width = query_ref.shape[1]
    step = pl.program_id(0)
    last = (pair_ref.shape[0] - 2 * MAXLEN) // BLOCK - 1
    fill_window(step * last if edge else step + 1, last, pair_ref, view)
    inner = SPAN - MAXLEN
    if edge:
        total[...] = jnp.zeros_like(total)
        sums = total
    else:
        rows = grad_own_ref.shape[0]

        @pl.when(step == 0)
        def _():
            low = pltpu.make_async_copy(edge_ref.at[0], grad_own_ref.at[pl.ds(0, inner)], sem.at[0])
            high = pltpu.make_async_copy(
                edge_ref.at[1], grad_own_ref.at[pl.ds(rows - inner, inner)], sem.at[1]
            )
            low.start()
            high.start()
            grad_own_ref[inner : rows - inner, :] = jnp.zeros((rows - 2 * inner, 2 * width), F32)
            low.wait()
            high.wait()

        sums = grad_own_ref.at[pl.ds(pl.multiple_of(step * BLOCK + BLOCK - MAXLEN, 64), SPAN)]
    fill_mask(key_mark_ref, query_mark_ref, bias)
    turned[...] = view[:, 0:width].T
    product = out_ref[...].astype(F32) * grad_ref[...].astype(F32)
    high = product.astype(BF)
    low = (product - high.astype(F32)).astype(BF)
    of_head = (
        lax.broadcasted_iota(jnp.int32, (HEADS, width), 1) // HEAD
        == lax.broadcasted_iota(jnp.int32, (HEADS, width), 0)
    ).astype(BF)
    delta[...] = dot_rows(of_head, high) + dot_rows(of_head, low)
    factor = SCORE_SCALE * LOG2E

    def pair(index, carry):
        for odd in range(2):
            head = 2 * index + odd
            first, inside = head_lanes(head, width)
            query = masked(query_ref, first, inside)
            grad = masked(grad_ref, first, inside)
            peak = peak_ref[pl.ds(head, 1), :]
            mean = delta[pl.ds(head, 1), :]
            for start in range(0, SPAN, CHUNK):
                rows = slice(start, start + CHUNK)
                score = dot_rows(view[rows, pl.ds(first, 256)], query) * factor
                power = jnp.exp2(score + (bias[rows, :] - peak))
                slope = dot_rows(view[rows, pl.ds(first + width, 256)], grad)
                low = power.astype(BF)
                signal = (power * (slope - mean)).astype(BF)
                signals[odd, rows, :] = signal
                sums[rows, pl.ds(first, 256)] += dot_plain(signal, query)
                sums[rows, pl.ds(first + width, 256)] += dot_plain(low, grad)
            base = pl.multiple_of(index * 2 * HEAD, 16)
            key = turned[pl.ds(pl.multiple_of(base + 64 * odd, 16), 80), :]
            part = dot_plain(key, signals[odd]) * SCORE_SCALE
            mixed[pl.ds(pl.multiple_of(base + HEAD * odd, 8), HEAD), :] = part[8 * odd : 8 * odd + HEAD]
        return carry

    lax.fori_loop(0, HEADS // 2, pair, 0)
    grad_query_ref[...] = mixed[...].T.astype(BF)
    if edge:

        @pl.when(step == 0)
        def _():
            rim_low_ref[:, :width] = (total[0:MAXLEN, :width] * SCORE_SCALE).astype(BF)
            rim_low_ref[:, width:] = total[0:MAXLEN, width:].astype(BF)
            grad_own_ref[0] = total[MAXLEN:SPAN, :]

        @pl.when(step == 1)
        def _():
            rim_high_ref[:, :width] = (total[inner:SPAN, :width] * SCORE_SCALE).astype(BF)
            rim_high_ref[:, width:] = total[inner:SPAN, width:].astype(BF)
            grad_own_ref[0] = total[0:inner, :]
    else:

        @pl.when(step == pl.num_programs(0) - 1)
        def _():
            grad_own_ref[:, :width] = grad_own_ref[:, :width] * SCORE_SCALE


def mark_windows(marker, marker_prev, marker_next):
    wide = jnp.concatenate([marker_prev, marker, marker_next])
    count = marker.shape[0] // BLOCK
    keys = jnp.stack([wide[i * BLOCK : i * BLOCK + SPAN] for i in range(count)])[:, None, :]
    return keys, marker.reshape(count, 1, BLOCK)


def whole(shape):
    return pl.BlockSpec(shape, lambda i: (0,) * len(shape))


def attention_calls(rows, width):
    count = rows // BLOCK
    last = count - 1
    inner = SPAN - MAXLEN
    scratch = [
        pltpu.VMEM((SPAN, BLOCK), F32),
        pltpu.VMEM((width, SPAN), BF),
    ]
    elements = SPAN * BLOCK * HEADS

    def block_specs(at):
        row_block = pl.BlockSpec((BLOCK, width), lambda i: (at(i), 0))
        lane_block = pl.BlockSpec((HEADS, BLOCK), lambda i: (0, at(i)))
        key_mark = pl.BlockSpec((1, 1, SPAN), lambda i: (at(i), 0, 0))
        query_mark = pl.BlockSpec((1, 1, BLOCK), lambda i: (at(i), 0, 0))
        return row_block, lane_block, key_mark, query_mark

    any_spec = pl.BlockSpec(memory_space=pl.ANY)
    params = pltpu.CompilerParams(vmem_limit_bytes=VMEM, dimension_semantics=("arbitrary",))
    pairs = once((rows + 2 * MAXLEN, 2 * width))
    view = pltpu.VMEM((SPAN, 2 * width), BF)

    def forward(queries, key_value, marks, after):
        row_block, lane_block, key_mark, query_mark = block_specs(lambda i: i)
        return pl.pallas_call(
            skipping(forward_kernel, 4, len(after)),
            grid=(count,),
            in_specs=[row_block, pairs, key_mark, query_mark] + [any_spec] * len(after),
            out_specs=[row_block, lane_block],
            out_shape=[
                jax.ShapeDtypeStruct((rows, width), BF),
                jax.ShapeDtypeStruct((HEADS, rows), F32),
            ],
            scratch_shapes=scratch
            + [
                pltpu.VMEM((2, SPAN, BLOCK), F32),
                pltpu.VMEM((2, SPAN, BLOCK), BF),
                pltpu.VMEM((width, BLOCK), F32),
                view,
            ],
            compiler_params=params,
            cost_estimate=cost(11.5 * count),
            name="attend",
        )(queries, key_value, *marks, *after)

    def backward(edge, queries, mixed, grad, peaks, key_value, marks, before=(), after=()):
        row_block, lane_block, key_mark, query_mark = block_specs(
            (lambda i: i * last) if edge else (lambda i: i + 1)
        )
        steps = 2 if edge else count - 2
        in_specs = [row_block, row_block, row_block, lane_block, pairs]
        in_specs += [key_mark, query_mark] + [any_spec] * (len(before) + len(after))
        rim = jax.ShapeDtypeStruct((MAXLEN, 2 * width), BF)
        if edge:
            out_specs = [row_block, whole(rim.shape), whole(rim.shape),
                         pl.BlockSpec((1, inner, 2 * width), lambda i: (i, 0, 0))]
            out_shape = [jax.ShapeDtypeStruct((rows, width), BF), rim, rim,
                         jax.ShapeDtypeStruct((2, inner, 2 * width), F32)]
            extra = [view, pltpu.VMEM((SPAN, 2 * width), F32)]
        else:
            out_specs = [row_block, whole((rows, 2 * width))]
            out_shape = [jax.ShapeDtypeStruct((rows, width), BF),
                         jax.ShapeDtypeStruct((rows, 2 * width), F32)]
            extra = [view, pltpu.SemaphoreType.DMA((2,))]
        return pl.pallas_call(
            skipping(functools.partial(backward_kernel, edge), 7 + len(before), len(after)),
            grid=(steps,),
            in_specs=in_specs,
            out_specs=out_specs,
            out_shape=out_shape,
            scratch_shapes=scratch
            + [
                pltpu.VMEM((2, SPAN, BLOCK), BF),
                pltpu.VMEM((2, SPAN, BLOCK), BF),
                pltpu.VMEM((width, BLOCK), F32),
                pltpu.VMEM((HEADS, BLOCK), F32),
            ]
            + extra,
            input_output_aliases={} if edge else {8: 0},
            compiler_params=params,
            cost_estimate=cost(2.2 * steps),
            name="attend_back_edge" if edge else "attend_back_inner",
        )(queries, mixed, grad, peaks, key_value, *marks, *before, *after)

    return forward, backward


BANDS = 4
EPSILON = 1e-06
ROOT = math.sqrt(2.0 / math.pi)
CUBE = 0.044715


def skipping(kernel, first, count):
    return lambda *refs: kernel(*refs[:first], *refs[first + count :])


def once(shape):
    return pl.BlockSpec(shape, lambda i, *_: (0,) * len(shape), pipeline_mode=pl.Buffered(buffer_count=1))


def rows_of(rows, width):
    return pl.BlockSpec((rows, width), lambda i, *_: (i, 0))


def kernel_params():
    return pltpu.CompilerParams(vmem_limit_bytes=VMEM, dimension_semantics=("arbitrary",))


def cost(microseconds):
    return pl.CostEstimate(flops=int(microseconds * 1.1e9), bytes_accessed=int(microseconds * 3e6), transcendentals=0)


def dot_turned(left, right):
    return lax.dot_general(left, right, (((0,), (0,)), ((), ())), preferred_element_type=F32)


def spread(select, parts_ref, part, width):
    return dot_plain(select, parts_ref[:, part * width : (part + 1) * width])


def normalise(block):
    centred = block - jnp.mean(block, axis=-1, keepdims=True)
    inverse = lax.rsqrt(jnp.mean(centred * centred, axis=-1, keepdims=True) + EPSILON)
    return centred * inverse, inverse


def norm_back(upstream, normed, inverse):
    return inverse * (
        upstream
        - jnp.mean(upstream, axis=-1, keepdims=True)
        - normed * jnp.mean(upstream * normed, axis=-1, keepdims=True)
    )


def image_sum(gather, block):
    high = block.astype(BF)
    low = (block - high.astype(F32)).astype(BF)
    return dot_plain(gather, high) + dot_plain(gather, low)


def column_sum(block):
    rows, width = block.shape
    return jnp.sum(block.reshape(rows // 8, 8, width), axis=0)


def piece_copies(place_ref, piece_refs, full, sems):
    copies = []
    for index, piece in enumerate(piece_refs):
        rows = piece.shape[0]
        start = pl.multiple_of(place_ref[index] * 16, 16)
        copies.append(pltpu.make_async_copy(piece, full.at[pl.ds(start, rows)], sems.at[index]))
    return copies


def begin_pieces(place_ref, piece_refs, full, sems):
    @pl.when(pl.program_id(0) == 0)
    def _():
        for copy in piece_copies(place_ref, piece_refs, full, sems):
            copy.start()


def end_pieces(place_ref, piece_refs, full, sems):
    @pl.when(pl.program_id(0) == 0)
    def _():
        for copy in piece_copies(place_ref, piece_refs, full, sems):
            copy.wait()


def project_kernel(own_rows, tokens_ref, select_ref, parts_ref, bias_ref, weight_ref, input_ref, query_ref, pair_ref):
    width = tokens_ref.shape[1]
    select = select_ref[...]
    normed, _ = normalise(tokens_ref[...].astype(F32))
    shift = spread(select, parts_ref, 0, width)
    scale = spread(select, parts_ref, 1, width)
    rows = (normed * (1.0 + scale) + shift).astype(BF)
    input_ref[...] = rows

    @pl.when(pl.program_id(0) * tokens_ref.shape[0] < own_rows)
    def _():
        query_ref[...] = (dot_plain(rows, weight_ref[:, :width]) + bias_ref[:, :width]).astype(BF)

    pair_ref[:, :width] = dot_plain(rows, weight_ref[:, width : 2 * width]).astype(BF)
    pair_ref[:, width:] = (dot_plain(rows, weight_ref[:, 2 * width :]) + bias_ref[:, width:]).astype(BF)


def project(weight, own_rows, tokens, select, parts, bias):
    rows, width = tokens.shape
    band = rows // BANDS
    return pl.pallas_call(
        functools.partial(project_kernel, own_rows),
        grid=(BANDS,),
        in_specs=[
            rows_of(band, width),
            rows_of(band, select.shape[1]),
            once(parts.shape),
            once(bias.shape),
            once(weight.shape),
        ],
        out_specs=[rows_of(band, width), rows_of(band, width), rows_of(band, 2 * width)],
        out_shape=[
            jax.ShapeDtypeStruct((rows, width), BF),
            jax.ShapeDtypeStruct((rows, width), BF),
            jax.ShapeDtypeStruct((rows, 2 * width), BF),
        ],
        compiler_params=kernel_params(),
        cost_estimate=cost(25),
        name="project",
    )(tokens, select, parts, bias, weight)


def enter_feed_kernel(count, place_ref, mixed_ref, tokens_ref, cotangent_ref, select_ref, parts_ref, bias_ref, *refs):
    pieces = refs[:count]
    attn_ref, middle_ref, input_ref, grad_feed_ref, full, sems = refs[count:]
    width = tokens_ref.shape[1]
    begin_pieces(place_ref, pieces, full, sems)
    select = select_ref[...]
    gate_mixer = spread(select, parts_ref, 0, width)
    shift = spread(select, parts_ref, 1, width)
    scale = spread(select, parts_ref, 2, width)
    gate_feed = spread(select, parts_ref, 3, width)
    grad_feed_ref[...] = (cotangent_ref[...].astype(F32) * gate_feed).astype(BF)
    end_pieces(place_ref, pieces, full, sems)
    attn = dot_plain(mixed_ref[...], full[...]) + bias_ref[...]
    attn_ref[...] = attn
    middle = tokens_ref[...].astype(F32) + gate_mixer * attn
    middle_ref[...] = middle
    normed, _ = normalise(middle)
    input_ref[...] = (normed * (1.0 + scale) + shift).astype(BF)


def enter_feed(place, pieces, mixed, tokens, cotangent, select, parts, bias, after):
    rows, width = tokens.shape
    band = rows // BANDS
    any_spec = pl.BlockSpec(memory_space=pl.ANY)
    block = rows_of(band, width)
    return pl.pallas_call(
        skipping(functools.partial(enter_feed_kernel, len(pieces)), 7 + len(pieces), len(after)),
        grid_spec=pltpu.PrefetchScalarGridSpec(
            num_scalar_prefetch=1,
            grid=(BANDS,),
            in_specs=[block, block, block, rows_of(band, select.shape[1]), once(parts.shape), once(bias.shape)]
            + [any_spec] * (len(pieces) + len(after)),
            out_specs=[block] * 4,
            scratch_shapes=[pltpu.VMEM((width, width), BF), pltpu.SemaphoreType.DMA((len(pieces),))],
        ),
        out_shape=[jax.ShapeDtypeStruct((rows, width), kind) for kind in (F32, F32, BF, BF)],
        compiler_params=kernel_params(),
        cost_estimate=cost(14),
        name="enter_feed",
    )(place, mixed, tokens, cotangent, select, parts, bias, *pieces, *after)


def feed_kernel(input_ref, grad_ref, expand_ref, contract_ref, bias_ref,
                out_ref, grad_input_ref, expand_grad_ref, contract_grad_ref, bias_grad_ref, grad_sum_ref,
                input_turned, grad_turned, active, hidden_grad):
    step = pl.program_id(0)
    rows, width = input_ref.shape

    @pl.when(step == 0)
    def _():
        input_turned[...] = input_ref[...].T
        grad_turned[...] = grad_ref[...].T
        grad_sum_ref[...] = column_sum(grad_ref[...].astype(F32))
        out_ref[...] = jnp.zeros_like(out_ref)
        grad_input_ref[...] = jnp.zeros_like(grad_input_ref)

    bias_grad_ref[...] = jnp.zeros_like(bias_grad_ref)

    def band(index, carry):
        here = pl.ds(pl.multiple_of(index * BLOCK, BLOCK), BLOCK)
        hidden = dot_plain(input_ref[here, :], expand_ref[...]) + bias_ref[...]
        square = hidden * hidden
        bent = jnp.tanh(ROOT * hidden * (1.0 + CUBE * square))
        half = 0.5 + 0.5 * bent
        active[here, :] = (hidden * half).astype(BF)
        slope = half + (0.5 * ROOT) * hidden * (1.0 - bent * bent) * (1.0 + (3.0 * CUBE) * square)
        pulled = dot_rows(grad_ref[here, :], contract_ref[...])
        low = (pulled * slope).astype(BF)
        hidden_grad[here, :] = low
        bias_grad_ref[...] += column_sum(low.astype(F32))
        out_ref[here, :] += dot_plain(active[here, :], contract_ref[...])
        grad_input_ref[here, :] += dot_rows(low, expand_ref[...])
        return carry

    lax.fori_loop(0, rows // BLOCK, band, 0)
    share = width // 4
    block = expand_grad_ref.shape[4]
    for index in range(4):
        part = dot_plain(input_turned[index * share : (index + 1) * share, :], hidden_grad[...]).astype(BF)
        for owner in range(width // block):
            expand_grad_ref[index, owner % 2, owner // 2] = part[:, owner * block : (owner + 1) * block]
    for index in range(4):
        here = slice(index * share, (index + 1) * share)
        part = dot_plain(grad_turned[here, :], active[...]).astype(BF)
        if len(contract_grad_ref.shape) == 3:
            contract_grad_ref[0, here, :] = part
        else:
            rows = contract_grad_ref.shape[3]
            for start in range(0, share, rows):
                rest, side = divmod((index * share + start) // rows, 2)
                contract_grad_ref[0, side, rest] = part[start : start + rows]


def feed(seq_count, inputs, grad_feed, expand, contract, bias):
    rows, width = inputs.shape
    hidden = expand.shape[1]
    steps = hidden // width
    whole_rows = once((rows, width))
    rest = seq_count // 2
    expand_shape = (4, 2, rest, width // 4, hidden // seq_count)
    if width // seq_count % 16 == 0:
        contract_shape = (steps, 2, rest, width // seq_count, width)
    else:
        contract_shape = (steps, width, width)
    result = pl.pallas_call(
        feed_kernel,
        grid=(steps,),
        in_specs=[
            whole_rows,
            whole_rows,
            pl.BlockSpec((width, width), lambda i: (0, i)),
            pl.BlockSpec((width, width), lambda i: (i, 0)),
            pl.BlockSpec((1, width), lambda i: (0, i)),
        ],
        out_specs=[
            whole_rows,
            whole_rows,
            pl.BlockSpec((4, 2, rest // steps) + expand_shape[3:], lambda i: (0, 0, i, 0, 0)),
            pl.BlockSpec((1,) + contract_shape[1:], lambda i: (i,) + (0,) * (len(contract_shape) - 1)),
            pl.BlockSpec((8, width), lambda i: (0, i)),
            once((8, width)),
        ],
        scratch_shapes=[
            pltpu.VMEM((width, rows), BF),
            pltpu.VMEM((width, rows), BF),
            pltpu.VMEM((rows, width), BF),
            pltpu.VMEM((rows, width), BF),
        ],
        out_shape=[
            jax.ShapeDtypeStruct((rows, width), F32),
            jax.ShapeDtypeStruct((rows, width), F32),
            jax.ShapeDtypeStruct(expand_shape, BF),
            jax.ShapeDtypeStruct(contract_shape, BF),
            jax.ShapeDtypeStruct((8, hidden), F32),
            jax.ShapeDtypeStruct((8, width), F32),
        ],
        compiler_params=kernel_params(),
        cost_estimate=cost(94),
        name="feed",
    )(inputs, grad_feed, expand, contract, bias)
    feed_out, grad_input, expand_grad, contract_grad, expand_sums, feed_sums = result
    if len(contract_shape) == 3:
        contract_grad = contract_grad.reshape(steps, rest, 2, width // seq_count, width).swapaxes(1, 2)
    return feed_out, grad_input, expand_grad, contract_grad, expand_sums, feed_sums


def leave_feed_kernel(count, place_ref, feed_ref, grad_input_ref, middle_ref, attn_ref, cotangent_ref, select_ref,
                      gather_ref, parts_ref, bias_ref, *refs):
    pieces = refs[:count]
    out_ref, grad_middle_ref, grad_attn_ref, grad_mixed_ref, image_ref, sum_ref, full, sems = refs[count:]
    width = middle_ref.shape[1]
    step = pl.program_id(0)
    begin_pieces(place_ref, pieces, full, sems)
    select = select_ref[...]
    gather = gather_ref[...]

    @pl.when(step == 0)
    def _():
        image_ref[...] = jnp.zeros_like(image_ref)
        sum_ref[...] = jnp.zeros_like(sum_ref)

    middle = middle_ref[...]
    grad_out = cotangent_ref[...].astype(F32)
    feed_out = feed_ref[...] + bias_ref[...]
    out_ref[...] = (middle + spread(select, parts_ref, 3, width) * feed_out).astype(BF)
    image_ref[:, 3 * width :] += image_sum(gather, grad_out * feed_out)
    grad_input = grad_input_ref[...]
    image_ref[:, width : 2 * width] += image_sum(gather, grad_input)
    normed, inverse = normalise(middle)
    image_ref[:, 2 * width : 3 * width] += image_sum(gather, grad_input * normed)
    scale = spread(select, parts_ref, 2, width)
    grad_middle = grad_out + norm_back(grad_input * (1.0 + scale), normed, inverse)
    grad_middle_ref[...] = grad_middle
    image_ref[:, :width] += image_sum(gather, grad_middle * attn_ref[...])
    grad_attn = (grad_middle * spread(select, parts_ref, 0, width)).astype(BF)
    grad_attn_ref[...] = grad_attn
    sum_ref[...] += column_sum(grad_attn.astype(F32))
    end_pieces(place_ref, pieces, full, sems)
    grad_mixed_ref[...] = dot_rows(grad_attn, full[...]).astype(BF)


def leave_feed(place, pieces, feed_out, grad_input, middle, attn, cotangent, select, gather, parts, bias, after):
    rows, width = middle.shape
    band = rows // BANDS
    any_spec = pl.BlockSpec(memory_space=pl.ANY)
    block = rows_of(band, width)
    images = gather.shape[0]
    return pl.pallas_call(
        skipping(functools.partial(leave_feed_kernel, len(pieces)), 10 + len(pieces), len(after)),
        grid_spec=pltpu.PrefetchScalarGridSpec(
            num_scalar_prefetch=1,
            grid=(BANDS,),
            in_specs=[block] * 5
            + [rows_of(band, select.shape[1]), pl.BlockSpec((images, band), lambda i, *_: (0, i)),
               once(parts.shape), once(bias.shape)]
            + [any_spec] * (len(pieces) + len(after)),
            out_specs=[block] * 4 + [once((images, 4 * width)), once((8, width))],
            scratch_shapes=[pltpu.VMEM((width, width), BF), pltpu.SemaphoreType.DMA((len(pieces),))],
        ),
        out_shape=[jax.ShapeDtypeStruct((rows, width), kind) for kind in (BF, F32, BF, BF)]
        + [jax.ShapeDtypeStruct((images, 4 * width), F32), jax.ShapeDtypeStruct((8, width), F32)],
        compiler_params=kernel_params(),
        cost_estimate=cost(2.2),
        name="leave_feed",
    )(place, feed_out, grad_input, middle, attn, cotangent, select, gather, parts, bias, *pieces, *after)


def store_owners(out_ref, lead, part, first, block, base):
    columns = part.shape[1]
    at = 0
    while at < columns:
        owner, offset = divmod(first + at, block)
        count = min(block - offset, columns - at)
        rest, side = divmod(owner, 2)
        out_ref[lead, side, rest, :, base + offset : base + offset + count] = part[:, at : at + count]
        at += count


def weight_grad_kernel(input_ref, query_ref, pair_ref, mixed_ref, attn_ref, out_ref, turned):
    step = pl.program_id(0)
    width = query_ref.shape[1]
    share = width // 4
    block = out_ref.shape[4] // 4

    def store(grad_ref, first, block, base):
        for index in range(4):
            part = dot_plain(turned[index * share : (index + 1) * share, :], grad_ref[...]).astype(BF)
            store_owners(out_ref, index, part, first, block, base)

    @pl.when(step == 0)
    def _():
        turned[...] = input_ref[...].T
        store(query_ref, 0, 3 * block, 0)

    for number in (1, 2):

        @pl.when(step == number)
        def _(number=number):
            store(pair_ref, number * width, 3 * block, 0)

    @pl.when(step == 3)
    def _():
        turned[...] = mixed_ref[...].T
        store(attn_ref, 0, block, 3 * block)


def weight_grad(seq_count, inputs, query, pair, mixed, attn, after):
    rows, width = query.shape
    shape = (4, 2, seq_count // 2, width // 4, 4 * width // seq_count)
    whole_rows = once((rows, width))
    return pl.pallas_call(
        skipping(weight_grad_kernel, 5, len(after)),
        grid=(4,),
        in_specs=[
            whole_rows,
            whole_rows,
            pl.BlockSpec((rows, width), lambda i: (0, jnp.clip(i - 1, 0, 1))),
            whole_rows,
            whole_rows,
        ]
        + [pl.BlockSpec(memory_space=pl.ANY)] * len(after),
        out_specs=once(shape),
        scratch_shapes=[pltpu.VMEM((width, rows), BF)],
        out_shape=jax.ShapeDtypeStruct(shape, BF),
        compiler_params=kernel_params(),
        cost_estimate=cost(2),
        name="weight_grad",
    )(inputs, query, pair, mixed, attn, *after)


def leave_kernel(query_ref, pair_ref, tokens_ref, grad_middle_ref, select_ref, gather_ref, parts_ref, weight_ref,
                 feed_images_ref, grad_ref, image_ref, sum_ref):
    width = tokens_ref.shape[1]
    select = select_ref[...]
    gather = gather_ref[...]

    @pl.when(pl.program_id(0) == 0)
    def _():
        image_ref[:, : 2 * width] = jnp.zeros_like(image_ref[:, : 2 * width])
        image_ref[:, 2 * width :] = feed_images_ref[...]
        sum_ref[...] = jnp.zeros_like(sum_ref)

    query = query_ref[...]
    pair = pair_ref[...]
    sum_ref[:, :width] += column_sum(query.astype(F32))
    sum_ref[:, width:] += column_sum(pair[:, width:].astype(F32))
    normed, inverse = normalise(tokens_ref[...].astype(F32))
    scale = spread(select, parts_ref, 1, width)
    grad_input = dot_rows(query, weight_ref[:, :width]) + dot_rows(pair, weight_ref[:, width:])
    image_ref[:, :width] += image_sum(gather, grad_input)
    image_ref[:, width : 2 * width] += image_sum(gather, grad_input * normed)
    grad_ref[...] = grad_middle_ref[...] + norm_back(grad_input * (1.0 + scale), normed, inverse)


def leave(weight, query, pair, tokens, grad_middle, select, gather, parts, feed_images, after):
    rows, width = tokens.shape
    band = rows // BANDS
    block = rows_of(band, width)
    images = gather.shape[0]
    return pl.pallas_call(
        skipping(leave_kernel, 9, len(after)),
        grid=(BANDS,),
        in_specs=[block, rows_of(band, 2 * width), block, block, rows_of(band, select.shape[1]),
                  pl.BlockSpec((images, band), lambda i: (0, i)), once(parts.shape), once(weight.shape),
                  once(feed_images.shape)]
        + [pl.BlockSpec(memory_space=pl.ANY)] * len(after),
        out_specs=[block, once((images, 6 * width)), once((8, 2 * width))],
        out_shape=[
            jax.ShapeDtypeStruct((rows, width), F32),
            jax.ShapeDtypeStruct((images, 6 * width), F32),
            jax.ShapeDtypeStruct((8, 2 * width), F32),
        ],
        compiler_params=kernel_params(),
        cost_estimate=cost(2.5),
        name="leave",
    )(query, pair, tokens, grad_middle, select, gather, parts, weight, feed_images, *after)


def partners(axis, bit):
    return [(i, i ^ bit) for i in range(lax.axis_size(axis))]


def bits_of(axis):
    bit = 1
    while bit < lax.axis_size(axis):
        yield bit
        bit *= 2


def doubled(value, axis, bits=None):
    place = lax.axis_index(axis)
    for bit in bits_of(axis) if bits is None else bits:
        other = lax.ppermute(value, axis, partners(axis, bit))
        mine = (place // bit) % 2
        value = jnp.concatenate([jnp.where(mine == 0, value, other), jnp.where(mine == 0, other, value)])
    return value


def neighbour_groups():
    dp_count, seq_count = lax.axis_size("dp"), lax.axis_size("seq")
    return [
        [d * seq_count + 2 * pair + side for d in range(dp_count) for side in range(2)]
        for pair in range(seq_count // 2)
    ]


def gathered(weight):
    rows = weight.shape[0] // 2
    half = lax.dynamic_slice_in_dim(weight, lax.axis_index("seq") % 2 * rows, rows, 0)
    return lax.all_gather(half, ("dp", "seq"), axis=0, tiled=True, axis_index_groups=neighbour_groups())


def scattered(grad):
    return lax.psum_scatter(
        grad.reshape(-1, *grad.shape[2:]), ("dp", "seq"), scatter_dimension=0, axis_index_groups=neighbour_groups()
    )


def along_rest(rest):
    stages = []
    for bit in list(bits_of("seq"))[1:]:
        pairs = rest.reshape(-1, 2, *rest.shape[1:])
        mine = (lax.axis_index("seq") // bit) % 2
        sent = lax.dynamic_index_in_dim(pairs, 1 - mine, 1, keepdims=False)
        rest = wide(lax.dynamic_index_in_dim(pairs, mine, 1, keepdims=False)) + wide(swapped(sent, "seq", bit))
        stages.append(rest)
    return stages


def gate(value, other):
    first = other[(0,) * other.ndim]
    return jnp.where(first == first, value, jnp.zeros_like(value))


def swapped(value, axis, bit, kind=BF):
    return lax.ppermute(value.astype(kind), axis, partners(axis, bit))


def wide(value):
    return value.astype(F32)


def split_owners(value):
    return value.reshape(2, -1, 2, *value.shape[2:])


def three_terms(value):
    high = lax.reduce_precision(value, 8, 7)
    middle = lax.reduce_precision(value - high, 8, 7)
    low = value - high - middle
    high, middle, low = high.astype(BF), middle.astype(BF), low.astype(BF)
    pad = jnp.zeros((TERMS - 3 * WIN, value.shape[1]), BF)
    return jnp.concatenate([high, middle, low, pad])


def shards(
    tokens,
    segments,
    condition,
    cotangent,
    modulation_weight,
    modulation_bias,
    input_weight,
    query_value_bias,
    output_weight,
    output_bias,
    expand_weight,
    expand_bias,
    contract_weight,
    contract_bias,
):
    token_rows = tokens[0]
    segment = segments[0]
    conditions = condition[0].astype(F32)
    grad_out = cotangent[0]
    row_count, width = token_rows.shape
    images = conditions.shape[0]
    own = lax.axis_index("dp")
    place_in_seq = lax.axis_index("seq")
    seq_count = lax.axis_size("seq")
    onward = [(i, i + 1) for i in range(seq_count - 1)]
    back = [(i + 1, i) for i in range(seq_count - 1)]
    columns = modulation_weight.shape[1] // seq_count
    row = lambda bias: bias.astype(F32)[None, :]

    input_full = gathered(input_weight)
    expand_full = gathered(expand_weight)
    contract_full = gathered(contract_weight)
    silu_all, silu_back = jax.vjp(jax.nn.silu, conditions)
    cond_act = silu_all.astype(BF)
    late = 2 * width
    mixer_columns = late // seq_count
    feed_columns = 4 * width // seq_count
    share_rows = width // 4
    seq_bits, dp_bits = list(bits_of("seq")), list(bits_of("dp"))

    def own_columns(array, axis):
        return jnp.concatenate(
            [
                lax.dynamic_slice_in_dim(array, place_in_seq * mixer_columns, mixer_columns, axis),
                lax.dynamic_slice_in_dim(array, late + place_in_seq * feed_columns, feed_columns, axis),
            ],
            axis=axis,
        )

    first_image = jnp.clip(segment[0] - BEFORE, 0, images - WIN)
    top = seq_bits[-1]
    first_of_top = lax.ppermute(first_image, "seq", partners("seq", top))
    marker = segment + 1
    low_marks = lax.ppermute(jnp.append(marker[row_count - MAXLEN :], first_image), "seq", onward)
    high_marks = lax.ppermute(jnp.append(marker[:MAXLEN], first_image), "seq", back)
    low_rows = lax.ppermute(token_rows[row_count - MAXLEN :], "seq", onward)
    high_rows = lax.ppermute(token_rows[:MAXLEN], "seq", back)
    first_of_next = jnp.where(place_in_seq % 2 == 0, high_marks[MAXLEN], low_marks[MAXLEN])
    piece = own_columns(modulation_weight, 1)
    piece_far = lax.ppermute(piece, "dp", partners("dp", 2))
    piece = jnp.concatenate([piece, piece_far])
    piece = jnp.concatenate([piece, lax.ppermute(piece, "dp", partners("dp", 1))])
    turned = [lax.dynamic_slice_in_dim(cond_act, (own ^ index) * share_rows, share_rows, 1) for index in (0, 2, 1, 3)]
    product = jnp.dot(jnp.concatenate(turned, axis=1), piece, preferred_element_type=F32)
    product += row(own_columns(modulation_bias, 0))
    product = doubled(product[None], "seq", seq_bits[:-1])
    for early in (low_rows, high_rows, first_of_next.astype(F32)[None], first_of_top.astype(F32)[None]):
        product = gate(product, early)
    mine = lax.dynamic_slice_in_dim(product, first_image, WIN, 1)
    other = lax.ppermute(lax.dynamic_slice_in_dim(product, first_of_top, WIN, 1), "seq", partners("seq", top))
    upper = place_in_seq // top
    windows = jnp.concatenate([jnp.where(upper == 0, mine, other), jnp.where(upper == 0, other, mine)])
    mixer_parts = three_terms(windows[:, :, :mixer_columns].swapaxes(0, 1).reshape(WIN, -1))
    feed_parts = three_terms(windows[:, :, mixer_columns:].swapaxes(0, 1).reshape(WIN, -1))
    marks = mark_windows(marker, low_marks[:MAXLEN], high_marks[:MAXLEN])
    wide_rows = jnp.concatenate([token_rows, low_rows, high_rows])
    wide_segment = jnp.concatenate([segment, low_marks[:MAXLEN] - 1, high_marks[:MAXLEN] - 1])
    image_select = (wide_segment - first_image)[:, None] == jnp.arange(WIN, dtype=jnp.int32)[None, :]
    select = jnp.concatenate(
        [image_select, image_select, image_select, jnp.zeros((wide_segment.shape[0], TERMS - 3 * WIN), bool)], axis=1
    ).astype(BF)
    gather = jnp.concatenate(
        [image_select[:row_count].T, jnp.zeros((WIN_PAD - WIN, row_count), bool)], axis=0
    ).astype(BF)

    input_attn, queries, key_value = project(
        input_full, row_count, wide_rows, select, mixer_parts, row(query_value_bias)
    )
    output_near = lax.ppermute(output_weight, "dp", partners("dp", 1))
    output_far = lax.ppermute(output_weight, "dp", partners("dp", 2))
    output_pieces = [output_weight, output_near, output_far, lax.ppermute(output_far, "dp", partners("dp", 1))]
    output_at = (jnp.stack([own ^ index for index in range(4)]) * (share_rows // 16)).astype(jnp.int32)
    acts = [cond_act] + [lax.ppermute(gate(cond_act, input_attn), "dp", partners("dp", mask)) for mask in (1, 2, 3)]
    own_slice = lax.dynamic_slice_in_dim(modulation_weight, place_in_seq * columns, columns, 1)
    slice_full = lax.all_gather(own_slice, "dp", axis=0, tiled=True)

    attend, attend_back = attention_calls(row_count, width)
    attn_mixed, row_peaks = attend(queries, key_value, marks, ())

    attn_out, middle, input_feed, grad_feed = enter_feed(
        output_at, output_pieces, attn_mixed, token_rows, grad_out, select, feed_parts, row(output_bias),
        (),
    )
    feed_out, grad_input_feed, expand_grad, contract_grad, expand_sums, feed_sums = feed(
        seq_count, input_feed, grad_feed, expand_full, contract_full, row(expand_bias)
    )
    contract_rest = scattered(contract_grad)
    expand_rest = scattered(expand_grad)
    layer_out, grad_middle, grad_attn, grad_mixed, feed_images, attn_sums = leave_feed(
        output_at, output_pieces, feed_out, grad_input_feed, middle, attn_out, grad_out, select, gather,
        feed_parts, row(contract_bias), (*acts[1:], slice_full),
    )
    grad_query_edge, rim_low, rim_high, grad_edge = attend_back(
        True, queries, attn_mixed, grad_mixed, row_peaks, key_value, marks
    )
    from_next = lax.ppermute(rim_low, "seq", back)
    from_prev = lax.ppermute(rim_high, "seq", onward)
    grad_query, own_grad = attend_back(
        False, queries, attn_mixed, grad_mixed, row_peaks, key_value,
        marks, (grad_edge, grad_query_edge), (contract_rest,),
    )
    rims = jnp.pad(from_prev.astype(F32), ((0, row_count - MAXLEN), (0, 0))) + jnp.pad(
        from_next.astype(F32), ((row_count - MAXLEN, 0), (0, 0))
    )
    grad_pair = (own_grad + rims).astype(BF)
    contract_stages = along_rest(contract_rest)
    total_contract = contract_stages[-1][0]
    total_expand = along_rest(expand_rest)[-1][0]
    input_grad = weight_grad(
        seq_count, input_attn, grad_query, grad_pair, attn_mixed, grad_attn, (contract_stages[0],)
    )
    input_rest = scattered(input_grad)
    grad_rows, all_images, packed_sums = leave(
        input_full, grad_query, grad_pair, token_rows, grad_middle, select, gather, mixer_parts, feed_images,
        (input_grad,),
    )
    input_total = along_rest(input_rest)[-1][0]
    input_width = 3 * width // seq_count
    total_input, total_output = input_total[:, :input_width], input_total[:, input_width:]

    window_grads = all_images[:WIN]
    sums = [
        jnp.sum(window_grads, axis=0),
        jnp.sum(packed_sums, axis=0),
        jnp.sum(attn_sums, axis=0),
        jnp.sum(expand_sums, axis=0),
        jnp.sum(feed_sums, axis=0),
    ]
    ends = [sum(part.shape[0] for part in sums[: index + 1]) for index in range(5)]
    biases = jnp.concatenate(sums + [jnp.zeros((-ends[-1] % columns,), F32)]).reshape(-1, columns)
    bias_rows = biases.shape[0]

    def joined(value, axis, bit):
        high = lax.reduce_precision(biases, 8, 7)
        low = lax.reduce_precision(biases - high, 8, 7)
        got = swapped(jnp.concatenate([value.reshape(-1, columns), high, low]), axis, bit)
        rest = high + low + (wide(got[-2 * bias_rows : -bias_rows]) + wide(got[-bias_rows:]))
        return wide(got[: -2 * bias_rows]).reshape(value.shape), rest

    window_blocks = window_grads.reshape(WIN, -1, 2, columns)
    mine = lax.dynamic_index_in_dim(window_blocks, place_in_seq % 2, 2, keepdims=False)
    sent = lax.dynamic_index_in_dim(window_blocks, 1 - place_in_seq % 2, 2, keepdims=False)
    got, biases = joined(sent.swapaxes(0, 1), "seq", 1)
    empty = jnp.zeros((seq_count // 2, images, columns), F32)
    column_grads = lax.dynamic_update_slice_in_dim(empty, mine.swapaxes(0, 1), first_image, 1)
    column_grads += lax.dynamic_update_slice_in_dim(empty, got, first_of_next, 1)
    for bit in seq_bits[1:]:
        pairs = column_grads.reshape(-1, 2, images, columns)
        mine = (place_in_seq // bit) % 2
        got, biases = joined(lax.dynamic_index_in_dim(pairs, 1 - mine, 1, keepdims=False), "seq", bit)
        column_grads = lax.dynamic_index_in_dim(pairs, mine, 1, keepdims=False) + got
    column_grads = column_grads[0]
    all_grads = column_grads[None].astype(BF)
    for bit in dp_bits:
        other, biases = joined(all_grads, "dp", bit)
        other = other.astype(BF)
        mine = (own // bit) % 2
        all_grads = jnp.concatenate([jnp.where(mine == 0, all_grads, other), jnp.where(mine == 0, other, all_grads)])
    all_grads = all_grads.reshape(-1, columns)
    acts = jnp.stack([lax.dynamic_slice_in_dim(act, own * share_rows, share_rows, 1) for act in acts])
    acts = [lax.dynamic_index_in_dim(acts, own ^ index, 0, keepdims=False) for index in range(4)]
    all_act = jnp.concatenate(acts)
    total_modulation = dot_turned(all_act, all_grads)
    grad_act = lax.dot_general(
        column_grads, slice_full.astype(F32), (((1,), (1,)), ((), ())), precision=lax.Precision.HIGHEST
    )
    grad_condition = silu_back(grad_act)[0].reshape(seq_count, -1, width)
    for bit in seq_bits:
        pairs = grad_condition.reshape(-1, 2, *grad_condition.shape[1:])
        mine = (place_in_seq // bit) % 2
        got = swapped(lax.dynamic_index_in_dim(pairs, 1 - mine, 1, keepdims=False), "seq", bit, F32)
        grad_condition = lax.dynamic_index_in_dim(pairs, mine, 1, keepdims=False) + got
    grad_condition = grad_condition[0]
    bias_modulation, bias_query_value, bias_output, bias_expand, bias_contract, _ = jnp.split(
        biases.reshape(-1), ends
    )
    return (
        layer_out[None],
        grad_rows[None],
        grad_condition[None],
        total_modulation,
        bias_modulation,
        total_input,
        bias_query_value,
        total_output,
        bias_output,
        total_expand,
        bias_expand,
        total_contract.T,
        bias_contract,
    )


def solution(mesh):
    in_specs = (
        P("dp", "seq", None),
        P("dp", "seq"),
        P("dp", None, None),
        P("dp", "seq", None),
        P("dp", None),
        P(),
        P("dp", None),
        P(),
        P("dp", None),
        P(),
        P("dp", None),
        P(),
        P("dp", None),
        P(),
    )
    out_specs = (
        P("dp", "seq", None),
        P("dp", "seq", None),
        P("dp", "seq", None),
        P("dp", "seq"),
        P(),
        P("dp", "seq"),
        P(),
        P("dp", "seq"),
        P(),
        P("dp", "seq"),
        P(),
        P("dp", "seq"),
        P(),
    )
    return jax.shard_map(shards, mesh=mesh, in_specs=in_specs, out_specs=out_specs, check_vma=False)
```

time: 1080 us -> 667 us (0.62)
  matrix products: 233 us -> 6 us
  Pallas kernels: 149 us -> 348 us
  blocking collectives: 149 us -> 0 us
  waiting for transfers between devices: 248 us -> 152 us
  other arithmetic: 116 us -> 34.8 us
  local copies, waits for them, and re-layouts: 112 us -> 46.3 us
    dot_general x17 -> x3, matrix products: 233 us -> 6 us  [the longest x1 2.68 us: shards(): jnp.dot(jnp.concatenate(turned, axis=1), piece, preferred_element_type=F32)]
    pallas_call x4 -> x9, Pallas kernels: 149 us -> 348 us  [the longest x2 106 us: backward(): pl.pallas_call(skipping(functools.partial(backward_kernel, edge), 7 + len...]
    all_gather x2 -> x0, blocking collectives: 106 us -> none  [the longest x1 96 us: shards(): all_grads = lax.all_gather(column_grads, 'dp', axis=0, tiled=True)]
    all_gather x5 -> x4, waiting for transfers between devices: 109 us -> 22.2 us  [the longest x3 22.2 us: gathered(): lax.all_gather(half, ('dp', 'seq'), axis=0, tiled=True, axis_index_groups...]
    psum x1 -> x0, blocking collectives: 42.2 us -> none  [shards(): lax.psum((grad_modulation_bias, grad_query_value_bias, grad_output_bias,...]
    unnamed x125 -> x73, local copies, waits for them, and re-layouts: 40.1 us -> 3.81 us
    convert_element_type x18 -> x3, local copies, waits for them, and re-layouts: 34.9 us -> 0.86 us  [swapped(): return lax.ppermute(value.astype(kind), axis, partners(axis, bit))]
    reduce_sum x7 -> x4, other arithmetic: 30 us -> 0.11 us  [the longest x1 0.04 us: shards(): jnp.sum(expand_sums, axis=0)]
  transfers between devices with their start and end apart: 33 -> 39, of which waited for: 11 -> 17; matrix products, arithmetic and copies ran while one was open for 41% -> 12% of each run, Pallas kernels for 14% -> 53%
where the time goes in v2:
time: 667 us; the launch traced here: 661 us
  Pallas kernels  348 us (52%)
  waiting for transfers between devices  152 us (23%)
  starting transfers between devices  50.3 us (8%)
  local copies, waits for them, and re-layouts  46.3 us (7%)
  other arithmetic  34.8 us (5%)
  between operations  24.2 us (4%)
    pallas_call x2, Pallas kernels, backward(): pl.pallas_call(skipping(functools.partial(backward_kernel, edge), 7 + len...  106 us
    pallas_call x1, Pallas kernels, feed(): pl.pallas_call(feed_kernel, grid=(steps,), in_specs=[whole_rows, whole_ro...  94.5 us
    ppermute x14, waiting for transfers between devices, swapped(): return lax.ppermute(value.astype(kind), axis, partners(axis, bit))  70.5 us
    pallas_call x1, Pallas kernels, forward(): pl.pallas_call(skipping(forward_kernel, 4, len(after)), grid=(count,), in...  43.4 us
    ppermute x2, waiting for transfers between devices, doubled(): other = lax.ppermute(value, axis, partners(axis, bit))  26.8 us
    pallas_call x1, Pallas kernels, leave(): pl.pallas_call(skipping(leave_kernel, 9, len(after)), grid=(BANDS,), in_s...  23.9 us
    pallas_call x1, Pallas kernels, weight_grad(): pl.pallas_call(skipping(weight_grad_kernel, 5, len(after)), grid=(4,), in...  22.7 us
    all_gather x3, waiting for transfers between devices, gathered(): lax.all_gather(half, ('dp', 'seq'), axis=0, tiled=True, axis_index_groups...  22.2 us
  transfers between devices with their start and end apart: 39, of which 17 were waited for; matrix products, arithmetic and copies ran while one was open for 12% of the time, Pallas kernels for 53%

profile of v2, /device:TPU:0, one launch (start us, length us, event | category | flops | bytes accessed | tf_op | source)
XLA Modules:
  0.0 661.3 jit_solution(4629653037826844018)
XLA Ops:
  7.3 2.4 constant_dynamic-slice_fusion.6
  9.7 1.2 constant_dynamic-slice_fusion.5
  11.0 2.5 constant_dynamic-slice_fusion.4
  13.6 3.0 collective-permute-start.11
  17.7 1.3 constant_dynamic-slice_fusion.8
  21.5 1.3 collective-permute-start.3
  22.8 6.3 collective-permute-start.4
  29.1 2.1 constant_dynamic-slice_fusion.3
  38.3 2.5 collective-permute-start.2
  43.4 12.1 %collective-permute-done.5 = bf16[288,864]{1,0:T(8,128)(2,1)} collective-permute-done((bf16[288,864]{1,0:T(8,128)(2,1)}, bf16[288,864]{1,0:T(8,128)(2,1)}, u32[]{:S(2)}, u32[]{:S(2)}) %collective-permute-start.5) | collective-permute-done | bytes 497696 | tf_op jit(solution)/shard_map/ppermute | solution.py:882
  55.5 1.3 collective-permute-start.1
  56.8 2.2 pad_maximum_fusion.1
  59.0 5.3 collective-permute-start
  64.5 2.7 fusion.11
  67.1 1.4 collective-permute-start.7
  72.1 23.7 %collective-permute-done.7 = f32[1,64,864]{2,1,0:T(8,128)} collective-permute-done((f32[1,64,864]{2,1,0:T(8,128)}, f32[1,64,864]{2,1,0:T(8,128)}, u32[]{:S(2)}, u32[]{:S(2)}) %collective-permute-start.7) | collective-permute-done | bytes 221216 | tf_op jit(solution)/shard_map/ppermute | solution.py:759
  96.9 4.0 collective-permute-start.8
  100.9 1.2 add_convert_fusion.1.select_ref.refs_4_.refs_6_
  103.9 1.2 slice.165
  106.4 3.1 collective-permute-done.8
  109.8 2.9 collective-permute-start.9
  112.7 5.4 pad_maximum_fusion.tokens_ref
  118.2 7.3 %collective-permute-done.9 = f32[4,24,864]{2,1,0:T(8,128)S(1)} collective-permute-done((f32[4,24,864]{2,1,0:T(8,128)S(1)}, f32[4,24,864]{2,1,0:T(8,128)S(1)}, u32[]{:S(2)}, u32[]{:S(2)}) %collective-permute-start.9) | collective-permute-done | bytes 331808 | tf_op jit(solution)/shard_map/ppermute | solution.py:892
  126.3 1.2 maximum_maximum_fusion.refs_5_.refs_8_
  128.5 22.0 %project.1 = (bf16[1408,1152]{1,0:T(8,128)(2,1)}, bf16[1408,1152]{1,0:T(8,128)(2,1)}, bf16[1408,2304]{1,0:T(8,128)(2,1)}) custom-call(bf16[1408,1152]{1,0:T(8,128)(2,1)} %pad_maximum_fusion.tokens_ref, bf16[1408,128]{1,0:T(8,128)(2,1)} %add_convert_fusion.1.select_ref.refs_4_.refs_6_, bf16[128,2304]{1,0:T(8,128)(2,1)} %maximum_maximum_fusion.1.parts_ref.refs_6_, ...), custom_call_target="tpu_custom_call" | custom-call | flops 27499999232 | bytes 75000000 | tf_op jit(solution)/shard_map/project/pallas_call | solution.py:405
  150.5 43.4 %attend.1 = (bf16[1024,1152]{1,0:T(8,128)(2,1)}, f32[16,1024]{1,0:T(8,128)}) custom-call(bf16[1408,1152]{1,0:T(8,128)(2,1)} %get-tuple-element.43.refs_0_, bf16[1408,2304]{1,0:T(8,128)(2,1)} %get-tuple-element.44.refs_1_.refs_4_, s32[4,1,640]{2,1,0:T(1,128)} %broadcast_in_dim.53.refs_2_.refs_5_, s32[4,1,256]{2,1,0:T(1,128)} %bitcast.161), custom_call_target="tpu_custom_call" | custom-call | flops 50600001536 | bytes 138000000 | tf_op jit(solution)/shard_map/attend/pallas_call | solution.py:240
  194.7 14.4 %enter_feed.1 = (f32[1024,1152]{1,0:T(8,128)}, f32[1024,1152]{1,0:T(8,128)}, bf16[1024,1152]{1,0:T(8,128)(2,1)}, bf16[1024,1152]{1,0:T(8,128)(2,1)}) custom-call(s32[4]{0:T(128)} %add_multiply_fusion.refs_0_, bf16[1024,1152]{1,0:T(8,128)(2,1)} %get-tuple-element.45.refs_1_.refs_3_, bf16[1024,1152]{1,0:T(8,128)(2,1)} %bitcast.130, ...), custom_call_target="tpu_custom_call" | custom-call | flops 15399999488 | bytes 42000000 | tf_op jit(solution)/shard_map/enter_feed/pallas_call | solution.py:452
  209.2 22.2 %all-gather.9.cloned.1.call-done.contract_ref = bf16[4608,1152]{1,0:T(8,128)(2,1)} async-done(((bf16[576,1152]{1,0:T(8,128)(2,1)}), bf16[4608,1152]{1,0:T(8,128)(2,1)}) %all-gather.9.cloned.1.call-update) | async-done | bytes 10616848 | tf_op jit(solution)/shard_map/all_gather | solution.py:776
  231.4 94.5 %feed.1 = (f32[1024,1152]{1,0:T(8,128)}, f32[1024,1152]{1,0:T(8,128)}, bf16[4,2,4,288,576]{4,3,2,1,0:T(8,128)(2,1)}, bf16[4,2,4,144,1152]{4,3,2,1,0:T(8,128)(2,1...) custom-call(bf16[1024,1152]{1,0:T(8,128)(2,1)} %get-tuple-element.46.input_ref, bf16[1024,1152]{1,0:T(8,128)(2,1)} %get-tuple-element.47.grad_ref, ...), custom_call_target="tpu_custom_call" | custom-call | flops 103399997440 | bytes 282000000 | tf_op jit(solution)/shard_map/feed/pallas_call | solution.py:531
  327.2 1.2 slice.145
  332.4 4.5 collective-permute-done.14.refs_15_
  336.8 1.8 collective-permute-done.15.refs_16_
  339.3 20.7 %leave_feed.1 = (bf16[1024,1152]{1,0:T(8,128)(2,1)}, f32[1024,1152]{1,0:T(8,128)}, bf16[1024,1152]{1,0:T(8,128)(2,1)}, bf16[1024,1152]{1,0:T(8,128)(2,1)}, f32[32,4608]{1,0:T(8,128)}, /*index=5*/f32[8,1152]{1,0:T(8,128)}) custom-call(s32[4]{0:T(128)} %add_multiply_fusion.refs_0_, f32[1024,1152]{1,0:T(8,128)} %get-tuple-element.48.refs_1_, ...), custom_call_target="tpu_custom_call" | custom-call | flops 2420000000 | bytes 6600000 | tf_op jit(solution)/shard_map/leave_feed/pallas_call | solution.py:614
  360.0 50.6 %attend_back_edge.1 = (bf16[1024,1152]{1,0:T(8,128)(2,1)}, bf16[192,2304]{1,0:T(8,128)(2,1)}, bf16[192,2304]{1,0:T(8,128)(2,1)}, f32[2,448,2304]{2,1,0:T(8,128)}) custom-call(bf16[1408,1152]{1,0:T(8,128)(2,1)} %get-tuple-element.43.refs_0_, bf16[1024,1152]{1,0:T(8,128)(2,1)} %get-tuple-element.45.refs_1_.refs_3_, ...), custom_call_target="tpu_custom_call" | custom-call | flops 4840000000 | bytes 13200000 | tf_op jit(solution)/shard_map/attend_back_edge/pallas_call | solution.py:280
  410.7 3.6 collective-permute-start.16
  414.2 1.3 collective-permute-start.17
  415.6 2.0 dynamic-slice_bitcast_fusion.2
  417.6 3.6 collective-permute-start.18
  421.1 55.8 %attend_back_inner.1 = (bf16[1024,1152]{1,0:T(8,128)(2,1)}, f32[1024,2304]{1,0:T(8,128)}) custom-call(bf16[1408,1152]{1,0:T(8,128)(2,1)} %get-tuple-element.43.refs_0_, bf16[1024,1152]{1,0:T(8,128)(2,1)} %get-tuple-element.45.refs_1_.refs_3_, bf16[1024,1152]{1,0:T(8,128)(2,1)} %get-tuple-element.54.refs_2_, ...), custom_call_target="tpu_custom_call", output_to_operand_aliasing={{0}: (8, {})} | custom-call | flops 4840000000 | bytes 13200000 | tf_op jit(solution)/shard_map/attend_back_inner/pallas_call | solution.py:280
  477.0 6.7 %add_convert_fusion.refs_2_.refs_1_ = bf16[1024,2304]{1,0:T(8,128)(2,1)} fusion(f32[1024,2304]{1,0:T(8,128)} %get-tuple-element.60, bf16[192,2304]{1,0:T(8,128)(2,1)S(1)} %collective-permute-done.17, bf16[192,2304]{1,0:T(8,128)(2,1)S(1)} %collective-permute-done.16), kind=kLoop, calls=%fused_computation | loop fusion | flops 11796480 | bytes 15925248 | tf_op jit(solution)/shard_map/convert_element_type | solution.py:947
  483.7 2.3 convert_add_fusion.2.refs_5_
  486.0 22.7 %weight_grad.1.refs_9_ = bf16[4,2,4,288,576]{4,3,2,1,0:T(8,128)(2,1)} custom-call(bf16[1408,1152]{1,0:T(8,128)(2,1)} %get-tuple-element.52.refs_0_, bf16[1024,1152]{1,0:T(8,128)(2,1)} %get-tuple-element.59.refs_1_.refs_0_, bf16[1024,2304]{1,0:T(8,128)(2,1)} %add_convert_fusion.refs_2_.refs_1_, bf16[1024,1152]{1,0:T(8,128)(2,1)} %get-tuple-element.45.refs_1_.refs_3_, ...), custom_call_target="tpu_custom_call" | custom-call | flops 2200000000 | bytes 6000000 | tf_op jit(solution)/shard_map/weight_grad/pallas_call | solution.py:677
  512.9 2.0 dynamic-slice_bitcast_fusion
  515.0 1.5 collective-permute-start.29
  517.2 2.4 collective-permute-start.31
  519.6 23.9 %leave.1 = (f32[1024,1152]{1,0:T(8,128)}, f32[32,6912]{1,0:T(8,128)}, f32[8,2304]{1,0:T(8,128)}) custom-call(bf16[1024,1152]{1,0:T(8,128)(2,1)} %get-tuple-element.59.refs_1_.refs_0_, bf16[1024,2304]{1,0:T(8,128)(2,1)} %add_convert_fusion.refs_2_.refs_1_, bf16[1024,1152]{1,0:T(8,128)(2,1)} %bitcast.131, f32[1024,1152]{1,0:T(8,128)} %get-tuple-element.63.refs_3_, ...), custom_call_target="tpu_custom_call" | custom-call | flops 2750000128 | bytes 7500000 | tf_op jit(solution)/shard_map/leave/pallas_call | solution.py:726
  543.6 1.3 fusion.58
  548.1 1.5 convert_add_fusion
  552.1 8.6 %collective-permute-done.19 = bf16[134,864]{1,0:T(8,128)(2,1)} collective-permute-done((bf16[134,864]{1,0:T(8,128)(2,1)}, bf16[134,864]{1,0:T(8,128)(2,1)}, u32[]{:S(2)}, u32[]{:S(2)}) %collective-permute-start.19) | collective-permute-done | bytes 231584 | tf_op jit(solution)/shard_map/ppermute | solution.py:802
  563.7 2.0 add_bitcast_fusion.2
  565.7 9.5 %collective-permute-done.20 = bf16[166,864]{1,0:T(8,128)(2,1)S(1)} collective-permute-done((bf16[166,864]{1,0:T(8,128)(2,1)S(1)}, bf16[166,864]{1,0:T(8,128)(2,1)S(1)}, u32[]{:S(2)}, u32[]{:S(2)}) %collective-permute-start.20) | collective-permute-done | bytes 286880 | tf_op jit(solution)/shard_map/ppermute | solution.py:802
  576.4 9.5 %collective-permute-done.21 = bf16[102,864]{1,0:T(8,128)(2,1)S(1)} collective-permute-done((bf16[102,864]{1,0:T(8,128)(2,1)S(1)}, bf16[102,864]{1,0:T(8,128)(2,1)S(1)}, u32[]{:S(2)}, u32[]{:S(2)}) %collective-permute-start.21) | collective-permute-done | bytes 176288 | tf_op jit(solution)/shard_map/ppermute | solution.py:802
  585.9 2.0 fusion.20
  587.9 1.2 collective-permute-start.22
  589.4 7.6 %collective-permute-done.22 = f32[4,8,1152]{2,1,0:T(8,128)S(1)} collective-permute-done((f32[4,8,1152]{2,1,0:T(8,128)S(1)}, f32[4,8,1152]{2,1,0:T(8,128)S(1)}, u32[]{:S(2)}, u32[]{:S(2)}) %collective-permute-start.22) | collective-permute-done | bytes 147488 | tf_op jit(solution)/shard_map/ppermute | solution.py:802
  597.2 4.2 collective-permute-done.23
  602.3 4.1 collective-permute-done.24
  607.0 5.6 reduce-scatter.6.cloned.1.call-done
  612.5 2.2 dynamic-slice_bitcast_fusion.1
  614.7 2.8 collective-permute-start.27
  621.2 12.5 %collective-permute-done.27 = bf16[2,288,576]{2,1,0:T(8,128)(2,1)S(1)} collective-permute-done((bf16[2,288,576]{2,1,0:T(8,128)(2,1)}, bf16[2,288,576]{2,1,0:T(8,128)(2,1)S(1)}, u32[]{:S(2)}, u32[]{:S(2)}) %collective-permute-start.27) | collective-permute-done | bytes 663584 | tf_op jit(solution)/shard_map/ppermute | solution.py:802
  634.0 2.1 collective-permute-start.28
  636.2 1.3 fusion.26
  637.5 14.6 %collective-permute-done.28 = bf16[1,288,576]{2,1,0:T(8,128)(2,1)S(1)} collective-permute-done((bf16[1,288,576]{2,1,0:T(8,128)(2,1)S(1)}, bf16[1,288,576]{2,1,0:T(8,128)(2,1)S(1)}, u32[]{:S(2)}, u32[]{:S(2)}) %collective-permute-start.28) | collective-permute-done | bytes 331808 | tf_op jit(solution)/shard_map/ppermute | solution.py:802
  (247 shorter events, 43.8 us)
Async XLA Ops:
  7.2 121.3 %all-gather.5.cloned.1.call-start = ((), (), s32[]{:S(2)}) async-start(), calls=%async_computation.3 | async-start | bytes 8957952 | tf_op jit(solution)/shard_map/all_gather | solution.py:776
  9.7 199.5 %all-gather.7.cloned.1.call-start = ((), (), s32[]{:S(2)}) async-start(), calls=%async_computation.4 | async-start | bytes 11943936 | tf_op jit(solution)/shard_map/all_gather | solution.py:776
  10.9 220.5 %all-gather.9.cloned.1.call-start = ((), (), s32[]{:S(2)}) async-start(), calls=%async_computation.5 | async-start | bytes 11943936 | tf_op jit(solution)/shard_map/all_gather | solution.py:776
  13.5 6.7 %copy-start.26 = (s32[1,1024]{1,0:T(1,128)S(1)}, s32[1,1024]{1,0:T(1,128)}, u32[]{:S(2)}) copy-start(s32[1,1024]{1,0:T(1,128)} %param.15) | copy-start | bytes 12292
  13.5 19.9 %copy-start.10 = (bf16[1,64,1152]{2,1,0:T(8,128)(2,1)S(1)}, bf16[1,64,1152]{2,1,0:T(8,128)(2,1)}, u32[]{:S(2)}) copy-start(bf16[1,64,1152]{2,1,0:T(8,128)(2,1)} %param.16) | copy-start | bytes 442372
  13.5 20.2 %copy-start.30 = (bf16[2304]{0:T(1024)(128)(2,1)S(1)}, bf16[2304]{0:T(1024)(128)(2,1)}, u32[]{:S(2)}) copy-start(bf16[2304]{0:T(1024)(128)(2,1)} %param.21) | copy-start | bytes 13828
  13.5 20.8 %copy-start.31 = (bf16[1152]{0:T(1024)(128)(2,1)S(1)}, bf16[1152]{0:T(1024)(128)(2,1)}, u32[]{:S(2)}) copy-start(bf16[1152]{0:T(1024)(128)(2,1)} %param.23) | copy-start | bytes 6916
  13.5 21.4 %copy-start.29 = (bf16[4608]{0:T(1024)(128)(2,1)S(1)}, bf16[4608]{0:T(1024)(128)(2,1)}, u32[]{:S(2)}) copy-start(bf16[4608]{0:T(1024)(128)(2,1)} %param.25) | copy-start | bytes 27652
  13.6 318.8 %all-gather.11.cloned.1.call-start = ((), (), s32[]{:S(2)}) async-start(), calls=%async_computation.6 | async-start | bytes 2580480 | tf_op jit(solution)/shard_map/all_gather | solution.py:917
  13.6 104.5 %collective-permute-start.11 = (bf16[288,1152]{1,0:T(8,128)(2,1)}, bf16[288,1152]{1,0:T(8,128)(2,1)}, u32[]{:S(2)}, u32[]{:S(2)}) collective-permute-start(bf16[288,1152]{1,0:T(8,128)(2,1)} %refs_10_.1), channel_id=1, source_target_pairs={{0,16},{8,24},{16,0},{24,8},{1,17},{9,25},{17,1},{25,9},{2,18},{10... | collective-permute-start | bytes 1990664 | tf_op jit(solution)/shard_map/ppermute | solution.py:912
  16.6 177.2 %collective-permute-start.10 = (bf16[288,1152]{1,0:T(8,128)(2,1)}, bf16[288,1152]{1,0:T(8,128)(2,1)}, u32[]{:S(2)}, u32[]{:S(2)}) collective-permute-start(bf16[288,1152]{1,0:T(8,128)(2,1)} %refs_10_.1), channel_id=1, source_target_pairs={{0,8},{8,0},{16,24},{24,16},{1,9},{9,1},{17,25},{25,17},{2,10},{10... | collective-permute-start | bytes 1990664 | tf_op jit(solution)/shard_map/ppermute | solution.py:911
  17.7 19.6 %copy-start.2 = (bf16[1,1024,1152]{2,1,0:T(8,128)(2,1)S(1)}, bf16[1,1024,1152]{2,1,0:T(8,128)(2,1)}, u32[]{:S(2)}) copy-start(bf16[1,1024,1152]{2,1,0:T(8,128)(2,1)} %param.14) | copy-start | bytes 7077892
  20.1 35.4 %collective-permute-start.5 = (bf16[288,864]{1,0:T(8,128)(2,1)}, bf16[288,864]{1,0:T(8,128)(2,1)}, u32[]{:S(2)}, u32[]{:S(2)}) collective-permute-start(bf16[288,864]{1,0:T(8,128)(2,1)} %pad_maximum_fusion.2), channel_id=1, source_target_pairs={{0,16},{8,24},{16,0},{24,8},{1,17},{9,25},{17,1},{25,9},{2,18},{10... | collective-permute-start | bytes 1493000 | tf_op jit(solution)/shard_map/ppermute | solution.py:882
  21.5 37.5 %collective-permute-start.3 = (s32[193]{0:T(256)S(1)}, s32[193]{0:T(256)S(1)}, u32[]{:S(2)}, u32[]{:S(2)}) collective-permute-start(s32[193]{0:T(256)S(1)} %pad_add_fusion.3), channel_id=1, source_target_pairs={{1,0},{2,1},{3,2},{4,3},{5,4},{6,5},{7,6},{9,8},{10,9},{11,10},{12... | collective-permute-start | bytes 2324 | tf_op jit(solution)/shard_map/ppermute | solution.py:877
  22.8 15.5 %collective-permute-start.4 = (s32[]{:T(128)}, s32[]{:T(128)}, u32[]{:S(2)}, u32[]{:S(2)}) collective-permute-start(s32[]{:T(128)} %bitcast.9), channel_id=1, source_target_pairs={{0,4},{1,5},{2,6},{3,7},{4,0},{5,1},{6,2},{7,3},{8,12},{9,13},{10,... | collective-permute-start | bytes 20 | tf_op jit(solution)/shard_map/ppermute | solution.py:874
  31.2 384.3 %reduce-scatter.4.cloned.1.call-start = ((), (), s32[]{:S(2)}) async-start(), calls=%async_computation.7 | async-start | bytes 11943936 | tf_op jit(solution)/shard_map/reduce_scatter | solution.py:780
  35.8 31.3 %copy-start.13 = (bf16[64,288]{1,0:T(8,128)(2,1)}, bf16[64,288]{1,0:T(8,128)(2,1)S(1)}, u32[]{:S(2)}) copy-start(bf16[64,288]{1,0:T(8,128)(2,1)S(1)} %get-tuple-element.134) | copy-start | bytes 110596
  38.3 20.7 %collective-permute-start.2 = (s32[193]{0:T(256)S(1)}, s32[193]{0:T(256)S(1)}, u32[]{:S(2)}, u32[]{:S(2)}) collective-permute-start(s32[193]{0:T(256)S(1)} %pad_add_fusion.4), channel_id=1, source_target_pairs={{0,1},{1,2},{2,3},{3,4},{4,5},{5,6},{6,7},{8,9},{9,10},{10,11},{11... | collective-permute-start | bytes 2324 | tf_op jit(solution)/shard_map/ppermute | solution.py:876
  55.5 46.6 %collective-permute-start.1 = (bf16[192,1152]{1,0:T(8,128)(2,1)}, bf16[192,1152]{1,0:T(8,128)(2,1)S(1)}, u32[]{:S(2)}, u32[]{:S(2)}) collective-permute-start(bf16[192,1152]{1,0:T(8,128)(2,1)} %get-tuple-element.104), channel_id=1, source_target_pairs={{1,0},{2,1},{3,2},{4,3},{5,4},{6,5},{7,6},{9,8},{10,9},{11,10},{12... | collective-permute-start | bytes 1327112 | tf_op jit(solution)/shard_map/ppermute | solution.py:879
  59.0 5.5 collective-permute-start.6
  59.0 44.9 %collective-permute-start = (bf16[192,1152]{1,0:T(8,128)(2,1)}, bf16[192,1152]{1,0:T(8,128)(2,1)}, u32[]{:S(2)}, u32[]{:S(2)}) collective-permute-start(bf16[192,1152]{1,0:T(8,128)(2,1)} %get-tuple-element.103), channel_id=1, source_target_pairs={{0,1},{1,2},{2,3},{3,4},{4,5},{5,6},{6,7},{8,9},{9,10},{10,11},{11... | collective-permute-start | bytes 1327112 | tf_op jit(solution)/shard_map/ppermute | solution.py:878
  64.4 6.6 %copy-start.19 = (pred[1408,24]{0,1:T(8,128)(4,1)}, pred[1408,24]{0,1:T(8,128)(4,1)S(1)}, u32[]{:S(2)}) copy-start(pred[1408,24]{0,1:T(8,128)(4,1)S(1)} %iota_compare_fusion) | copy-start | bytes 101380
  67.1 28.7 %collective-permute-start.7 = (f32[1,64,864]{2,1,0:T(8,128)}, f32[1,64,864]{2,1,0:T(8,128)}, u32[]{:S(2)}, u32[]{:S(2)}) collective-permute-start(f32[1,64,864]{2,1,0:T(8,128)} %fusion.11), channel_id=1, source_target_pairs={{0,1},{1,0},{2,3},{3,2},{4,5},{5,4},{6,7},{7,6},{8,9},{9,8},{10,11... | collective-permute-start | bytes 663560 | tf_op jit(solution)/shard_map/ppermute | solution.py:759
  96.9 12.6 %collective-permute-start.8 = (f32[2,64,864]{2,1,0:T(8,128)S(1)}, f32[2,64,864]{2,1,0:T(8,128)S(1)}, u32[]{:S(2)}, u32[]{:S(2)}) collective-permute-start(f32[2,64,864]{2,1,0:T(8,128)S(1)} %pad_maximum_fusion.4), channel_id=1, source_target_pairs={{0,2},{1,3},{2,0},{3,1},{4,6},{5,7},{6,4},{7,5},{8,10},{9,11},{10,... | collective-permute-start | bytes 1327112 | tf_op jit(solution)/shard_map/ppermute | solution.py:759
  109.8 15.6 %collective-permute-start.9 = (f32[4,24,864]{2,1,0:T(8,128)S(1)}, f32[4,24,864]{2,1,0:T(8,128)S(1)}, u32[]{:S(2)}, u32[]{:S(2)}) collective-permute-start(f32[4,24,864]{2,1,0:T(8,128)S(1)} %constant_dynamic-slice_fusion.7), channel_id=1, source_target_pairs={{0,4},{1,5},{2,6},{3,7},{4,0},{5,1},{6,2},{7,3},{8,12},{9,13},{10,... | collective-permute-start | bytes 995336 | tf_op jit(solution)/shard_map/ppermute | solution.py:892
  118.1 75.7 %collective-permute-start.12 = (bf16[288,1152]{1,0:T(8,128)(2,1)}, bf16[288,1152]{1,0:T(8,128)(2,1)S(1)}, u32[]{:S(2)}, u32[]{:S(2)}) collective-permute-start(bf16[288,1152]{1,0:T(8,128)(2,1)} %collective-permute-done.11.refs_9_.refs_12_), channel_id=1, source_target_pairs={{0,8},{8,0},{16,24},{24,16},{1,9},{9,1},{17,25},{25,17},{2,10},{10... | collective-permute-start | bytes 1990664 | tf_op jit(solution)/shard_map/ppermute | solution.py:913
  325.9 187.0 %reduce-scatter.8.cloned.1.call-start = ((), (), s32[]{:S(2)}) async-start(), calls=%async_computation.9 | async-start | bytes 13271040 | tf_op jit(solution)/shard_map/reduce_scatter | solution.py:780
  325.9 3.8 copy-start.11
  326.0 5.8 copy-start.20
  326.5 286.1 %reduce-scatter.6.cloned.1.call-start = ((), (), s32[]{:S(2)}) async-start(), calls=%async_computation.8 | async-start | bytes 13271040 | tf_op jit(solution)/shard_map/reduce_scatter | solution.py:780
  329.8 2.6 collective-permute-start.13
  330.2 6.7 %collective-permute-start.14 = (bf16[64,1152]{1,0:T(8,128)(2,1)S(1)}, bf16[64,1152]{1,0:T(8,128)(2,1)S(1)}, u32[]{:S(2)}, u32[]{:S(2)}) collective-permute-start(bf16[64,1152]{1,0:T(8,128)(2,1)S(1)} %broadcast_select_fusion.4), channel_id=1, source_target_pairs={{0,16},{8,24},{16,0},{24,8},{1,17},{9,25},{17,1},{25,9},{2,18},{10... | collective-permute-start | bytes 442376 | tf_op jit(solution)/shard_map/ppermute | solution.py:915
  331.2 7.5 %collective-permute-start.15 = (bf16[64,1152]{1,0:T(8,128)(2,1)S(1)}, bf16[64,1152]{1,0:T(8,128)(2,1)S(1)}, u32[]{:S(2)}, u32[]{:S(2)}) collective-permute-start(bf16[64,1152]{1,0:T(8,128)(2,1)S(1)} %broadcast_select_fusion.4), channel_id=1, source_target_pairs={{0,24},{8,16},{16,8},{24,0},{1,25},{9,17},{17,9},{25,1},{2,26},{10... | collective-permute-start | bytes 442376 | tf_op jit(solution)/shard_map/ppermute | solution.py:915
  332.4 6.2 copy-start.16
  410.7 66.3 %collective-permute-start.16 = (bf16[192,2304]{1,0:T(8,128)(2,1)}, bf16[192,2304]{1,0:T(8,128)(2,1)S(1)}, u32[]{:S(2)}, u32[]{:S(2)}) collective-permute-start(bf16[192,2304]{1,0:T(8,128)(2,1)} %get-tuple-element.61), channel_id=1, source_target_pairs={{0,1},{1,2},{2,3},{3,4},{4,5},{5,6},{6,7},{8,9},{9,10},{10,11},{11... | collective-permute-start | bytes 2654216 | tf_op jit(solution)/shard_map/ppermute | solution.py:939
  414.2 62.7 %collective-permute-start.17 = (bf16[192,2304]{1,0:T(8,128)(2,1)}, bf16[192,2304]{1,0:T(8,128)(2,1)S(1)}, u32[]{:S(2)}, u32[]{:S(2)}) collective-permute-start(bf16[192,2304]{1,0:T(8,128)(2,1)} %get-tuple-element.62), channel_id=1, source_target_pairs={{1,0},{2,1},{3,2},{4,3},{5,4},{6,5},{7,6},{9,8},{10,9},{11,10},{12... | collective-permute-start | bytes 2654216 | tf_op jit(solution)/shard_map/ppermute | solution.py:938
  417.6 66.1 %collective-permute-start.18 = (bf16[2,144,1152]{2,1,0:T(8,128)(2,1)}, bf16[2,144,1152]{2,1,0:T(8,128)(2,1)}, u32[]{:S(2)}, u32[]{:S(2)}) collective-permute-start(bf16[2,144,1152]{2,1,0:T(8,128)(2,1)} %dynamic-slice_bitcast_fusion.2), channel_id=1, source_target_pairs={{0,2},{1,3},{2,0},{3,1},{4,6},{5,7},{6,4},{7,5},{8,10},{9,11},{10,... | collective-permute-start | bytes 1990664 | tf_op jit(solution)/shard_map/ppermute | solution.py:802
  477.0 6.7 %copy-start.4 = (bf16[1,4,144,1152]{3,2,1,0:T(8,128)(2,1)S(1)}, bf16[1,4,144,1152]{3,2,1,0:T(8,128)(2,1)}, u32[]{:S(2)}) copy-start(bf16[1,4,144,1152]{3,2,1,0:T(8,128)(2,1)} %reduce-scatter.4.cloned.1.call-done) | copy-start | bytes 3981316
  508.7 3.2 copy-start.14
  508.7 3.9 copy-start.28
  508.7 4.0 copy-start.24
  508.8 4.0 copy-start.27
  508.8 7.7 %copy-start.3 = (f32[2,144,1152]{2,1,0:T(8,128)S(1)}, f32[2,144,1152]{2,1,0:T(8,128)}, u32[]{:S(2)}) copy-start(f32[2,144,1152]{2,1,0:T(8,128)} %convert_add_fusion.2.refs_5_) | copy-start | bytes 3981316
  515.0 33.1 %collective-permute-start.29 = (bf16[2,288,576]{2,1,0:T(8,128)(2,1)}, bf16[2,288,576]{2,1,0:T(8,128)(2,1)}, u32[]{:S(2)}, u32[]{:S(2)}) collective-permute-start(bf16[2,288,576]{2,1,0:T(8,128)(2,1)} %dynamic-slice_bitcast_fusion), channel_id=1, source_target_pairs={{0,2},{1,3},{2,0},{3,1},{4,6},{5,7},{6,4},{7,5},{8,10},{9,11},{10,... | collective-permute-start | bytes 1990664 | tf_op jit(solution)/shard_map/ppermute | solution.py:802
  517.2 46.5 %collective-permute-start.31 = (bf16[1,144,1152]{2,1,0:T(8,128)(2,1)}, bf16[1,144,1152]{2,1,0:T(8,128)(2,1)}, u32[]{:S(2)}, u32[]{:S(2)}) collective-permute-start(bf16[1,144,1152]{2,1,0:T(8,128)(2,1)} %dynamic-slice_convert_fusion.2), channel_id=1, source_target_pairs={{0,4},{1,5},{2,6},{3,7},{4,0},{5,1},{6,2},{7,3},{8,12},{9,13},{10,... | collective-permute-start | bytes 995336 | tf_op jit(solution)/shard_map/ppermute | solution.py:802
  547.1 13.6 %collective-permute-start.19 = (bf16[134,864]{1,0:T(8,128)(2,1)}, bf16[134,864]{1,0:T(8,128)(2,1)}, u32[]{:S(2)}, u32[]{:S(2)}) collective-permute-start(bf16[134,864]{1,0:T(8,128)(2,1)} %pad_maximum_fusion.8), channel_id=1, source_target_pairs={{0,1},{1,0},{2,3},{3,2},{4,5},{5,4},{6,7},{7,6},{8,9},{9,8},{10,11... | collective-permute-start | bytes 694664 | tf_op jit(solution)/shard_map/ppermute | solution.py:802
  550.8 24.6 %collective-permute-start.30 = (bf16[1,288,576]{2,1,0:T(8,128)(2,1)S(1)}, bf16[1,288,576]{2,1,0:T(8,128)(2,1)S(1)}, u32[]{:S(2)}, u32[]{:S(2)}) collective-permute-start(bf16[1,288,576]{2,1,0:T(8,128)(2,1)S(1)} %dynamic-slice_convert_fusion), channel_id=1, source_target_pairs={{0,4},{1,5},{2,6},{3,7},{4,0},{5,1},{6,2},{7,3},{8,12},{9,13},{10,... | collective-permute-start | bytes 995336 | tf_op jit(solution)/shard_map/ppermute | solution.py:802
  563.6 11.8 %copy-start.6 = (f32[2,288,576]{2,1,0:T(8,128)S(1)}, f32[2,288,576]{2,1,0:T(8,128)}, u32[]{:S(2)}) copy-start(f32[2,288,576]{2,1,0:T(8,128)} %copy-done.5) | copy-start | bytes 3981316
  563.6 11.5 %collective-permute-start.20 = (bf16[166,864]{1,0:T(8,128)(2,1)S(1)}, bf16[166,864]{1,0:T(8,128)(2,1)S(1)}, u32[]{:S(2)}, u32[]{:S(2)}) collective-permute-start(bf16[166,864]{1,0:T(8,128)(2,1)S(1)} %pad_maximum_fusion.6), channel_id=1, source_target_pairs={{0,2},{1,3},{2,0},{3,1},{4,6},{5,7},{6,4},{7,5},{8,10},{9,11},{10,... | collective-permute-start | bytes 860552 | tf_op jit(solution)/shard_map/ppermute | solution.py:802
  565.7 20.2 %copy-start.7 = (bf16[1152,864]{1,0:T(8,128)(2,1)S(1)}, bf16[1152,864]{1,0:T(8,128)(2,1)}, u32[]{:S(2)}) copy-start(bf16[1152,864]{1,0:T(8,128)(2,1)} %all-gather.11.cloned.1.call-done.refs_17_) | copy-start | bytes 5971972
  565.7 20.2 %copy-start.12 = (bf16[1,64,1152]{2,1,0:T(8,128)(2,1)S(1)}, bf16[1,64,1152]{2,1,0:T(8,128)(2,1)}, u32[]{:S(2)}) copy-start(bf16[1,64,1152]{2,1,0:T(8,128)(2,1)} %param.16) | copy-start | bytes 442372
  575.3 10.5 %collective-permute-start.21 = (bf16[102,864]{1,0:T(8,128)(2,1)S(1)}, bf16[102,864]{1,0:T(8,128)(2,1)S(1)}, u32[]{:S(2)}, u32[]{:S(2)}) collective-permute-start(bf16[102,864]{1,0:T(8,128)(2,1)S(1)} %pad_maximum_fusion.11), channel_id=1, source_target_pairs={{0,4},{1,5},{2,6},{3,7},{4,0},{5,1},{6,2},{7,3},{8,12},{9,13},{10,... | collective-permute-start | bytes 528776 | tf_op jit(solution)/shard_map/ppermute | solution.py:802
  587.9 9.0 %collective-permute-start.22 = (f32[4,8,1152]{2,1,0:T(8,128)S(1)}, f32[4,8,1152]{2,1,0:T(8,128)S(1)}, u32[]{:S(2)}, u32[]{:S(2)}) collective-permute-start(f32[4,8,1152]{2,1,0:T(8,128)S(1)} %dynamic-slice_bitcast_fusion.3), channel_id=1, source_target_pairs={{0,1},{1,0},{2,3},{3,2},{4,5},{5,4},{6,7},{7,6},{8,9},{9,8},{10,11... | collective-permute-start | bytes 442376 | tf_op jit(solution)/shard_map/ppermute | solution.py:802
  589.3 7.8 %collective-permute-start.25 = (bf16[102,864]{1,0:T(8,128)(2,1)S(1)}, bf16[102,864]{1,0:T(8,128)(2,1)S(1)}, u32[]{:S(2)}, u32[]{:S(2)}) collective-permute-start(bf16[102,864]{1,0:T(8,128)(2,1)S(1)} %pad_maximum_fusion.12), channel_id=1, source_target_pairs={{0,8},{8,0},{16,24},{24,16},{1,9},{9,1},{17,25},{25,17},{2,10},{10... | collective-permute-start | bytes 528776 | tf_op jit(solution)/shard_map/ppermute | solution.py:802
  597.0 4.4 collective-permute-start.23
  601.4 4.9 collective-permute-start.24
  602.3 15.2 %collective-permute-start.26 = (bf16[166,864]{1,0:T(8,128)(2,1)}, bf16[166,864]{1,0:T(8,128)(2,1)S(1)}, u32[]{:S(2)}, u32[]{:S(2)}) collective-permute-start(bf16[166,864]{1,0:T(8,128)(2,1)} %pad_maximum_fusion.7), channel_id=1, source_target_pairs={{0,16},{8,24},{16,0},{24,8},{1,17},{9,25},{17,1},{25,9},{2,18},{10... | collective-permute-start | bytes 860552 | tf_op jit(solution)/shard_map/ppermute | solution.py:802
  612.5 21.2 %copy-start.8 = (bf16[1,4,288,576]{3,2,1,0:T(8,128)(2,1)S(1)}, bf16[1,4,288,576]{3,2,1,0:T(8,128)(2,1)}, u32[]{:S(2)}) copy-start(bf16[1,4,288,576]{3,2,1,0:T(8,128)(2,1)} %reduce-scatter.6.cloned.1.call-done) | copy-start | bytes 3981316
  614.7 19.0 %collective-permute-start.27 = (bf16[2,288,576]{2,1,0:T(8,128)(2,1)}, bf16[2,288,576]{2,1,0:T(8,128)(2,1)S(1)}, u32[]{:S(2)}, u32[]{:S(2)}) collective-permute-start(bf16[2,288,576]{2,1,0:T(8,128)(2,1)} %dynamic-slice_bitcast_fusion.1), channel_id=1, source_target_pairs={{0,2},{1,3},{2,0},{3,1},{4,6},{5,7},{6,4},{7,5},{8,10},{9,11},{10,... | collective-permute-start | bytes 1990664 | tf_op jit(solution)/shard_map/ppermute | solution.py:802
  621.2 15.0 %copy-start.21 = (bf16[64,288]{1,0:T(8,128)(2,1)S(1)}, bf16[64,288]{1,0:T(8,128)(2,1)}, u32[]{:S(2)}) copy-start(bf16[64,288]{1,0:T(8,128)(2,1)} %get-tuple-element.128) | copy-start | bytes 110596
  621.2 15.0 %copy-start.22 = (bf16[64,288]{1,0:T(8,128)(2,1)S(1)}, bf16[64,288]{1,0:T(8,128)(2,1)}, u32[]{:S(2)}) copy-start(bf16[64,288]{1,0:T(8,128)(2,1)} %get-tuple-element.129) | copy-start | bytes 110596
  621.2 15.0 %copy-start.23 = (bf16[64,288]{1,0:T(8,128)(2,1)S(1)}, bf16[64,288]{1,0:T(8,128)(2,1)}, u32[]{:S(2)}) copy-start(bf16[64,288]{1,0:T(8,128)(2,1)} %get-tuple-element.130) | copy-start | bytes 110596
  634.0 18.1 %collective-permute-start.28 = (bf16[1,288,576]{2,1,0:T(8,128)(2,1)S(1)}, bf16[1,288,576]{2,1,0:T(8,128)(2,1)S(1)}, u32[]{:S(2)}, u32[]{:S(2)}) collective-permute-start(bf16[1,288,576]{2,1,0:T(8,128)(2,1)S(1)} %dynamic-slice_convert_fusion.1), channel_id=1, source_target_pairs={{0,4},{1,5},{2,6},{3,7},{4,0},{5,1},{6,2},{7,3},{8,12},{9,13},{10,... | collective-permute-start | bytes 995336 | tf_op jit(solution)/shard_map/ppermute | solution.py:802
  636.2 17.8 %copy-start.1 = (bf16[288,4608]{1,0:T(8,128)(2,1)S(1)}, bf16[288,4608]{1,0:T(8,128)(2,1)}, u32[]{:S(2)}) copy-start(bf16[288,4608]{1,0:T(8,128)(2,1)} %param.24) | copy-start | bytes 7962628
  (8 other events, 11.6 us)
Sparse Core Ops, SparseCore 0:
  10.5 85.9 all-gather.4
  98.3 67.2 all-gather.6
  167.5 63.8 all-gather.8
  233.4 22.3 all-gather.10
  326.0 82.2 reduce-scatter.3
  411.6 101.2 reduce-scatter.7
  516.9 95.6 reduce-scatter.5

commit v3 on v2

--- a/solution.py
+++ b/solution.py
@@ -18,6 +18,8 @@
 BLOCK = 256
 SPAN = BLOCK + 2 * MAXLEN
 CHUNK = 128
+STRIP = 320
+STRIP_BACK = 640
 BF, F32 = jnp.bfloat16, jnp.float32
 SCORE_SCALE = 1.0 / math.sqrt(HEAD)
 LOG2E = 1.4426950408889634
@@ -87,11 +89,11 @@
             first, inside = head_lanes(head, width)
             query = masked(query_ref, first, inside)
             peak = jnp.full((8, BLOCK), -3e38, F32)
-            for start in range(0, SPAN, CHUNK):
-                rows = slice(start, start + CHUNK)
+            for start in range(0, SPAN, STRIP):
+                rows = slice(start, start + STRIP)
                 score = dot_rows(view[rows, pl.ds(first, 256)], query) * factor + bias[rows, :]
                 scores[odd, rows, :] = score
-                peak = jnp.maximum(peak, jnp.max(score.reshape(CHUNK // 8, 8, BLOCK), axis=0))
+                peak = jnp.maximum(peak, jnp.max(score.reshape(STRIP // 8, 8, BLOCK), axis=0))
             peak = jnp.max(peak, axis=0, keepdims=True)
             total = jnp.zeros((8, BLOCK), F32)
             for start in range(0, SPAN, CHUNK):
@@ -164,8 +166,8 @@
             grad = masked(grad_ref, first, inside)
             peak = peak_ref[pl.ds(head, 1), :]
             mean = delta[pl.ds(head, 1), :]
-            for start in range(0, SPAN, CHUNK):
-                rows = slice(start, start + CHUNK)
+            for start in range(0, SPAN, STRIP_BACK):
+                rows = slice(start, start + STRIP_BACK)
                 score = dot_rows(view[rows, pl.ds(first, 256)], query) * factor
                 power = jnp.exp2(score + (bias[rows, :] - peak))
                 slope = dot_rows(view[rows, pl.ds(first + width, 256)], grad)
@@ -301,6 +303,7 @@
 
 
 BANDS = 4
+FEED_ROWS = 512
 EPSILON = 1e-06
 ROOT = math.sqrt(2.0 / math.pi)
 CUBE = 0.044715
@@ -466,8 +469,35 @@
     )(place, mixed, tokens, cotangent, select, parts, bias, *pieces, *after)
 
 
-def feed_kernel(input_ref, grad_ref, expand_ref, contract_ref, bias_ref,
-                out_ref, grad_input_ref, expand_grad_ref, contract_grad_ref, bias_grad_ref, grad_sum_ref,
+def feed_kernel(later, place_ref, input_ref, grad_ref, expand_ref, bias_ref, *refs):
+    if later:
+        contract_ref, before_out_ref, before_grad_ref = refs[:3]
+        refs = refs[7:]
+    else:
+        own_ref, near_ref = refs[:2]
+        held, sems = refs[-2:]
+        refs = refs[2:-2]
+        before_out_ref = before_grad_ref = None
+        step = pl.program_id(0)
+        own_copy = pltpu.make_async_copy(own_ref, held.at[0], sems.at[0])
+        near_copy = pltpu.make_async_copy(near_ref, held.at[1], sems.at[1])
+
+        @pl.when(step == 0)
+        def _():
+            own_copy.start()
+            near_copy.start()
+            own_copy.wait()
+
+        @pl.when(step == 1)
+        def _():
+            near_copy.wait()
+
+        contract_ref = held.at[step]
+    feed_step(place_ref, input_ref, grad_ref, expand_ref, contract_ref, bias_ref, before_out_ref, before_grad_ref, *refs)
+
+
+def feed_step(place_ref, input_ref, grad_ref, expand_ref, contract_ref, bias_ref, before_out_ref, before_grad_ref,
+                out_ref, grad_input_ref, keep_ref, send_ref, contract_grad_ref, bias_grad_ref, grad_sum_ref,
                 input_turned, grad_turned, active, hidden_grad):
     step = pl.program_id(0)
     rows, width = input_ref.shape
@@ -477,13 +507,17 @@
         input_turned[...] = input_ref[...].T
         grad_turned[...] = grad_ref[...].T
         grad_sum_ref[...] = column_sum(grad_ref[...].astype(F32))
-        out_ref[...] = jnp.zeros_like(out_ref)
-        grad_input_ref[...] = jnp.zeros_like(grad_input_ref)
+        if before_out_ref is None:
+            out_ref[...] = jnp.zeros_like(out_ref)
+            grad_input_ref[...] = jnp.zeros_like(grad_input_ref)
+        else:
+            out_ref[...] = before_out_ref[...]
+            grad_input_ref[...] = before_grad_ref[...]
 
     bias_grad_ref[...] = jnp.zeros_like(bias_grad_ref)
 
     def band(index, carry):
-        here = pl.ds(pl.multiple_of(index * BLOCK, BLOCK), BLOCK)
+        here = pl.ds(pl.multiple_of(index * FEED_ROWS, FEED_ROWS), FEED_ROWS)
         hidden = dot_plain(input_ref[here, :], expand_ref[...]) + bias_ref[...]
         square = hidden * hidden
         bent = jnp.tanh(ROOT * hidden * (1.0 + CUBE * square))
@@ -498,13 +532,13 @@
         grad_input_ref[here, :] += dot_rows(low, expand_ref[...])
         return carry
 
-    lax.fori_loop(0, rows // BLOCK, band, 0)
+    lax.fori_loop(0, rows // FEED_ROWS, band, 0)
     share = width // 4
-    block = expand_grad_ref.shape[4]
+    block = keep_ref.shape[4]
     for index in range(4):
-        part = dot_plain(input_turned[index * share : (index + 1) * share, :], hidden_grad[...]).astype(BF)
-        for owner in range(width // block):
-            expand_grad_ref[index, owner % 2, owner // 2] = part[:, owner * block : (owner + 1) * block]
+        start = pl.multiple_of(place_ref[index] * 16, 16)
+        part = dot_plain(input_turned[pl.ds(start, share), :], hidden_grad[...]).astype(BF)
+        store_owners(send_ref if index % 2 else keep_ref, place_ref[4 + index], part, 0, block, 0)
     for index in range(4):
         here = slice(index * share, (index + 1) * share)
         part = dot_plain(grad_turned[here, :], active[...]).astype(BF)
@@ -517,57 +551,68 @@
                 contract_grad_ref[0, side, rest] = part[start : start + rows]
 
 
-def feed(seq_count, inputs, grad_feed, expand, contract, bias):
+def feed(place, seq_count, inputs, grad_feed, expand, contracts, bias, before=()):
     rows, width = inputs.shape
     hidden = expand.shape[1]
-    steps = hidden // width
+    quarters = hidden // width
     whole_rows = once((rows, width))
     rest = seq_count // 2
-    expand_shape = (4, 2, rest, width // 4, hidden // seq_count)
+    expand_shape = (2, 2, rest, width // 4, hidden // seq_count)
+    expand_block = pl.BlockSpec((2, 2, rest // quarters) + expand_shape[3:], lambda i, place: (0, 0, place[8 + i], 0, 0))
     if width // seq_count % 16 == 0:
-        contract_shape = (steps, 2, rest, width // seq_count, width)
+        contract_shape = (quarters, 2, rest, width // seq_count, width)
     else:
-        contract_shape = (steps, width, width)
+        contract_shape = (quarters, width, width)
+    zeros = (0,) * (len(contract_shape) - 1)
+    any_spec = pl.BlockSpec(memory_space=pl.ANY)
     result = pl.pallas_call(
-        feed_kernel,
-        grid=(steps,),
-        in_specs=[
-            whole_rows,
-            whole_rows,
-            pl.BlockSpec((width, width), lambda i: (0, i)),
-            pl.BlockSpec((width, width), lambda i: (i, 0)),
-            pl.BlockSpec((1, width), lambda i: (0, i)),
-        ],
-        out_specs=[
-            whole_rows,
-            whole_rows,
-            pl.BlockSpec((4, 2, rest // steps) + expand_shape[3:], lambda i: (0, 0, i, 0, 0)),
-            pl.BlockSpec((1,) + contract_shape[1:], lambda i: (i,) + (0,) * (len(contract_shape) - 1)),
-            pl.BlockSpec((8, width), lambda i: (0, i)),
-            once((8, width)),
-        ],
-        scratch_shapes=[
-            pltpu.VMEM((width, rows), BF),
-            pltpu.VMEM((width, rows), BF),
-            pltpu.VMEM((rows, width), BF),
-            pltpu.VMEM((rows, width), BF),
-        ],
+        functools.partial(feed_kernel, bool(before)),
+        grid_spec=pltpu.PrefetchScalarGridSpec(
+            num_scalar_prefetch=1,
+            grid=(quarters // 2,),
+            in_specs=[
+                whole_rows,
+                whole_rows,
+                pl.BlockSpec((width, width), lambda i, place: (0, place[8 + i])),
+                pl.BlockSpec((1, width), lambda i, place: (0, place[8 + i])),
+            ]
+            + (
+                [pl.BlockSpec((width, width), lambda i, place: (place[8 + i], 0))] + [whole_rows] * 2 + [any_spec] * 4
+                if before
+                else [any_spec] * 2
+            ),
+            out_specs=[
+                whole_rows,
+                whole_rows,
+                expand_block,
+                expand_block,
+                pl.BlockSpec((1,) + contract_shape[1:], lambda i, place: (place[8 + i],) + zeros),
+                pl.BlockSpec((8, width), lambda i, place: (0, place[8 + i])),
+                once((8, width)),
+            ],
+            scratch_shapes=[
+                pltpu.VMEM((width, rows), BF),
+                pltpu.VMEM((width, rows), BF),
+                pltpu.VMEM((rows, width), BF),
+                pltpu.VMEM((rows, width), BF),
+            ]
+            + ([] if before else [pltpu.VMEM((2, width, width), BF), pltpu.SemaphoreType.DMA((2,))]),
+        ),
         out_shape=[
             jax.ShapeDtypeStruct((rows, width), F32),
             jax.ShapeDtypeStruct((rows, width), F32),
+            jax.ShapeDtypeStruct(expand_shape, BF),
             jax.ShapeDtypeStruct(expand_shape, BF),
             jax.ShapeDtypeStruct(contract_shape, BF),
             jax.ShapeDtypeStruct((8, hidden), F32),
             jax.ShapeDtypeStruct((8, width), F32),
         ],
+        input_output_aliases={8: 2, 9: 3, 10: 4, 11: 5} if before else {},
         compiler_params=kernel_params(),
-        cost_estimate=cost(94),
-        name="feed",
-    )(inputs, grad_feed, expand, contract, bias)
-    feed_out, grad_input, expand_grad, contract_grad, expand_sums, feed_sums = result
-    if len(contract_shape) == 3:
-        contract_grad = contract_grad.reshape(steps, rest, 2, width // seq_count, width).swapaxes(1, 2)
-    return feed_out, grad_input, expand_grad, contract_grad, expand_sums, feed_sums
+        cost_estimate=cost(47),
+        name="feed_later" if before else "feed",
+    )(place, inputs, grad_feed, expand, bias, *contracts, *before)
+    return result
 
 
 def leave_feed_kernel(count, place_ref, feed_ref, grad_input_ref, middle_ref, attn_ref, cotangent_ref, select_ref,
@@ -642,16 +687,17 @@
         at += count
 
 
-def weight_grad_kernel(input_ref, query_ref, pair_ref, mixed_ref, attn_ref, out_ref, turned):
+def weight_grad_kernel(place_ref, input_ref, query_ref, pair_ref, mixed_ref, attn_ref, keep_ref, send_ref, turned):
     step = pl.program_id(0)
     width = query_ref.shape[1]
     share = width // 4
-    block = out_ref.shape[4] // 4
+    block = keep_ref.shape[4] // 4
 
     def store(grad_ref, first, block, base):
         for index in range(4):
-            part = dot_plain(turned[index * share : (index + 1) * share, :], grad_ref[...]).astype(BF)
-            store_owners(out_ref, index, part, first, block, base)
+            start = pl.multiple_of(place_ref[index] * 16, 16)
+            part = dot_plain(turned[pl.ds(start, share), :], grad_ref[...]).astype(BF)
+            store_owners(send_ref if index % 2 else keep_ref, place_ref[4 + index], part, first, block, base)
 
     @pl.when(step == 0)
     def _():
@@ -670,28 +716,31 @@
         store(attn_ref, 0, block, 3 * block)
 
 
-def weight_grad(seq_count, inputs, query, pair, mixed, attn, after):
+def weight_grad(place, seq_count, inputs, query, pair, mixed, attn, after):
     rows, width = query.shape
-    shape = (4, 2, seq_count // 2, width // 4, 4 * width // seq_count)
+    shape = (2, 2, seq_count // 2, width // 4, 4 * width // seq_count)
     whole_rows = once((rows, width))
     return pl.pallas_call(
-        skipping(weight_grad_kernel, 5, len(after)),
+        skipping(weight_grad_kernel, 6, len(after)),
+        grid_spec=pltpu.PrefetchScalarGridSpec(
+        num_scalar_prefetch=1,
         grid=(4,),
         in_specs=[
             whole_rows,
             whole_rows,
-            pl.BlockSpec((rows, width), lambda i: (0, jnp.clip(i - 1, 0, 1))),
+            pl.BlockSpec((rows, width), lambda i, *_: (0, jnp.clip(i - 1, 0, 1))),
             whole_rows,
             whole_rows,
         ]
         + [pl.BlockSpec(memory_space=pl.ANY)] * len(after),
-        out_specs=once(shape),
+        out_specs=[once(shape), once(shape)],
         scratch_shapes=[pltpu.VMEM((width, rows), BF)],
-        out_shape=jax.ShapeDtypeStruct(shape, BF),
+        ),
+        out_shape=[jax.ShapeDtypeStruct(shape, BF)] * 2,
         compiler_params=kernel_params(),
         cost_estimate=cost(2),
         name="weight_grad",
-    )(inputs, query, pair, mixed, attn, *after)
+    )(place, inputs, query, pair, mixed, attn, *after)
 
 
 def leave_kernel(query_ref, pair_ref, tokens_ref, grad_middle_ref, select_ref, gather_ref, parts_ref, weight_ref,
@@ -779,6 +828,19 @@
 def scattered(grad):
     return lax.psum_scatter(
         grad.reshape(-1, *grad.shape[2:]), ("dp", "seq"), scatter_dimension=0, axis_index_groups=neighbour_groups()
+    )
+
+
+def scattered_core(keep, send, other):
+    seq_count = lax.axis_size("seq")
+    total = gate((wide(keep) + wide(swapped(send, "dp", 1))).astype(BF), other)
+    groups = [
+        [(2 * y + core) * seq_count + 2 * pair + side for y in range(2) for side in range(2)]
+        for core in range(2)
+        for pair in range(seq_count // 2)
+    ]
+    return total, lax.psum_scatter(
+        total.reshape(-1, *total.shape[2:]), ("dp", "seq"), scatter_dimension=0, axis_index_groups=groups
     )
 
 
@@ -885,7 +947,9 @@
     turned = [lax.dynamic_slice_in_dim(cond_act, (own ^ index) * share_rows, share_rows, 1) for index in (0, 2, 1, 3)]
     product = jnp.dot(jnp.concatenate(turned, axis=1), piece, preferred_element_type=F32)
     product += row(own_columns(modulation_bias, 0))
-    product = doubled(product[None], "seq", seq_bits[:-1])
+    product = doubled(product[None], "seq", seq_bits[:1])
+    output_far = lax.ppermute(gate(output_weight, product), "dp", partners("dp", 2))
+    product = doubled(product, "seq", seq_bits[1:-1])
     for early in (low_rows, high_rows, first_of_next.astype(F32)[None], first_of_top.astype(F32)[None]):
         product = gate(product, early)
     mine = lax.dynamic_slice_in_dim(product, first_image, WIN, 1)
@@ -909,7 +973,6 @@
         input_full, row_count, wide_rows, select, mixer_parts, row(query_value_bias)
     )
     output_near = lax.ppermute(output_weight, "dp", partners("dp", 1))
-    output_far = lax.ppermute(output_weight, "dp", partners("dp", 2))
     output_pieces = [output_weight, output_near, output_far, lax.ppermute(output_far, "dp", partners("dp", 1))]
     output_at = (jnp.stack([own ^ index for index in range(4)]) * (share_rows // 16)).astype(jnp.int32)
     acts = [cond_act] + [lax.ppermute(gate(cond_act, input_attn), "dp", partners("dp", mask)) for mask in (1, 2, 3)]
@@ -923,17 +986,24 @@
         output_at, output_pieces, attn_mixed, token_rows, grad_out, select, feed_parts, row(output_bias),
         (),
     )
-    feed_out, grad_input_feed, expand_grad, contract_grad, expand_sums, feed_sums = feed(
-        seq_count, input_feed, grad_feed, expand_full, contract_full, row(expand_bias)
-    )
+    chunks = jnp.stack([own ^ index for index in range(4)])
+    chunks = jnp.concatenate([chunks * (share_rows // 16), chunks // 2, chunks]).astype(jnp.int32)
+    contract_pair = contract_weight, lax.ppermute(contract_weight, "dp", partners("dp", 1))
+    feed_before = feed(chunks[:10], seq_count, input_feed, grad_feed, expand_full, contract_pair, row(expand_bias))
+    later = jnp.concatenate([chunks[:8], chunks[10:]])
+    feed_out, grad_input_feed, expand_keep, expand_send, contract_grad, expand_sums, feed_sums = feed(
+        later, seq_count, input_feed, grad_feed, expand_full, (contract_full,), row(expand_bias), feed_before[:6]
+    )
+    if len(contract_grad.shape) == 3:
+        contract_grad = contract_grad.reshape(4, seq_count // 2, 2, width // seq_count, width).swapaxes(1, 2)
     contract_rest = scattered(contract_grad)
-    expand_rest = scattered(expand_grad)
     layer_out, grad_middle, grad_attn, grad_mixed, feed_images, attn_sums = leave_feed(
         output_at, output_pieces, feed_out, grad_input_feed, middle, attn_out, grad_out, select, gather,
         feed_parts, row(contract_bias), (*acts[1:], slice_full),
     )
+    expand_total, expand_rest = scattered_core(expand_keep, expand_send, grad_mixed)
     grad_query_edge, rim_low, rim_high, grad_edge = attend_back(
-        True, queries, attn_mixed, grad_mixed, row_peaks, key_value, marks
+        True, queries, attn_mixed, grad_mixed, row_peaks, key_value, marks, (), (expand_total,)
     )
     from_next = lax.ppermute(rim_low, "seq", back)
     from_prev = lax.ppermute(rim_high, "seq", onward)
@@ -948,15 +1018,16 @@
     contract_stages = along_rest(contract_rest)
     total_contract = contract_stages[-1][0]
     total_expand = along_rest(expand_rest)[-1][0]
-    input_grad = weight_grad(
-        seq_count, input_attn, grad_query, grad_pair, attn_mixed, grad_attn, (contract_stages[0],)
-    )
-    input_rest = scattered(input_grad)
+    input_keep, input_send = weight_grad(
+        chunks, seq_count, input_attn, grad_query, grad_pair, attn_mixed, grad_attn, ()
+    )
+    input_rest = scattered_core(input_keep, input_send, input_keep)[1]
     grad_rows, all_images, packed_sums = leave(
         input_full, grad_query, grad_pair, token_rows, grad_middle, select, gather, mixer_parts, feed_images,
-        (input_grad,),
-    )
-    input_total = along_rest(input_rest)[-1][0]
+        (input_send, contract_stages[0]),
+    )
+    input_stages = along_rest(input_rest)
+    input_total = input_stages[-1][0]
     input_width = 3 * width // seq_count
     total_input, total_output = input_total[:, :input_width], input_total[:, input_width:]
 
@@ -987,6 +1058,8 @@
     column_grads = lax.dynamic_update_slice_in_dim(empty, mine.swapaxes(0, 1), first_image, 1)
     column_grads += lax.dynamic_update_slice_in_dim(empty, got, first_of_next, 1)
     for bit in seq_bits[1:]:
+        if bit == top:
+            column_grads = gate(column_grads, input_rest)
         pairs = column_grads.reshape(-1, 2, images, columns)
         mine = (place_in_seq // bit) % 2
         got, biases = joined(lax.dynamic_index_in_dim(pairs, 1 - mine, 1, keepdims=False), "seq", bit)
@@ -1008,6 +1081,8 @@
     )
     grad_condition = silu_back(grad_act)[0].reshape(seq_count, -1, width)
     for bit in seq_bits:
+        if bit == seq_bits[1]:
+            grad_condition = gate(grad_condition, input_stages[0])
         pairs = grad_condition.reshape(-1, 2, *grad_condition.shape[1:])
         mine = (place_in_seq // bit) % 2
         got = swapped(lax.dynamic_index_in_dim(pairs, 1 - mine, 1, keepdims=False), "seq", bit, F32)

time: 667 us -> 646 us (0.969)
  waiting for transfers between devices: 152 us -> 111 us
  Pallas kernels: 348 us -> 310 us
  starting transfers between devices: 50.3 us -> 69.2 us
  other arithmetic: 34.8 us -> 50.5 us
  local copies, waits for them, and re-layouts: 46.3 us -> 62 us
    pallas_call x2, Pallas kernels: 106 us -> 63.1 us  [backward(): pl.pallas_call(skipping(functools.partial(backward_kernel, edge), 7 + len...]
    ppermute x14 -> x16, starting transfers between devices: 15 us -> 38.7 us  [swapped(): return lax.ppermute(value.astype(kind), axis, partners(axis, bit))]
    all_gather x3, waiting for transfers between devices: 22.2 us -> 0.04 us  [gathered(): lax.all_gather(half, ('dp', 'seq'), axis=0, tiled=True, axis_index_groups...]
    select_n x2 -> x7, other arithmetic: 0.23 us -> 17.7 us  [gate(): return jnp.where(first == first, value, jnp.zeros_like(value))]
    pallas_call x2 -> x3, Pallas kernels: 117 us -> 132 us  [the longest x2 108 us: feed(): pl.pallas_call(functools.partial(feed_kernel, bool(before)), grid_spec=pl...]
    ppermute x14 -> x16, waiting for transfers between devices: 70.5 us -> 55.5 us  [swapped(): return lax.ppermute(value.astype(kind), axis, partners(axis, bit))]
    ppermute x1, waiting for transfers between devices: 12.1 us -> 0.01 us  [shards(): piece_far = lax.ppermute(piece, 'dp', partners('dp', 2))]
    ppermute x1, waiting for transfers between devices: 0.01 us -> 11.1 us  [shards(): from_prev = lax.ppermute(rim_high, 'seq', onward)]
  transfers between devices with their start and end apart: 39 -> 42, of which waited for: 17 -> 20; matrix products, arithmetic and copies ran while one was open for 12% -> 17% of each run, Pallas kernels for 53% -> 48%
where the time goes in v3:
time: 646 us; the launch traced here: 639 us
  Pallas kernels  310 us (48%)
  waiting for transfers between devices  111 us (17%)
  starting transfers between devices  69.2 us (11%)
  local copies, waits for them, and re-layouts  62 us (10%)
  other arithmetic  50.5 us (8%)
  between operations  30.6 us (5%)
    pallas_call x2, Pallas kernels, feed(): pl.pallas_call(functools.partial(feed_kernel, bool(before)), grid_spec=pl...  108 us
    pallas_call x2, Pallas kernels, backward(): pl.pallas_call(skipping(functools.partial(backward_kernel, edge), 7 + len...  63.1 us
    ppermute x16, waiting for transfers between devices, swapped(): return lax.ppermute(value.astype(kind), axis, partners(axis, bit))  55.5 us
    ppermute x16, starting transfers between devices, swapped(): return lax.ppermute(value.astype(kind), axis, partners(axis, bit))  38.7 us
    pallas_call x1, Pallas kernels, forward(): pl.pallas_call(skipping(forward_kernel, 4, len(after)), grid=(count,), in...  33.5 us
    pallas_call x1, Pallas kernels, weight_grad(): pl.pallas_call(skipping(weight_grad_kernel, 6, len(after)), grid_spec=plt...  24.8 us
    pallas_call x1, Pallas kernels, leave(): pl.pallas_call(skipping(leave_kernel, 9, len(after)), grid=(BANDS,), in_s...  23.1 us
    pallas_call x1, Pallas kernels, leave_feed(): pl.pallas_call(skipping(functools.partial(leave_feed_kernel, len(pieces))...  22.1 us
  transfers between devices with their start and end apart: 42, of which 20 were waited for; matrix products, arithmetic and copies ran while one was open for 17% of the time, Pallas kernels for 48%

profile of v3, /device:TPU:0, one launch (start us, length us, event | category | flops | bytes accessed | tf_op | source)
XLA Modules:
  0.0 639.3 jit_solution(6304351629114798603)
XLA Ops:
  7.3 2.4 constant_dynamic-slice_fusion.6
  11.0 2.5 constant_dynamic-slice_fusion.4
  17.6 2.5 collective-permute-start.5
  22.8 4.5 collective-permute-start.2
  27.3 4.0 collective-permute-start.4
  31.3 2.1 constant_dynamic-slice_fusion.3
  44.3 5.7 collective-permute-start
  50.1 2.4 pad_maximum_fusion.1
  54.5 1.5 collective-permute-done.6
  56.0 1.9 fusion.13
  57.9 1.8 collective-permute-start.7
  65.4 7.8 %collective-permute-done = bf16[192,1152]{1,0:T(8,128)(2,1)} collective-permute-done((bf16[192,1152]{1,0:T(8,128)(2,1)}, bf16[192,1152]{1,0:T(8,128)(2,1)}, u32[]{:S(2)}, u32[]{:S(2)}) %collective-permute-start) | collective-permute-done | bytes 442400 | tf_op jit(solution)/shard_map/ppermute | solution.py:940
  75.7 7.2 %collective-permute-done.7 = f32[1,64,864]{2,1,0:T(8,128)S(1)} collective-permute-done((f32[1,64,864]{2,1,0:T(8,128)S(1)}, f32[1,64,864]{2,1,0:T(8,128)S(1)}, u32[]{:S(2)}, u32[]{:S(2)}) %collective-permute-start.7) | collective-permute-done | bytes 221216 | tf_op jit(solution)/shard_map/ppermute | solution.py:808
  86.5 9.2 %collective-permute-done.8 = f32[2,64,864]{2,1,0:T(8,128)S(1)} collective-permute-done((f32[2,64,864]{2,1,0:T(8,128)S(1)}, f32[2,64,864]{2,1,0:T(8,128)S(1)}, u32[]{:S(2)}, u32[]{:S(2)}) %collective-permute-start.8) | collective-permute-done | bytes 442400 | tf_op jit(solution)/shard_map/ppermute | solution.py:808
  96.4 4.7 pad_maximum_fusion.tokens_ref
  101.1 1.5 collective-permute-done.11.refs_9_.refs_12_
  102.7 10.6 %collective-permute-done.9 = f32[4,24,864]{2,1,0:T(8,128)S(1)} collective-permute-done((f32[4,24,864]{2,1,0:T(8,128)S(1)}, f32[4,24,864]{2,1,0:T(8,128)S(1)}, u32[]{:S(2)}, u32[]{:S(2)}) %collective-permute-start.9) | collective-permute-done | bytes 331808 | tf_op jit(solution)/shard_map/ppermute | solution.py:956
  116.4 21.8 %project.1 = (bf16[1408,1152]{1,0:T(8,128)(2,1)}, bf16[1408,1152]{1,0:T(8,128)(2,1)}, bf16[1408,2304]{1,0:T(8,128)(2,1)}) custom-call(bf16[1408,1152]{1,0:T(8,128)(2,1)} %pad_maximum_fusion.tokens_ref, bf16[1408,128]{1,0:T(8,128)(2,1)} %add_convert_fusion.3.select_ref.refs_4_.refs_6_, bf16[128,2304]{1,0:T(8,128)(2,1)} %maximum_maximum_fusion.1.parts_ref.refs_6_, ...), custom_call_target="tpu_custom_call" | custom-call | flops 27499999232 | bytes 75000000 | tf_op jit(solution)/shard_map/project/pallas_call | solution.py:408
  138.2 33.5 %attend.1 = (bf16[1024,1152]{1,0:T(8,128)(2,1)}, f32[16,1024]{1,0:T(8,128)}) custom-call(bf16[1408,1152]{1,0:T(8,128)(2,1)} %get-tuple-element.52.refs_0_, bf16[1408,2304]{1,0:T(8,128)(2,1)} %get-tuple-element.53.refs_1_.refs_4_, s32[4,1,640]{2,1,0:T(1,128)} %broadcast_in_dim.63.refs_2_.refs_5_, s32[4,1,256]{2,1,0:T(1,128)} %bitcast.171), custom_call_target="tpu_custom_call" | custom-call | flops 50600001536 | bytes 138000000 | tf_op jit(solution)/shard_map/attend/pallas_call | solution.py:242
  172.5 14.0 %enter_feed.1 = (f32[1024,1152]{1,0:T(8,128)}, f32[1024,1152]{1,0:T(8,128)}, bf16[1024,1152]{1,0:T(8,128)(2,1)}, bf16[1024,1152]{1,0:T(8,128)(2,1)}) custom-call(s32[4]{0:T(128)} %copy-done.31, bf16[1024,1152]{1,0:T(8,128)(2,1)} %get-tuple-element.54.refs_1_.refs_4_, bf16[1024,1152]{1,0:T(8,128)(2,1)} %bitcast.140, bf16[1024,1152]{1,0:T(8,128)(2,1)} %bitcast.149, ...), custom_call_target="tpu_custom_call" | custom-call | flops 15399999488 | bytes 42000000 | tf_op jit(solution)/shard_map/enter_feed/pallas_call | solution.py:455
  186.5 54.0 %feed.1 = (f32[1024,1152]{1,0:T(8,128)}, f32[1024,1152]{1,0:T(8,128)}, bf16[2,2,4,288,576]{4,3,2,1,0:T(8,128)(2,1)}, bf16[2,2,4,288,576]{4,3,2,1,0:T(8,128)(2,1)...) custom-call(s32[10]{0:T(128)} %get-tuple-element.178.place_ref, ...), custom_call_target="tpu_custom_call" | custom-call | flops 51699998720 | bytes 141000000 | tf_op jit(solution)/shard_map/feed/pallas_call | solution.py:568
  240.6 53.5 %feed_later.1 = (f32[1024,1152]{1,0:T(8,128)}, f32[1024,1152]{1,0:T(8,128)}, bf16[2,2,4,288,576]{4,3,2,1,0:T(8,128)(2,1)}, bf16[2,2,4,288,576]{4,3,2,1,0:T(8,128...) custom-call(s32[10]{0:T(128)} %get-tuple-element.179.place_ref, ...), custom_call_target="tpu_custom_call", output_to_operand_aliasing={{2}: (8, {}), {3}: (9, {}), {4}: (10, {}), {5}: (11, {})} | custom-call | flops 51699998720 | bytes 141000000 | tf_op jit(solution)/shard_map/feed_later/pallas_call | solution.py:568
  298.4 1.5 collective-permute-start.16
  300.6 3.7 collective-permute-done.14.refs_14_
  305.0 1.9 collective-permute-done.16.refs_16_
  307.5 22.1 %leave_feed.1 = (bf16[1024,1152]{1,0:T(8,128)(2,1)}, f32[1024,1152]{1,0:T(8,128)}, bf16[1024,1152]{1,0:T(8,128)(2,1)}, bf16[1024,1152]{1,0:T(8,128)(2,1)}, f32[32,4608]{1,0:T(8,128)}, /*index=5*/f32[8,1152]{1,0:T(8,128)}) custom-call(s32[4]{0:T(128)} %copy-done.31, f32[1024,1152]{1,0:T(8,128)} %get-tuple-element.63.refs_1_, ...), custom_call_target="tpu_custom_call" | custom-call | flops 2420000000 | bytes 6600000 | tf_op jit(solution)/shard_map/leave_feed/pallas_call | solution.py:659
  332.1 9.0 %fusion.refs_7_ = bf16[2,2,4,288,576]{4,3,2,1,0:T(8,128)(2,1)} fusion(bf16[2,2,4,288,576]{4,3,2,1,0:T(8,128)(2,1)} %collective-permute-done.17, bf16[2,2,4,288,576]{4,3,2,1,0:T(8,128)(2,1)} %get-tuple-element.71, pred[]{:T(512)} %bitcast.25), kind=kLoop, calls=%fused_computation.3 | loop fusion | flops 13271040 | bytes 15925249 | tf_op jit(solution)/shard_map/jit(_where)/select_n | solution.py:860
  341.2 31.2 %attend_back_edge.1 = (bf16[1024,1152]{1,0:T(8,128)(2,1)}, bf16[192,2304]{1,0:T(8,128)(2,1)}, bf16[192,2304]{1,0:T(8,128)(2,1)}, f32[2,448,2304]{2,1,0:T(8,128)}) custom-call(bf16[1408,1152]{1,0:T(8,128)(2,1)} %get-tuple-element.52.refs_0_, bf16[1024,1152]{1,0:T(8,128)(2,1)} %get-tuple-element.54.refs_1_.refs_4_, ...), custom_call_target="tpu_custom_call" | custom-call | flops 4840000000 | bytes 13200000 | tf_op jit(solution)/shard_map/attend_back_edge/pallas_call | solution.py:282
  372.4 3.9 collective-permute-start.18
  376.3 1.3 collective-permute-start.19
  378.2 32.0 %attend_back_inner.1 = (bf16[1024,1152]{1,0:T(8,128)(2,1)}, f32[1024,2304]{1,0:T(8,128)}) custom-call(bf16[1408,1152]{1,0:T(8,128)(2,1)} %get-tuple-element.52.refs_0_, bf16[1024,1152]{1,0:T(8,128)(2,1)} %get-tuple-element.54.refs_1_.refs_4_, bf16[1024,1152]{1,0:T(8,128)(2,1)} %get-tuple-element.69.refs_2_, ...), custom_call_target="tpu_custom_call", output_to_operand_aliasing={{0}: (8, {})} | custom-call | flops 4840000000 | bytes 13200000 | tf_op jit(solution)/shard_map/attend_back_inner/pallas_call | solution.py:282
  410.2 11.1 %collective-permute-done.18 = bf16[192,2304]{1,0:T(8,128)(2,1)S(1)} collective-permute-done((bf16[192,2304]{1,0:T(8,128)(2,1)}, bf16[192,2304]{1,0:T(8,128)(2,1)S(1)}, u32[]{:S(2)}, u32[]{:S(2)}) %collective-permute-start.18) | collective-permute-done | bytes 884768 | tf_op jit(solution)/shard_map/ppermute | solution.py:1009
  421.3 6.6 %add_convert_fusion.2.refs_3_.refs_1_ = bf16[1024,2304]{1,0:T(8,128)(2,1)} fusion(f32[1024,2304]{1,0:T(8,128)} %get-tuple-element.77, bf16[192,2304]{1,0:T(8,128)(2,1)S(1)} %collective-permute-done.19, bf16[192,2304]{1,0:T(8,128)(2,1)S(1)} %collective-permute-done.18), kind=kLoop, calls=%fused_computation.2 | loop fusion | flops 11796480 | bytes 15925248 | tf_op jit(solution)/shard_map/convert_element_type | solution.py:1017
  427.9 24.8 %weight_grad.1 = (bf16[2,2,4,288,576]{4,3,2,1,0:T(8,128)(2,1)}, bf16[2,2,4,288,576]{4,3,2,1,0:T(8,128)(2,1)}) custom-call(s32[12]{0:T(128)} %concatenate.133.refs_0_, bf16[1408,1152]{1,0:T(8,128)(2,1)} %get-tuple-element.67.refs_1_, bf16[1024,1152]{1,0:T(8,128)(2,1)} %get-tuple-element.76.refs_2_.refs_0_, ...), custom_call_target="tpu_custom_call" | custom-call | flops 2200000000 | bytes 6000000 | tf_op jit(solution)/shard_map/weight_grad/pallas_call | solution.py:723
  455.3 7.3 %collective-permute-done.21 = bf16[2,2,4,288,576]{4,3,2,1,0:T(8,128)(2,1)S(1)} collective-permute-done((bf16[2,2,4,288,576]{4,3,2,1,0:T(8,128)(2,1)}, bf16[2,2,4,288,576]{4,3,2,1,0:T(8,128)(2,1)S(1)}, u32[]{:S(2)}, u32[]{:S(2)}) %collective-permute-start.21) | collective-permute-done | bytes 5308448 | tf_op jit(solution)/shard_map/ppermute | solution.py:864
  462.6 7.2 %fusion.1 = bf16[2,2,4,288,576]{4,3,2,1,0:T(8,128)(2,1)} fusion(bf16[2,2,4,288,576]{4,3,2,1,0:T(8,128)(2,1)S(1)} %collective-permute-done.21, bf16[2,2,4,288,576]{4,3,2,1,0:T(8,128)(2,1)} %get-tuple-element.85, pred[]{:T(512)} %bitcast.32), kind=kLoop, calls=%fused_computation.4 | loop fusion | flops 13271040 | bytes 15925249 | tf_op jit(solution)/shard_map/jit(_where)/select_n | solution.py:860
  475.0 2.1 dynamic-slice_bitcast_fusion
  477.1 2.0 collective-permute-start.32
  479.1 10.0 %collective-permute-done.20 = bf16[2,144,1152]{2,1,0:T(8,128)(2,1)S(1)} collective-permute-done((bf16[2,144,1152]{2,1,0:T(8,128)(2,1)S(1)}, bf16[2,144,1152]{2,1,0:T(8,128)(2,1)S(1)}, u32[]{:S(2)}, u32[]{:S(2)}) %collective-permute-start.20) | collective-permute-done | bytes 663584 | tf_op jit(solution)/shard_map/ppermute | solution.py:864
  490.2 23.1 %leave.1 = (f32[1024,1152]{1,0:T(8,128)}, f32[32,6912]{1,0:T(8,128)}, f32[8,2304]{1,0:T(8,128)}) custom-call(bf16[1024,1152]{1,0:T(8,128)(2,1)} %get-tuple-element.76.refs_2_.refs_0_, bf16[1024,2304]{1,0:T(8,128)(2,1)} %add_convert_fusion.2.refs_3_.refs_1_, bf16[1024,1152]{1,0:T(8,128)(2,1)} %bitcast.141, f32[1024,1152]{1,0:T(8,128)} %get-tuple-element.80.refs_3_, ...), custom_call_target="tpu_custom_call" | custom-call | flops 2750000128 | bytes 7500000 | tf_op jit(solution)/shard_map/leave/pallas_call | solution.py:775
  513.4 1.3 fusion.62
  515.9 1.4 constant_dynamic-update-slice_fusion.5
  517.3 1.3 constant_dynamic-update-slice_fusion.4
  518.6 1.3 constant_dynamic-update-slice_fusion.3
  520.0 1.4 constant_dynamic-update-slice_fusion.2
  521.3 1.3 constant_dynamic-update-slice_fusion.1
  522.6 1.3 constant_dynamic-update-slice_fusion
  525.0 3.1 collective-permute-start.23
  528.9 8.4 %collective-permute-start.34 = (bf16[1,144,1152]{2,1,0:T(8,128)(2,1)}, bf16[1,144,1152]{2,1,0:T(8,128)(2,1)}, u32[]{:S(2)}, u32[]{:S(2)}) collective-permute-start(bf16[1,144,1152]{2,1,0:T(8,128)(2,1)} %dynamic-slice_convert_fusion.2), channel_id=1, source_target_pairs={{0,4},{1,5},{2,6},{3,7},{4,0},{5,1},{6,2},{7,3},{8,12},{9,13},{10,... | collective-permute-start | bytes 995336 | tf_op jit(solution)/shard_map/ppermute | solution.py:864
  540.9 1.5 convert_add_fusion
  543.6 10.9 %collective-permute-start.33 = (bf16[1,288,576]{2,1,0:T(8,128)(2,1)S(1)}, bf16[1,288,576]{2,1,0:T(8,128)(2,1)}, u32[]{:S(2)}, u32[]{:S(2)}) collective-permute-start(bf16[1,288,576]{2,1,0:T(8,128)(2,1)S(1)} %dynamic-slice_convert_fusion), channel_id=1, source_target_pairs={{0,4},{1,5},{2,6},{3,7},{4,0},{5,1},{6,2},{7,3},{8,12},{9,13},{10,... | collective-permute-start | bytes 995336 | tf_op jit(solution)/shard_map/ppermute | solution.py:864
  555.5 1.3 slice.195
  558.3 5.6 collective-permute-start.25
  563.9 1.9 add_bitcast_fusion.2
  565.7 11.0 %collective-permute-done.25 = bf16[102,864]{1,0:T(8,128)(2,1)S(1)} collective-permute-done((bf16[102,864]{1,0:T(8,128)(2,1)S(1)}, bf16[102,864]{1,0:T(8,128)(2,1)S(1)}, u32[]{:S(2)}, u32[]{:S(2)}) %collective-permute-start.25) | collective-permute-done | bytes 176288 | tf_op jit(solution)/shard_map/ppermute | solution.py:864
  577.0 2.0 add_bitcast_fusion
  580.5 2.6 collective-permute-start.30
  583.1 2.0 fusion.23
  586.9 3.6 collective-permute-done.30
  592.5 2.2 fusion.29
  594.7 4.3 collective-permute-done.22
  606.2 1.5 collective-permute-done.27
  607.7 2.0 collective-permute-start.28
  613.6 15.5 %collective-permute-done.31 = bf16[1,288,576]{2,1,0:T(8,128)(2,1)S(1)} collective-permute-done((bf16[1,288,576]{2,1,0:T(8,128)(2,1)S(1)}, bf16[1,288,576]{2,1,0:T(8,128)(2,1)S(1)}, u32[]{:S(2)}, u32[]{:S(2)}) %collective-permute-start.31) | collective-permute-done | bytes 331808 | tf_op jit(solution)/shard_map/ppermute | solution.py:864
  (273 shorter events, 70.1 us)
Async XLA Ops:
  7.2 109.2 %all-gather.5.cloned.1.call-start = ((), (), s32[]{:S(2)}) async-start(), calls=%async_computation.3 | async-start | bytes 8957952 | tf_op jit(solution)/shard_map/all_gather | solution.py:825
  9.7 176.9 %all-gather.7.cloned.1.call-start = ((), (), s32[]{:S(2)}) async-start(), calls=%async_computation.4 | async-start | bytes 11943936 | tf_op jit(solution)/shard_map/all_gather | solution.py:825
  10.9 229.7 %all-gather.9.cloned.1.call-start = ((), (), s32[]{:S(2)}) async-start(), calls=%async_computation.5 | async-start | bytes 11943936 | tf_op jit(solution)/shard_map/all_gather | solution.py:825
  11.0 9.1 %copy-start.26 = (s32[1,1024]{1,0:T(1,128)S(1)}, s32[1,1024]{1,0:T(1,128)}, u32[]{:S(2)}) copy-start(s32[1,1024]{1,0:T(1,128)} %param.15) | copy-start | bytes 12292
  13.5 22.1 %copy-start.12 = (bf16[1,64,1152]{2,1,0:T(8,128)(2,1)S(1)}, bf16[1,64,1152]{2,1,0:T(8,128)(2,1)}, u32[]{:S(2)}) copy-start(bf16[1,64,1152]{2,1,0:T(8,128)(2,1)} %param.16) | copy-start | bytes 442372
  13.5 22.2 %copy-start.2 = (bf16[1,1024,1152]{2,1,0:T(8,128)(2,1)S(1)}, bf16[1,1024,1152]{2,1,0:T(8,128)(2,1)}, u32[]{:S(2)}) copy-start(bf16[1,1024,1152]{2,1,0:T(8,128)(2,1)} %param.14) | copy-start | bytes 7077892
  13.5 287.0 %all-gather.11.cloned.1.call-start = ((), (), s32[]{:S(2)}) async-start(), calls=%async_computation.6 | async-start | bytes 2580480 | tf_op jit(solution)/shard_map/all_gather | solution.py:980
  13.6 172.9 %collective-permute-start.13 = (bf16[1152,1152]{1,0:T(8,128)(2,1)}, bf16[1152,1152]{1,0:T(8,128)(2,1)}, u32[]{:S(2)}, u32[]{:S(2)}) collective-permute-start(bf16[1152,1152]{1,0:T(8,128)(2,1)} %refs_0_.1), channel_id=1, source_target_pairs={{0,8},{8,0},{16,24},{24,16},{1,9},{9,1},{17,25},{25,17},{2,10},{10... | collective-permute-start | bytes 7962632 | tf_op jit(solution)/shard_map/ppermute | solution.py:991
  16.6 21.2 %copy-start.30 = (bf16[2304]{0:T(1024)(128)(2,1)S(1)}, bf16[2304]{0:T(1024)(128)(2,1)}, u32[]{:S(2)}) copy-start(bf16[2304]{0:T(1024)(128)(2,1)} %param.21) | copy-start | bytes 13828
  16.6 21.7 %copy-start.35 = (bf16[1152]{0:T(1024)(128)(2,1)S(1)}, bf16[1152]{0:T(1024)(128)(2,1)}, u32[]{:S(2)}) copy-start(bf16[1152]{0:T(1024)(128)(2,1)} %param.23) | copy-start | bytes 6916
  16.6 22.3 %copy-start.29 = (bf16[4608]{0:T(1024)(128)(2,1)S(1)}, bf16[4608]{0:T(1024)(128)(2,1)}, u32[]{:S(2)}) copy-start(bf16[4608]{0:T(1024)(128)(2,1)} %param.25) | copy-start | bytes 27652
  17.6 32.5 %collective-permute-start.5 = (bf16[288,864]{1,0:T(8,128)(2,1)}, bf16[288,864]{1,0:T(8,128)(2,1)}, u32[]{:S(2)}, u32[]{:S(2)}) collective-permute-start(bf16[288,864]{1,0:T(8,128)(2,1)} %pad_maximum_fusion.2), channel_id=1, source_target_pairs={{0,16},{8,24},{16,0},{24,8},{1,17},{9,25},{17,1},{25,9},{2,18},{10... | collective-permute-start | bytes 1493000 | tf_op jit(solution)/shard_map/ppermute | solution.py:944
  21.4 28.6 %collective-permute-start.3 = (s32[193]{0:T(256)S(1)}, s32[193]{0:T(256)S(1)}, u32[]{:S(2)}, u32[]{:S(2)}) collective-permute-start(s32[193]{0:T(256)S(1)} %pad_add_fusion.3), channel_id=1, source_target_pairs={{1,0},{2,1},{3,2},{4,3},{5,4},{6,5},{7,6},{9,8},{10,9},{11,10},{12... | collective-permute-start | bytes 2324 | tf_op jit(solution)/shard_map/ppermute | solution.py:939
  22.8 21.5 %collective-permute-start.2 = (s32[193]{0:T(256)S(1)}, s32[193]{0:T(256)S(1)}, u32[]{:S(2)}, u32[]{:S(2)}) collective-permute-start(s32[193]{0:T(256)S(1)} %pad_add_fusion.4), channel_id=1, source_target_pairs={{0,1},{1,2},{2,3},{3,4},{4,5},{5,6},{6,7},{8,9},{9,10},{10,11},{11... | collective-permute-start | bytes 2324 | tf_op jit(solution)/shard_map/ppermute | solution.py:938
  27.3 13.1 %collective-permute-start.4 = (s32[]{:T(128)}, s32[]{:T(128)}, u32[]{:S(2)}, u32[]{:S(2)}) collective-permute-start(s32[]{:T(128)} %bitcast.9), channel_id=1, source_target_pairs={{0,4},{1,5},{2,6},{3,7},{4,0},{5,1},{6,2},{7,3},{8,12},{9,13},{10,... | collective-permute-start | bytes 20 | tf_op jit(solution)/shard_map/ppermute | solution.py:936
  33.4 344.8 %reduce-scatter.8.cloned.1.call-start = ((), (), s32[]{:S(2)}) async-start(), calls=%async_computation.7 | async-start | bytes 11943936 | tf_op jit(solution)/shard_map/reduce_scatter | solution.py:829
  36.7 17.8 %copy-start.33 = (s32[4]{0:T(128)}, s32[4]{0:T(128)S(1)}, u32[]{:S(2)}) copy-start(s32[4]{0:T(128)S(1)} %get-tuple-element.134) | copy-start | bytes 52
  36.8 21.1 %copy-start.31 = (s32[4]{0:T(128)}, s32[4]{0:T(128)S(1)}, u32[]{:S(2)}) copy-start(s32[4]{0:T(128)S(1)} %broadcast_multiply_fusion.refs_0_) | copy-start | bytes 52
  37.0 20.9 %copy-start.14 = (bf16[64,288]{1,0:T(8,128)(2,1)}, bf16[64,288]{1,0:T(8,128)(2,1)S(1)}, u32[]{:S(2)}) copy-start(bf16[64,288]{1,0:T(8,128)(2,1)S(1)} %get-tuple-element.167) | copy-start | bytes 110596
  40.4 22.5 %collective-permute-start.1 = (bf16[192,1152]{1,0:T(8,128)(2,1)}, bf16[192,1152]{1,0:T(8,128)(2,1)}, u32[]{:S(2)}, u32[]{:S(2)}) collective-permute-start(bf16[192,1152]{1,0:T(8,128)(2,1)} %get-tuple-element.137), channel_id=1, source_target_pairs={{1,0},{2,1},{3,2},{4,3},{5,4},{6,5},{7,6},{9,8},{10,9},{11,10},{12... | collective-permute-start | bytes 1327112 | tf_op jit(solution)/shard_map/ppermute | solution.py:941
  44.3 28.9 %collective-permute-start = (bf16[192,1152]{1,0:T(8,128)(2,1)}, bf16[192,1152]{1,0:T(8,128)(2,1)}, u32[]{:S(2)}, u32[]{:S(2)}) collective-permute-start(bf16[192,1152]{1,0:T(8,128)(2,1)} %get-tuple-element.136), channel_id=1, source_target_pairs={{0,1},{1,2},{2,3},{3,4},{4,5},{5,6},{6,7},{8,9},{9,10},{10,11},{11... | collective-permute-start | bytes 1327112 | tf_op jit(solution)/shard_map/ppermute | solution.py:940
  50.0 121.7 %collective-permute-start.10 = (bf16[288,1152]{1,0:T(8,128)(2,1)}, bf16[288,1152]{1,0:T(8,128)(2,1)}, u32[]{:S(2)}, u32[]{:S(2)}) collective-permute-start(bf16[288,1152]{1,0:T(8,128)(2,1)} %refs_10_.1), channel_id=1, source_target_pairs={{0,8},{8,0},{16,24},{24,16},{1,9},{9,1},{17,25},{25,17},{2,10},{10... | collective-permute-start | bytes 1990664 | tf_op jit(solution)/shard_map/ppermute | solution.py:975
  52.4 3.6 collective-permute-start.6
  57.9 24.9 %collective-permute-start.7 = (f32[1,64,864]{2,1,0:T(8,128)S(1)}, f32[1,64,864]{2,1,0:T(8,128)S(1)}, u32[]{:S(2)}, u32[]{:S(2)}) collective-permute-start(f32[1,64,864]{2,1,0:T(8,128)S(1)} %fusion.13), channel_id=1, source_target_pairs={{0,1},{1,0},{2,3},{3,2},{4,5},{5,4},{6,7},{7,6},{8,9},{9,8},{10,11... | collective-permute-start | bytes 663560 | tf_op jit(solution)/shard_map/ppermute | solution.py:808
  83.4 12.3 %collective-permute-start.8 = (f32[2,64,864]{2,1,0:T(8,128)S(1)}, f32[2,64,864]{2,1,0:T(8,128)S(1)}, u32[]{:S(2)}, u32[]{:S(2)}) collective-permute-start(f32[2,64,864]{2,1,0:T(8,128)S(1)} %pad_maximum_fusion.4), channel_id=1, source_target_pairs={{0,2},{1,3},{2,0},{3,1},{4,6},{5,7},{6,4},{7,5},{8,10},{9,11},{10,... | collective-permute-start | bytes 1327112 | tf_op jit(solution)/shard_map/ppermute | solution.py:808
  85.9 16.7 %collective-permute-start.11 = (bf16[288,1152]{1,0:T(8,128)(2,1)S(1)}, bf16[288,1152]{1,0:T(8,128)(2,1)S(1)}, u32[]{:S(2)}, u32[]{:S(2)}) collective-permute-start(bf16[288,1152]{1,0:T(8,128)(2,1)S(1)} %broadcast_select_fusion), channel_id=1, source_target_pairs={{0,16},{8,24},{16,0},{24,8},{1,17},{9,25},{17,1},{25,9},{2,18},{10... | collective-permute-start | bytes 1990664 | tf_op jit(solution)/shard_map/ppermute | solution.py:951
  96.0 17.3 %collective-permute-start.9 = (f32[4,24,864]{2,1,0:T(8,128)S(1)}, f32[4,24,864]{2,1,0:T(8,128)S(1)}, u32[]{:S(2)}, u32[]{:S(2)}) collective-permute-start(f32[4,24,864]{2,1,0:T(8,128)S(1)} %constant_dynamic-slice_fusion.7), channel_id=1, source_target_pairs={{0,4},{1,5},{2,6},{3,7},{4,0},{5,1},{6,2},{7,3},{8,12},{9,13},{10,... | collective-permute-start | bytes 995336 | tf_op jit(solution)/shard_map/ppermute | solution.py:956
  102.7 11.2 %copy-start.10 = (bf16[288,1152]{1,0:T(8,128)(2,1)}, bf16[288,1152]{1,0:T(8,128)(2,1)S(1)}, u32[]{:S(2)}) copy-start(bf16[288,1152]{1,0:T(8,128)(2,1)S(1)} %collective-permute-done.11.refs_9_.refs_12_) | copy-start | bytes 1990660
  102.7 69.0 %collective-permute-start.12 = (bf16[288,1152]{1,0:T(8,128)(2,1)S(1)}, bf16[288,1152]{1,0:T(8,128)(2,1)S(1)}, u32[]{:S(2)}, u32[]{:S(2)}) collective-permute-start(bf16[288,1152]{1,0:T(8,128)(2,1)S(1)} %collective-permute-done.11.refs_9_.refs_12_), channel_id=1, source_target_pairs={{0,8},{8,0},{16,24},{24,16},{1,9},{9,1},{17,25},{25,17},{2,10},{10... | collective-permute-start | bytes 1990664 | tf_op jit(solution)/shard_map/ppermute | solution.py:976
  294.2 5.8 copy-start.23
  294.2 180.8 %reduce-scatter.12.cloned.1.call-start = ((), (), s32[]{:S(2)}) async-start(), calls=%async_computation.9 | async-start | bytes 7372800
  294.2 37.9 %collective-permute-start.17 = (bf16[2,2,4,288,576]{4,3,2,1,0:T(8,128)(2,1)}, bf16[2,2,4,288,576]{4,3,2,1,0:T(8,128)(2,1)}, u32[]{:S(2)}, u32[]{:S(2)}) collective-permute-start(bf16[2,2,4,288,576]{4,3,2,1,0:T(8,128)(2,1)} %get-tuple-element.72), channel_id=1, source_target_pairs={{0,8},{8,0},{16,24},{24,16},{1,9},{9,1},{17,25},{25,17},{2,10},{10... | collective-permute-start | bytes 15925256 | tf_op jit(solution)/shard_map/ppermute | solution.py:864
  298.0 6.3 collective-permute-start.14
  298.3 6.7 %collective-permute-start.15 = (bf16[64,1152]{1,0:T(8,128)(2,1)S(1)}, bf16[64,1152]{1,0:T(8,128)(2,1)S(1)}, u32[]{:S(2)}, u32[]{:S(2)}) collective-permute-start(bf16[64,1152]{1,0:T(8,128)(2,1)S(1)} %broadcast_select_fusion.5), channel_id=1, source_target_pairs={{0,16},{8,24},{16,0},{24,8},{1,17},{9,25},{17,1},{25,9},{2,18},{10... | collective-permute-start | bytes 442376 | tf_op jit(solution)/shard_map/ppermute | solution.py:978
  298.4 8.4 %collective-permute-start.16 = (bf16[64,1152]{1,0:T(8,128)(2,1)S(1)}, bf16[64,1152]{1,0:T(8,128)(2,1)S(1)}, u32[]{:S(2)}, u32[]{:S(2)}) collective-permute-start(bf16[64,1152]{1,0:T(8,128)(2,1)S(1)} %broadcast_select_fusion.5), channel_id=1, source_target_pairs={{0,24},{8,16},{16,8},{24,0},{1,25},{9,17},{17,9},{25,1},{2,26},{10... | collective-permute-start | bytes 442376 | tf_op jit(solution)/shard_map/ppermute | solution.py:978
  341.1 214.4 %reduce-scatter.10.cloned.1.call-start = ((), (), s32[]{:S(2)}) async-start(), calls=%async_computation.8 | async-start | bytes 7372800
  341.2 36.4 %copy-start.32 = (s32[4]{0:T(128)S(1)}, s32[4]{0:T(128)}, u32[]{:S(2)}) copy-start(s32[4]{0:T(128)} %copy-done.31) | copy-start | bytes 52
  341.2 36.4 %copy-start.34 = (s32[4]{0:T(128)S(1)}, s32[4]{0:T(128)}, u32[]{:S(2)}) copy-start(s32[4]{0:T(128)} %copy-done.33) | copy-start | bytes 52
  372.4 49.0 %collective-permute-start.18 = (bf16[192,2304]{1,0:T(8,128)(2,1)}, bf16[192,2304]{1,0:T(8,128)(2,1)S(1)}, u32[]{:S(2)}, u32[]{:S(2)}) collective-permute-start(bf16[192,2304]{1,0:T(8,128)(2,1)} %get-tuple-element.78), channel_id=1, source_target_pairs={{0,1},{1,2},{2,3},{3,4},{4,5},{5,6},{6,7},{8,9},{9,10},{10,11},{11... | collective-permute-start | bytes 2654216 | tf_op jit(solution)/shard_map/ppermute | solution.py:1009
  376.3 45.0 %collective-permute-start.19 = (bf16[192,2304]{1,0:T(8,128)(2,1)}, bf16[192,2304]{1,0:T(8,128)(2,1)S(1)}, u32[]{:S(2)}, u32[]{:S(2)}) collective-permute-start(bf16[192,2304]{1,0:T(8,128)(2,1)} %get-tuple-element.79), channel_id=1, source_target_pairs={{1,0},{2,1},{3,2},{4,3},{5,4},{6,5},{7,6},{9,8},{10,9},{11,10},{12... | collective-permute-start | bytes 2654216 | tf_op jit(solution)/shard_map/ppermute | solution.py:1008
  452.7 9.9 %collective-permute-start.21 = (bf16[2,2,4,288,576]{4,3,2,1,0:T(8,128)(2,1)}, bf16[2,2,4,288,576]{4,3,2,1,0:T(8,128)(2,1)S(1)}, u32[]{:S(2)}, u32[]{:S(2)}) collective-permute-start(bf16[2,2,4,288,576]{4,3,2,1,0:T(8,128)(2,1)} %get-tuple-element.83.refs_9_), channel_id=1, source_target_pairs={{0,8},{8,0},{16,24},{24,16},{1,9},{9,1},{17,25},{25,17},{2,10},{10... | collective-permute-start | bytes 15925256 | tf_op jit(solution)/shard_map/ppermute | solution.py:864
  469.8 5.0 copy-start.28
  469.9 5.1 copy-start.27
  471.2 17.8 %collective-permute-start.20 = (bf16[2,144,1152]{2,1,0:T(8,128)(2,1)S(1)}, bf16[2,144,1152]{2,1,0:T(8,128)(2,1)S(1)}, u32[]{:S(2)}, u32[]{:S(2)}) collective-permute-start(bf16[2,144,1152]{2,1,0:T(8,128)(2,1)S(1)} %dynamic-slice_bitcast_fusion.2), channel_id=1, source_target_pairs={{0,2},{1,3},{2,0},{3,1},{4,6},{5,7},{6,4},{7,5},{8,10},{9,11},{10,... | collective-permute-start | bytes 1990664 | tf_op jit(solution)/shard_map/ppermute | solution.py:864
  477.1 63.9 %collective-permute-start.32 = (bf16[2,288,576]{2,1,0:T(8,128)(2,1)}, bf16[2,288,576]{2,1,0:T(8,128)(2,1)}, u32[]{:S(2)}, u32[]{:S(2)}) collective-permute-start(bf16[2,288,576]{2,1,0:T(8,128)(2,1)} %dynamic-slice_bitcast_fusion), channel_id=1, source_target_pairs={{0,2},{1,3},{2,0},{3,1},{4,6},{5,7},{6,4},{7,5},{8,10},{9,11},{10,... | collective-permute-start | bytes 1990664 | tf_op jit(solution)/shard_map/ppermute | solution.py:864
  513.4 14.7 %copy-start.3 = (f32[2,144,1152]{2,1,0:T(8,128)S(1)}, f32[2,144,1152]{2,1,0:T(8,128)}, u32[]{:S(2)}) copy-start(f32[2,144,1152]{2,1,0:T(8,128)} %convert_add_fusion.2.refs_10_) | copy-start | bytes 3981316
  525.0 13.8 %collective-permute-start.23 = (bf16[134,864]{1,0:T(8,128)(2,1)S(1)}, bf16[134,864]{1,0:T(8,128)(2,1)S(1)}, u32[]{:S(2)}, u32[]{:S(2)}) collective-permute-start(bf16[134,864]{1,0:T(8,128)(2,1)S(1)} %pad_maximum_fusion.8), channel_id=1, source_target_pairs={{0,1},{1,0},{2,3},{3,2},{4,5},{5,4},{6,7},{7,6},{8,9},{9,8},{10,11... | collective-permute-start | bytes 694664 | tf_op jit(solution)/shard_map/ppermute | solution.py:864
  528.9 35.0 %collective-permute-start.34 = (bf16[1,144,1152]{2,1,0:T(8,128)(2,1)}, bf16[1,144,1152]{2,1,0:T(8,128)(2,1)}, u32[]{:S(2)}, u32[]{:S(2)}) collective-permute-start(bf16[1,144,1152]{2,1,0:T(8,128)(2,1)} %dynamic-slice_convert_fusion.2), channel_id=1, source_target_pairs={{0,4},{1,5},{2,6},{3,7},{4,0},{5,1},{6,2},{7,3},{8,12},{9,13},{10,... | collective-permute-start | bytes 995336 | tf_op jit(solution)/shard_map/ppermute | solution.py:864
  540.1 15.3 %collective-permute-start.24 = (bf16[166,864]{1,0:T(8,128)(2,1)S(1)}, bf16[166,864]{1,0:T(8,128)(2,1)S(1)}, u32[]{:S(2)}, u32[]{:S(2)}) collective-permute-start(bf16[166,864]{1,0:T(8,128)(2,1)S(1)} %pad_maximum_fusion.6), channel_id=1, source_target_pairs={{0,2},{1,3},{2,0},{3,1},{4,6},{5,7},{6,4},{7,5},{8,10},{9,11},{10,... | collective-permute-start | bytes 860552 | tf_op jit(solution)/shard_map/ppermute | solution.py:864
  543.6 33.4 %collective-permute-start.33 = (bf16[1,288,576]{2,1,0:T(8,128)(2,1)S(1)}, bf16[1,288,576]{2,1,0:T(8,128)(2,1)}, u32[]{:S(2)}, u32[]{:S(2)}) collective-permute-start(bf16[1,288,576]{2,1,0:T(8,128)(2,1)S(1)} %dynamic-slice_convert_fusion), channel_id=1, source_target_pairs={{0,4},{1,5},{2,6},{3,7},{4,0},{5,1},{6,2},{7,3},{8,12},{9,13},{10,... | collective-permute-start | bytes 995336 | tf_op jit(solution)/shard_map/ppermute | solution.py:864
  555.5 21.5 %copy-start.6 = (f32[2,288,576]{2,1,0:T(8,128)S(1)}, f32[2,288,576]{2,1,0:T(8,128)}, u32[]{:S(2)}) copy-start(f32[2,288,576]{2,1,0:T(8,128)} %copy-done.5) | copy-start | bytes 3981316
  558.2 20.8 %copy-start.9 = (bf16[1,4,288,576]{3,2,1,0:T(8,128)(2,1)S(1)}, bf16[1,4,288,576]{3,2,1,0:T(8,128)(2,1)}, u32[]{:S(2)}) copy-start(bf16[1,4,288,576]{3,2,1,0:T(8,128)(2,1)} %reduce-scatter.10.cloned.1.call-done) | copy-start | bytes 3981316
  558.3 18.5 %collective-permute-start.25 = (bf16[102,864]{1,0:T(8,128)(2,1)S(1)}, bf16[102,864]{1,0:T(8,128)(2,1)S(1)}, u32[]{:S(2)}, u32[]{:S(2)}) collective-permute-start(bf16[102,864]{1,0:T(8,128)(2,1)S(1)} %pad_maximum_fusion.11), channel_id=1, source_target_pairs={{0,4},{1,5},{2,6},{3,7},{4,0},{5,1},{6,2},{7,3},{8,12},{9,13},{10,... | collective-permute-start | bytes 528776 | tf_op jit(solution)/shard_map/ppermute | solution.py:864
  576.9 6.2 copy-start.8
  576.9 3.4 collective-permute-start.29
  580.0 19.0 %collective-permute-start.22 = (bf16[2,288,576]{2,1,0:T(8,128)(2,1)}, bf16[2,288,576]{2,1,0:T(8,128)(2,1)S(1)}, u32[]{:S(2)}, u32[]{:S(2)}) collective-permute-start(bf16[2,288,576]{2,1,0:T(8,128)(2,1)} %dynamic-slice_bitcast_fusion.1), channel_id=1, source_target_pairs={{0,2},{1,3},{2,0},{3,1},{4,6},{5,7},{6,4},{7,5},{8,10},{9,11},{10,... | collective-permute-start | bytes 1990664 | tf_op jit(solution)/shard_map/ppermute | solution.py:864
  580.5 10.0 %collective-permute-start.30 = (bf16[166,864]{1,0:T(8,128)(2,1)S(1)}, bf16[166,864]{1,0:T(8,128)(2,1)S(1)}, u32[]{:S(2)}, u32[]{:S(2)}) collective-permute-start(bf16[166,864]{1,0:T(8,128)(2,1)S(1)} %pad_maximum_fusion.7), channel_id=1, source_target_pairs={{0,16},{8,24},{16,0},{24,8},{1,17},{9,25},{17,1},{25,9},{2,18},{10... | collective-permute-start | bytes 860552 | tf_op jit(solution)/shard_map/ppermute | solution.py:864
  585.1 5.4 copy-start.17
  585.9 17.3 %collective-permute-start.26 = (f32[4,8,1152]{2,1,0:T(8,128)}, f32[4,8,1152]{2,1,0:T(8,128)S(1)}, u32[]{:S(2)}, u32[]{:S(2)}) collective-permute-start(f32[4,8,1152]{2,1,0:T(8,128)} %dynamic-slice_bitcast_fusion.3), channel_id=1, source_target_pairs={{0,1},{1,0},{2,3},{3,2},{4,5},{5,4},{6,7},{7,6},{8,9},{9,8},{10,11... | collective-permute-start | bytes 442376 | tf_op jit(solution)/shard_map/ppermute | solution.py:864
  592.4 10.8 %copy-start.18 = (f32[64,1152]{1,0:T(8,128)S(1)}, f32[64,1152]{1,0:T(8,128)}, u32[]{:S(2)}) copy-start(f32[64,1152]{1,0:T(8,128)} %copy-done.17) | copy-start | bytes 884740
  603.2 4.4 collective-permute-start.27
  605.5 26.7 %copy-start.1 = (bf16[288,4608]{1,0:T(8,128)(2,1)S(1)}, bf16[288,4608]{1,0:T(8,128)(2,1)}, u32[]{:S(2)}) copy-start(bf16[288,4608]{1,0:T(8,128)(2,1)} %param.24) | copy-start | bytes 7962628
  607.7 5.3 collective-permute-start.28
  610.9 18.3 %collective-permute-start.31 = (bf16[1,288,576]{2,1,0:T(8,128)(2,1)S(1)}, bf16[1,288,576]{2,1,0:T(8,128)(2,1)S(1)}, u32[]{:S(2)}, u32[]{:S(2)}) collective-permute-start(bf16[1,288,576]{2,1,0:T(8,128)(2,1)S(1)} %dynamic-slice_convert_fusion.1), channel_id=1, source_target_pairs={{0,4},{1,5},{2,6},{3,7},{4,0},{5,1},{6,2},{7,3},{8,12},{9,13},{10,... | collective-permute-start | bytes 995336 | tf_op jit(solution)/shard_map/ppermute | solution.py:864
  (15 other events, 34.1 us)
Sparse Core Ops, SparseCore 0:
  10.5 79.3 all-gather.4
  91.8 63.5 all-gather.6
  157.3 63.7 all-gather.8
  222.5 22.3 all-gather.10
  294.3 83.5 reduce-scatter.7
  380.7 91.5 reduce-scatter.11
  475.3 74.7 reduce-scatter.9

commit v4 on v3

--- a/solution.py
+++ b/solution.py
@@ -1019,12 +1019,12 @@
     total_contract = contract_stages[-1][0]
     total_expand = along_rest(expand_rest)[-1][0]
     input_keep, input_send = weight_grad(
-        chunks, seq_count, input_attn, grad_query, grad_pair, attn_mixed, grad_attn, ()
+        chunks, seq_count, input_attn, grad_query, grad_pair, attn_mixed, grad_attn, (contract_stages[0],)
     )
     input_rest = scattered_core(input_keep, input_send, input_keep)[1]
     grad_rows, all_images, packed_sums = leave(
         input_full, grad_query, grad_pair, token_rows, grad_middle, select, gather, mixer_parts, feed_images,
-        (input_send, contract_stages[0]),
+        (input_send,),
     )
     input_stages = along_rest(input_rest)
     input_total = input_stages[-1][0]
@@ -1040,7 +1040,10 @@
         jnp.sum(feed_sums, axis=0),
     ]
     ends = [sum(part.shape[0] for part in sums[: index + 1]) for index in range(5)]
-    biases = jnp.concatenate(sums + [jnp.zeros((-ends[-1] % columns,), F32)]).reshape(-1, columns)
+    whole_length = -(-ends[-1] // columns) * columns
+    biases = sum(
+        jnp.pad(part, (end - part.shape[0], whole_length - end)) for part, end in zip(sums, ends)
+    ).reshape(-1, columns)
     bias_rows = biases.shape[0]
 
     def joined(value, axis, bit):
@@ -1058,13 +1061,11 @@
     column_grads = lax.dynamic_update_slice_in_dim(empty, mine.swapaxes(0, 1), first_image, 1)
     column_grads += lax.dynamic_update_slice_in_dim(empty, got, first_of_next, 1)
     for bit in seq_bits[1:]:
-        if bit == top:
-            column_grads = gate(column_grads, input_rest)
         pairs = column_grads.reshape(-1, 2, images, columns)
         mine = (place_in_seq // bit) % 2
         got, biases = joined(lax.dynamic_index_in_dim(pairs, 1 - mine, 1, keepdims=False), "seq", bit)
         column_grads = lax.dynamic_index_in_dim(pairs, mine, 1, keepdims=False) + got
-    column_grads = column_grads[0]
+    column_grads = gate(column_grads[0], input_rest)
     all_grads = column_grads[None].astype(BF)
     for bit in dp_bits:
         other, biases = joined(all_grads, "dp", bit)

time: 646 us -> 633 us (0.980)
  local copies, waits for them, and re-layouts: 62 us -> 50.2 us
    unnamed x81 -> x80, local copies, waits for them, and re-layouts: 13.6 us -> 3.87 us
    select_n x7 -> x6, other arithmetic: 17.7 us -> 17.5 us  [gate(): return jnp.where(first == first, value, jnp.zeros_like(value))]
  transfers between devices with their start and end apart: 42 -> 42, of which waited for: 20 -> 18; matrix products, arithmetic and copies ran while one was open for 17% -> 16% of each run, Pallas kernels for 48% -> 49%
where the time goes in v4:
time: 633 us; the launch traced here: 627 us
  Pallas kernels  310 us (49%)
  waiting for transfers between devices  109 us (17%)
  starting transfers between devices  70 us (11%)
  other arithmetic  51.9 us (8%)
  local copies, waits for them, and re-layouts  50.2 us (8%)
  between operations  30.5 us (5%)
    pallas_call x2, Pallas kernels, feed(): pl.pallas_call(functools.partial(feed_kernel, bool(before)), grid_spec=pl...  108 us
    pallas_call x2, Pallas kernels, backward(): pl.pallas_call(skipping(functools.partial(backward_kernel, edge), 7 + len...  62.7 us
    ppermute x16, waiting for transfers between devices, swapped(): return lax.ppermute(value.astype(kind), axis, partners(axis, bit))  56.9 us
    ppermute x16, starting transfers between devices, swapped(): return lax.ppermute(value.astype(kind), axis, partners(axis, bit))  39.5 us
    pallas_call x1, Pallas kernels, forward(): pl.pallas_call(skipping(forward_kernel, 4, len(after)), grid=(count,), in...  33.5 us
    pallas_call x1, Pallas kernels, weight_grad(): pl.pallas_call(skipping(weight_grad_kernel, 6, len(after)), grid_spec=plt...  25.1 us
    pallas_call x1, Pallas kernels, leave(): pl.pallas_call(skipping(leave_kernel, 9, len(after)), grid=(BANDS,), in_s...  22.8 us
    pallas_call x1, Pallas kernels, leave_feed(): pl.pallas_call(skipping(functools.partial(leave_feed_kernel, len(pieces))...  22.1 us
  transfers between devices with their start and end apart: 42, of which 18 were waited for; matrix products, arithmetic and copies ran while one was open for 16% of the time, Pallas kernels for 49%

profile of v4, /device:TPU:0, one launch (start us, length us, event | category | flops | bytes accessed | tf_op | source)
XLA Modules:
  0.0 626.7 jit_solution(10128084857700343118)
XLA Ops:
  7.3 2.4 constant_dynamic-slice_fusion.6
  11.0 2.5 constant_dynamic-slice_fusion.4
  14.1 1.3 constant_dynamic-slice_fusion.9
  17.6 2.5 collective-permute-start.5
  21.4 1.3 collective-permute-start.3
  22.8 4.5 collective-permute-start.2
  27.3 4.0 collective-permute-start.4
  31.3 2.1 constant_dynamic-slice_fusion.3
  40.4 1.3 collective-permute-start.1
  44.2 5.7 collective-permute-start
  50.0 2.4 pad_maximum_fusion.1
  54.5 1.5 collective-permute-done.6
  56.0 1.9 fusion.13
  57.9 1.8 collective-permute-start.7
  65.4 7.8 %collective-permute-done = bf16[192,1152]{1,0:T(8,128)(2,1)} collective-permute-done((bf16[192,1152]{1,0:T(8,128)(2,1)}, bf16[192,1152]{1,0:T(8,128)(2,1)}, u32[]{:S(2)}, u32[]{:S(2)}) %collective-permute-start) | collective-permute-done | bytes 442400 | tf_op jit(solution)/shard_map/ppermute | solution.py:940
  75.7 7.2 %collective-permute-done.7 = f32[1,64,864]{2,1,0:T(8,128)S(1)} collective-permute-done((f32[1,64,864]{2,1,0:T(8,128)S(1)}, f32[1,64,864]{2,1,0:T(8,128)S(1)}, u32[]{:S(2)}, u32[]{:S(2)}) %collective-permute-start.7) | collective-permute-done | bytes 221216 | tf_op jit(solution)/shard_map/ppermute | solution.py:808
  86.5 9.2 %collective-permute-done.8 = f32[2,64,864]{2,1,0:T(8,128)S(1)} collective-permute-done((f32[2,64,864]{2,1,0:T(8,128)S(1)}, f32[2,64,864]{2,1,0:T(8,128)S(1)}, u32[]{:S(2)}, u32[]{:S(2)}) %collective-permute-start.8) | collective-permute-done | bytes 442400 | tf_op jit(solution)/shard_map/ppermute | solution.py:808
  96.4 4.7 pad_maximum_fusion.tokens_ref
  101.1 1.5 collective-permute-done.11.refs_9_.refs_12_
  102.7 10.6 %collective-permute-done.9 = f32[4,24,864]{2,1,0:T(8,128)S(1)} collective-permute-done((f32[4,24,864]{2,1,0:T(8,128)S(1)}, f32[4,24,864]{2,1,0:T(8,128)S(1)}, u32[]{:S(2)}, u32[]{:S(2)}) %collective-permute-start.9) | collective-permute-done | bytes 331808 | tf_op jit(solution)/shard_map/ppermute | solution.py:956
  114.2 1.2 maximum_maximum_fusion.refs_5_.refs_8_
  116.4 21.8 %project.1 = (bf16[1408,1152]{1,0:T(8,128)(2,1)}, bf16[1408,1152]{1,0:T(8,128)(2,1)}, bf16[1408,2304]{1,0:T(8,128)(2,1)}) custom-call(bf16[1408,1152]{1,0:T(8,128)(2,1)} %pad_maximum_fusion.tokens_ref, bf16[1408,128]{1,0:T(8,128)(2,1)} %add_convert_fusion.3.select_ref.refs_4_.refs_6_, bf16[128,2304]{1,0:T(8,128)(2,1)} %maximum_maximum_fusion.1.parts_ref.refs_6_, ...), custom_call_target="tpu_custom_call" | custom-call | flops 27499999232 | bytes 75000000 | tf_op jit(solution)/shard_map/project/pallas_call | solution.py:408
  138.2 33.5 %attend.1 = (bf16[1024,1152]{1,0:T(8,128)(2,1)}, f32[16,1024]{1,0:T(8,128)}) custom-call(bf16[1408,1152]{1,0:T(8,128)(2,1)} %get-tuple-element.52.refs_0_, bf16[1408,2304]{1,0:T(8,128)(2,1)} %get-tuple-element.53.refs_1_.refs_4_, s32[4,1,640]{2,1,0:T(1,128)} %broadcast_in_dim.61.refs_2_.refs_5_, s32[4,1,256]{2,1,0:T(1,128)} %bitcast.173), custom_call_target="tpu_custom_call" | custom-call | flops 50600001536 | bytes 138000000 | tf_op jit(solution)/shard_map/attend/pallas_call | solution.py:242
  172.5 14.0 %enter_feed.1 = (f32[1024,1152]{1,0:T(8,128)}, f32[1024,1152]{1,0:T(8,128)}, bf16[1024,1152]{1,0:T(8,128)(2,1)}, bf16[1024,1152]{1,0:T(8,128)(2,1)}) custom-call(s32[4]{0:T(128)} %copy-done.33, bf16[1024,1152]{1,0:T(8,128)(2,1)} %get-tuple-element.54.refs_1_.refs_4_, bf16[1024,1152]{1,0:T(8,128)(2,1)} %bitcast.142, bf16[1024,1152]{1,0:T(8,128)(2,1)} %bitcast.151, ...), custom_call_target="tpu_custom_call" | custom-call | flops 15399999488 | bytes 42000000 | tf_op jit(solution)/shard_map/enter_feed/pallas_call | solution.py:455
  186.5 54.0 %feed.1 = (f32[1024,1152]{1,0:T(8,128)}, f32[1024,1152]{1,0:T(8,128)}, bf16[2,2,4,288,576]{4,3,2,1,0:T(8,128)(2,1)}, bf16[2,2,4,288,576]{4,3,2,1,0:T(8,128)(2,1)...) custom-call(s32[10]{0:T(128)} %get-tuple-element.178.place_ref, ...), custom_call_target="tpu_custom_call" | custom-call | flops 51699998720 | bytes 141000000 | tf_op jit(solution)/shard_map/feed/pallas_call | solution.py:568
  240.6 53.5 %feed_later.1 = (f32[1024,1152]{1,0:T(8,128)}, f32[1024,1152]{1,0:T(8,128)}, bf16[2,2,4,288,576]{4,3,2,1,0:T(8,128)(2,1)}, bf16[2,2,4,288,576]{4,3,2,1,0:T(8,128...) custom-call(s32[10]{0:T(128)} %get-tuple-element.179.place_ref, ...), custom_call_target="tpu_custom_call", output_to_operand_aliasing={{2}: (8, {}), {3}: (9, {}), {4}: (10, {}), {5}: (11, {})} | custom-call | flops 51699998720 | bytes 141000000 | tf_op jit(solution)/shard_map/feed_later/pallas_call | solution.py:568
  298.4 1.5 collective-permute-start.16
  300.5 3.8 collective-permute-done.14.refs_14_
  305.0 1.8 collective-permute-done.16.refs_16_
  307.4 22.1 %leave_feed.1 = (bf16[1024,1152]{1,0:T(8,128)(2,1)}, f32[1024,1152]{1,0:T(8,128)}, bf16[1024,1152]{1,0:T(8,128)(2,1)}, bf16[1024,1152]{1,0:T(8,128)(2,1)}, f32[32,4608]{1,0:T(8,128)}, /*index=5*/f32[8,1152]{1,0:T(8,128)}) custom-call(s32[4]{0:T(128)} %copy-done.33, f32[1024,1152]{1,0:T(8,128)} %get-tuple-element.63.refs_1_, ...), custom_call_target="tpu_custom_call" | custom-call | flops 2420000000 | bytes 6600000 | tf_op jit(solution)/shard_map/leave_feed/pallas_call | solution.py:659
  332.0 9.0 %fusion.refs_7_ = bf16[2,2,4,288,576]{4,3,2,1,0:T(8,128)(2,1)} fusion(bf16[2,2,4,288,576]{4,3,2,1,0:T(8,128)(2,1)} %collective-permute-done.17, bf16[2,2,4,288,576]{4,3,2,1,0:T(8,128)(2,1)} %get-tuple-element.71, pred[]{:T(512)} %bitcast.25), kind=kLoop, calls=%fused_computation.3 | loop fusion | flops 13271040 | bytes 15925249 | tf_op jit(solution)/shard_map/jit(_where)/select_n | solution.py:860
  341.1 31.2 %attend_back_edge.1 = (bf16[1024,1152]{1,0:T(8,128)(2,1)}, bf16[192,2304]{1,0:T(8,128)(2,1)}, bf16[192,2304]{1,0:T(8,128)(2,1)}, f32[2,448,2304]{2,1,0:T(8,128)}) custom-call(bf16[1408,1152]{1,0:T(8,128)(2,1)} %get-tuple-element.52.refs_0_, bf16[1024,1152]{1,0:T(8,128)(2,1)} %get-tuple-element.54.refs_1_.refs_4_, ...), custom_call_target="tpu_custom_call" | custom-call | flops 4840000000 | bytes 13200000 | tf_op jit(solution)/shard_map/attend_back_edge/pallas_call | solution.py:282
  372.2 3.9 collective-permute-start.18
  376.2 1.3 collective-permute-start.19
  378.1 2.0 dynamic-slice_bitcast_fusion.2
  380.1 2.0 collective-permute-start.20
  382.1 31.6 %attend_back_inner.1 = (bf16[1024,1152]{1,0:T(8,128)(2,1)}, f32[1024,2304]{1,0:T(8,128)}) custom-call(bf16[1408,1152]{1,0:T(8,128)(2,1)} %get-tuple-element.52.refs_0_, bf16[1024,1152]{1,0:T(8,128)(2,1)} %get-tuple-element.54.refs_1_.refs_4_, bf16[1024,1152]{1,0:T(8,128)(2,1)} %get-tuple-element.69.refs_2_, ...), custom_call_target="tpu_custom_call", output_to_operand_aliasing={{0}: (8, {})} | custom-call | flops 4840000000 | bytes 13200000 | tf_op jit(solution)/shard_map/attend_back_inner/pallas_call | solution.py:282
  413.7 7.4 %collective-permute-done.18 = bf16[192,2304]{1,0:T(8,128)(2,1)S(1)} collective-permute-done((bf16[192,2304]{1,0:T(8,128)(2,1)}, bf16[192,2304]{1,0:T(8,128)(2,1)S(1)}, u32[]{:S(2)}, u32[]{:S(2)}) %collective-permute-start.18) | collective-permute-done | bytes 884768 | tf_op jit(solution)/shard_map/ppermute | solution.py:1009
  421.1 6.5 %add_convert_fusion.2.refs_3_.refs_1_ = bf16[1024,2304]{1,0:T(8,128)(2,1)} fusion(f32[1024,2304]{1,0:T(8,128)} %get-tuple-element.77, bf16[192,2304]{1,0:T(8,128)(2,1)S(1)} %collective-permute-done.19, bf16[192,2304]{1,0:T(8,128)(2,1)S(1)} %collective-permute-done.18), kind=kLoop, calls=%fused_computation.2 | loop fusion | flops 11796480 | bytes 15925248 | tf_op jit(solution)/shard_map/convert_element_type | solution.py:1017
  427.6 2.3 convert_add_fusion.2.refs_6_
  429.9 25.1 %weight_grad.1 = (bf16[2,2,4,288,576]{4,3,2,1,0:T(8,128)(2,1)}, bf16[2,2,4,288,576]{4,3,2,1,0:T(8,128)(2,1)}) custom-call(s32[12]{0:T(128)} %concatenate.130.refs_0_, bf16[1408,1152]{1,0:T(8,128)(2,1)} %get-tuple-element.67.refs_1_, bf16[1024,1152]{1,0:T(8,128)(2,1)} %get-tuple-element.76.refs_2_.refs_0_, ...), custom_call_target="tpu_custom_call" | custom-call | flops 2200000000 | bytes 6000000 | tf_op jit(solution)/shard_map/weight_grad/pallas_call | solution.py:723
  457.6 7.3 %collective-permute-done.21 = bf16[2,2,4,288,576]{4,3,2,1,0:T(8,128)(2,1)S(1)} collective-permute-done((bf16[2,2,4,288,576]{4,3,2,1,0:T(8,128)(2,1)}, bf16[2,2,4,288,576]{4,3,2,1,0:T(8,128)(2,1)S(1)}, u32[]{:S(2)}, u32[]{:S(2)}) %collective-permute-start.21) | collective-permute-done | bytes 5308448 | tf_op jit(solution)/shard_map/ppermute | solution.py:864
  464.9 7.1 %fusion.1 = bf16[2,2,4,288,576]{4,3,2,1,0:T(8,128)(2,1)} fusion(bf16[2,2,4,288,576]{4,3,2,1,0:T(8,128)(2,1)S(1)} %collective-permute-done.21, bf16[2,2,4,288,576]{4,3,2,1,0:T(8,128)(2,1)} %get-tuple-element.85, pred[]{:T(512)} %bitcast.32), kind=kLoop, calls=%fused_computation.4 | loop fusion | flops 13271040 | bytes 15925249 | tf_op jit(solution)/shard_map/jit(_where)/select_n | solution.py:860
  475.8 2.1 dynamic-slice_bitcast_fusion
  477.9 22.8 %leave.1 = (f32[1024,1152]{1,0:T(8,128)}, f32[32,6912]{1,0:T(8,128)}, f32[8,2304]{1,0:T(8,128)}) custom-call(bf16[1024,1152]{1,0:T(8,128)(2,1)} %get-tuple-element.76.refs_2_.refs_0_, bf16[1024,2304]{1,0:T(8,128)(2,1)} %add_convert_fusion.2.refs_3_.refs_1_, bf16[1024,1152]{1,0:T(8,128)(2,1)} %bitcast.143, f32[1024,1152]{1,0:T(8,128)} %get-tuple-element.80.refs_3_, ...), custom_call_target="tpu_custom_call" | custom-call | flops 2750000128 | bytes 7500000 | tf_op jit(solution)/shard_map/leave/pallas_call | solution.py:775
  500.7 1.3 fusion.68
  503.4 3.2 collective-permute-start.23
  507.4 13.5 %collective-permute-start.34 = (bf16[1,144,1152]{2,1,0:T(8,128)(2,1)}, bf16[1,144,1152]{2,1,0:T(8,128)(2,1)}, u32[]{:S(2)}, u32[]{:S(2)}) collective-permute-start(bf16[1,144,1152]{2,1,0:T(8,128)(2,1)} %dynamic-slice_convert_fusion.2), channel_id=1, source_target_pairs={{0,4},{1,5},{2,6},{3,7},{4,0},{5,1},{6,2},{7,3},{8,12},{9,13},{10,... | collective-permute-start | bytes 995336 | tf_op jit(solution)/shard_map/ppermute | solution.py:864
  524.3 1.5 convert_add_fusion
  525.9 11.2 %collective-permute-start.33 = (bf16[1,288,576]{2,1,0:T(8,128)(2,1)S(1)}, bf16[1,288,576]{2,1,0:T(8,128)(2,1)}, u32[]{:S(2)}, u32[]{:S(2)}) collective-permute-start(bf16[1,288,576]{2,1,0:T(8,128)(2,1)S(1)} %dynamic-slice_convert_fusion), channel_id=1, source_target_pairs={{0,4},{1,5},{2,6},{3,7},{4,0},{5,1},{6,2},{7,3},{8,12},{9,13},{10,... | collective-permute-start | bytes 995336 | tf_op jit(solution)/shard_map/ppermute | solution.py:864
  537.2 7.3 %collective-permute-done.24 = bf16[166,864]{1,0:T(8,128)(2,1)S(1)} collective-permute-done((bf16[166,864]{1,0:T(8,128)(2,1)S(1)}, bf16[166,864]{1,0:T(8,128)(2,1)S(1)}, u32[]{:S(2)}, u32[]{:S(2)}) %collective-permute-start.24) | collective-permute-done | bytes 286880 | tf_op jit(solution)/shard_map/ppermute | solution.py:864
  545.0 1.9 add_bitcast_fusion.2
  546.9 13.9 %collective-permute-done.25 = bf16[102,864]{1,0:T(8,128)(2,1)S(1)} collective-permute-done((bf16[102,864]{1,0:T(8,128)(2,1)S(1)}, bf16[102,864]{1,0:T(8,128)(2,1)S(1)}, u32[]{:S(2)}, u32[]{:S(2)}) %collective-permute-start.25) | collective-permute-done | bytes 176288 | tf_op jit(solution)/shard_map/ppermute | solution.py:864
  560.8 1.2 slice.195
  563.6 2.3 add_bitcast_fusion
  567.6 2.4 collective-permute-start.30
  570.0 2.0 fusion.22
  573.1 4.5 collective-permute-done.30
  578.0 2.1 fusion.29
  580.1 5.8 collective-permute-done.22
  585.9 1.5 convert_add_fusion.1
  593.6 1.2 collective-permute-done.27
  594.9 2.3 collective-permute-start.28
  600.4 16.2 %collective-permute-done.31 = bf16[1,288,576]{2,1,0:T(8,128)(2,1)S(1)} collective-permute-done((bf16[1,288,576]{2,1,0:T(8,128)(2,1)S(1)}, bf16[1,288,576]{2,1,0:T(8,128)(2,1)S(1)}, u32[]{:S(2)}, u32[]{:S(2)}) %collective-permute-start.31) | collective-permute-done | bytes 331808 | tf_op jit(solution)/shard_map/ppermute | solution.py:864
  (271 shorter events, 56.2 us)
Async XLA Ops:
  7.2 109.2 %all-gather.5.cloned.1.call-start = ((), (), s32[]{:S(2)}) async-start(), calls=%async_computation.3 | async-start | bytes 8957952 | tf_op jit(solution)/shard_map/all_gather | solution.py:825
  9.7 176.9 %all-gather.7.cloned.1.call-start = ((), (), s32[]{:S(2)}) async-start(), calls=%async_computation.4 | async-start | bytes 11943936 | tf_op jit(solution)/shard_map/all_gather | solution.py:825
  10.9 229.7 %all-gather.9.cloned.1.call-start = ((), (), s32[]{:S(2)}) async-start(), calls=%async_computation.5 | async-start | bytes 11943936 | tf_op jit(solution)/shard_map/all_gather | solution.py:825
  11.0 9.1 %copy-start.28 = (s32[1,1024]{1,0:T(1,128)S(1)}, s32[1,1024]{1,0:T(1,128)}, u32[]{:S(2)}) copy-start(s32[1,1024]{1,0:T(1,128)} %param.15) | copy-start | bytes 12292
  13.5 22.1 %copy-start.11 = (bf16[1,64,1152]{2,1,0:T(8,128)(2,1)S(1)}, bf16[1,64,1152]{2,1,0:T(8,128)(2,1)}, u32[]{:S(2)}) copy-start(bf16[1,64,1152]{2,1,0:T(8,128)(2,1)} %param.16) | copy-start | bytes 442372
  13.5 22.2 %copy-start.2 = (bf16[1,1024,1152]{2,1,0:T(8,128)(2,1)S(1)}, bf16[1,1024,1152]{2,1,0:T(8,128)(2,1)}, u32[]{:S(2)}) copy-start(bf16[1,1024,1152]{2,1,0:T(8,128)(2,1)} %param.14) | copy-start | bytes 7077892
  13.5 287.0 %all-gather.11.cloned.1.call-start = ((), (), s32[]{:S(2)}) async-start(), calls=%async_computation.6 | async-start | bytes 2580480 | tf_op jit(solution)/shard_map/all_gather | solution.py:980
  13.6 172.9 %collective-permute-start.13 = (bf16[1152,1152]{1,0:T(8,128)(2,1)}, bf16[1152,1152]{1,0:T(8,128)(2,1)}, u32[]{:S(2)}, u32[]{:S(2)}) collective-permute-start(bf16[1152,1152]{1,0:T(8,128)(2,1)} %refs_0_.1), channel_id=1, source_target_pairs={{0,8},{8,0},{16,24},{24,16},{1,9},{9,1},{17,25},{25,17},{2,10},{10... | collective-permute-start | bytes 7962632 | tf_op jit(solution)/shard_map/ppermute | solution.py:991
  16.6 21.2 %copy-start.32 = (bf16[2304]{0:T(1024)(128)(2,1)S(1)}, bf16[2304]{0:T(1024)(128)(2,1)}, u32[]{:S(2)}) copy-start(bf16[2304]{0:T(1024)(128)(2,1)} %param.21) | copy-start | bytes 13828
  16.6 21.8 %copy-start.37 = (bf16[1152]{0:T(1024)(128)(2,1)S(1)}, bf16[1152]{0:T(1024)(128)(2,1)}, u32[]{:S(2)}) copy-start(bf16[1152]{0:T(1024)(128)(2,1)} %param.23) | copy-start | bytes 6916
  16.6 22.3 %copy-start.31 = (bf16[4608]{0:T(1024)(128)(2,1)S(1)}, bf16[4608]{0:T(1024)(128)(2,1)}, u32[]{:S(2)}) copy-start(bf16[4608]{0:T(1024)(128)(2,1)} %param.25) | copy-start | bytes 27652
  17.6 32.4 %collective-permute-start.5 = (bf16[288,864]{1,0:T(8,128)(2,1)}, bf16[288,864]{1,0:T(8,128)(2,1)}, u32[]{:S(2)}, u32[]{:S(2)}) collective-permute-start(bf16[288,864]{1,0:T(8,128)(2,1)} %pad_maximum_fusion.2), channel_id=1, source_target_pairs={{0,16},{8,24},{16,0},{24,8},{1,17},{9,25},{17,1},{25,9},{2,18},{10... | collective-permute-start | bytes 1493000 | tf_op jit(solution)/shard_map/ppermute | solution.py:944
  21.4 28.5 %collective-permute-start.3 = (s32[193]{0:T(256)S(1)}, s32[193]{0:T(256)S(1)}, u32[]{:S(2)}, u32[]{:S(2)}) collective-permute-start(s32[193]{0:T(256)S(1)} %pad_add_fusion.4), channel_id=1, source_target_pairs={{1,0},{2,1},{3,2},{4,3},{5,4},{6,5},{7,6},{9,8},{10,9},{11,10},{12... | collective-permute-start | bytes 2324 | tf_op jit(solution)/shard_map/ppermute | solution.py:939
  22.8 21.4 %collective-permute-start.2 = (s32[193]{0:T(256)S(1)}, s32[193]{0:T(256)S(1)}, u32[]{:S(2)}, u32[]{:S(2)}) collective-permute-start(s32[193]{0:T(256)S(1)} %pad_add_fusion.5), channel_id=1, source_target_pairs={{0,1},{1,2},{2,3},{3,4},{4,5},{5,6},{6,7},{8,9},{9,10},{10,11},{11... | collective-permute-start | bytes 2324 | tf_op jit(solution)/shard_map/ppermute | solution.py:938
  27.3 13.1 %collective-permute-start.4 = (s32[]{:T(128)}, s32[]{:T(128)}, u32[]{:S(2)}, u32[]{:S(2)}) collective-permute-start(s32[]{:T(128)} %bitcast.9), channel_id=1, source_target_pairs={{0,4},{1,5},{2,6},{3,7},{4,0},{5,1},{6,2},{7,3},{8,12},{9,13},{10,... | collective-permute-start | bytes 20 | tf_op jit(solution)/shard_map/ppermute | solution.py:936
  33.4 344.7 %reduce-scatter.8.cloned.1.call-start = ((), (), s32[]{:S(2)}) async-start(), calls=%async_computation.7 | async-start | bytes 11943936 | tf_op jit(solution)/shard_map/reduce_scatter | solution.py:829
  36.8 17.7 %copy-start.35 = (s32[4]{0:T(128)}, s32[4]{0:T(128)S(1)}, u32[]{:S(2)}) copy-start(s32[4]{0:T(128)S(1)} %get-tuple-element.134) | copy-start | bytes 52
  36.8 21.1 %copy-start.33 = (s32[4]{0:T(128)}, s32[4]{0:T(128)S(1)}, u32[]{:S(2)}) copy-start(s32[4]{0:T(128)S(1)} %broadcast_multiply_fusion.refs_0_) | copy-start | bytes 52
  37.0 20.9 %copy-start.14 = (bf16[64,288]{1,0:T(8,128)(2,1)}, bf16[64,288]{1,0:T(8,128)(2,1)S(1)}, u32[]{:S(2)}) copy-start(bf16[64,288]{1,0:T(8,128)(2,1)S(1)} %get-tuple-element.167) | copy-start | bytes 110596
  40.4 22.5 %collective-permute-start.1 = (bf16[192,1152]{1,0:T(8,128)(2,1)}, bf16[192,1152]{1,0:T(8,128)(2,1)}, u32[]{:S(2)}, u32[]{:S(2)}) collective-permute-start(bf16[192,1152]{1,0:T(8,128)(2,1)} %get-tuple-element.137), channel_id=1, source_target_pairs={{1,0},{2,1},{3,2},{4,3},{5,4},{6,5},{7,6},{9,8},{10,9},{11,10},{12... | collective-permute-start | bytes 1327112 | tf_op jit(solution)/shard_map/ppermute | solution.py:941
  44.2 29.0 %collective-permute-start = (bf16[192,1152]{1,0:T(8,128)(2,1)}, bf16[192,1152]{1,0:T(8,128)(2,1)}, u32[]{:S(2)}, u32[]{:S(2)}) collective-permute-start(bf16[192,1152]{1,0:T(8,128)(2,1)} %get-tuple-element.136), channel_id=1, source_target_pairs={{0,1},{1,2},{2,3},{3,4},{4,5},{5,6},{6,7},{8,9},{9,10},{10,11},{11... | collective-permute-start | bytes 1327112 | tf_op jit(solution)/shard_map/ppermute | solution.py:940
  49.9 121.8 %collective-permute-start.10 = (bf16[288,1152]{1,0:T(8,128)(2,1)}, bf16[288,1152]{1,0:T(8,128)(2,1)}, u32[]{:S(2)}, u32[]{:S(2)}) collective-permute-start(bf16[288,1152]{1,0:T(8,128)(2,1)} %refs_10_.1), channel_id=1, source_target_pairs={{0,8},{8,0},{16,24},{24,16},{1,9},{9,1},{17,25},{25,17},{2,10},{10... | collective-permute-start | bytes 1990664 | tf_op jit(solution)/shard_map/ppermute | solution.py:975
  52.4 3.6 collective-permute-start.6
  57.9 24.9 %collective-permute-start.7 = (f32[1,64,864]{2,1,0:T(8,128)S(1)}, f32[1,64,864]{2,1,0:T(8,128)S(1)}, u32[]{:S(2)}, u32[]{:S(2)}) collective-permute-start(f32[1,64,864]{2,1,0:T(8,128)S(1)} %fusion.13), channel_id=1, source_target_pairs={{0,1},{1,0},{2,3},{3,2},{4,5},{5,4},{6,7},{7,6},{8,9},{9,8},{10,11... | collective-permute-start | bytes 663560 | tf_op jit(solution)/shard_map/ppermute | solution.py:808
  83.4 12.3 %collective-permute-start.8 = (f32[2,64,864]{2,1,0:T(8,128)S(1)}, f32[2,64,864]{2,1,0:T(8,128)S(1)}, u32[]{:S(2)}, u32[]{:S(2)}) collective-permute-start(f32[2,64,864]{2,1,0:T(8,128)S(1)} %pad_maximum_fusion.4), channel_id=1, source_target_pairs={{0,2},{1,3},{2,0},{3,1},{4,6},{5,7},{6,4},{7,5},{8,10},{9,11},{10,... | collective-permute-start | bytes 1327112 | tf_op jit(solution)/shard_map/ppermute | solution.py:808
  86.0 16.7 %collective-permute-start.11 = (bf16[288,1152]{1,0:T(8,128)(2,1)S(1)}, bf16[288,1152]{1,0:T(8,128)(2,1)S(1)}, u32[]{:S(2)}, u32[]{:S(2)}) collective-permute-start(bf16[288,1152]{1,0:T(8,128)(2,1)S(1)} %broadcast_select_fusion), channel_id=1, source_target_pairs={{0,16},{8,24},{16,0},{24,8},{1,17},{9,25},{17,1},{25,9},{2,18},{10... | collective-permute-start | bytes 1990664 | tf_op jit(solution)/shard_map/ppermute | solution.py:951
  96.0 17.3 %collective-permute-start.9 = (f32[4,24,864]{2,1,0:T(8,128)S(1)}, f32[4,24,864]{2,1,0:T(8,128)S(1)}, u32[]{:S(2)}, u32[]{:S(2)}) collective-permute-start(f32[4,24,864]{2,1,0:T(8,128)S(1)} %constant_dynamic-slice_fusion.7), channel_id=1, source_target_pairs={{0,4},{1,5},{2,6},{3,7},{4,0},{5,1},{6,2},{7,3},{8,12},{9,13},{10,... | collective-permute-start | bytes 995336 | tf_op jit(solution)/shard_map/ppermute | solution.py:956
  102.7 11.2 %copy-start.9 = (bf16[288,1152]{1,0:T(8,128)(2,1)}, bf16[288,1152]{1,0:T(8,128)(2,1)S(1)}, u32[]{:S(2)}) copy-start(bf16[288,1152]{1,0:T(8,128)(2,1)S(1)} %collective-permute-done.11.refs_9_.refs_12_) | copy-start | bytes 1990660
  102.7 69.0 %collective-permute-start.12 = (bf16[288,1152]{1,0:T(8,128)(2,1)S(1)}, bf16[288,1152]{1,0:T(8,128)(2,1)S(1)}, u32[]{:S(2)}, u32[]{:S(2)}) collective-permute-start(bf16[288,1152]{1,0:T(8,128)(2,1)S(1)} %collective-permute-done.11.refs_9_.refs_12_), channel_id=1, source_target_pairs={{0,8},{8,0},{16,24},{24,16},{1,9},{9,1},{17,25},{25,17},{2,10},{10... | collective-permute-start | bytes 1990664 | tf_op jit(solution)/shard_map/ppermute | solution.py:976
  294.1 5.7 copy-start.22
  294.2 181.7 %reduce-scatter.12.cloned.1.call-start = ((), (), s32[]{:S(2)}) async-start(), calls=%async_computation.9 | async-start | bytes 7372800
  294.2 37.8 %collective-permute-start.17 = (bf16[2,2,4,288,576]{4,3,2,1,0:T(8,128)(2,1)}, bf16[2,2,4,288,576]{4,3,2,1,0:T(8,128)(2,1)}, u32[]{:S(2)}, u32[]{:S(2)}) collective-permute-start(bf16[2,2,4,288,576]{4,3,2,1,0:T(8,128)(2,1)} %get-tuple-element.72), channel_id=1, source_target_pairs={{0,8},{8,0},{16,24},{24,16},{1,9},{9,1},{17,25},{25,17},{2,10},{10... | collective-permute-start | bytes 15925256 | tf_op jit(solution)/shard_map/ppermute | solution.py:864
  297.9 6.4 %collective-permute-start.14 = (bf16[64,1152]{1,0:T(8,128)(2,1)S(1)}, bf16[64,1152]{1,0:T(8,128)(2,1)S(1)}, u32[]{:S(2)}, u32[]{:S(2)}) collective-permute-start(bf16[64,1152]{1,0:T(8,128)(2,1)S(1)} %broadcast_select_fusion.5), channel_id=1, source_target_pairs={{0,8},{8,0},{16,24},{24,16},{1,9},{9,1},{17,25},{25,17},{2,10},{10... | collective-permute-start | bytes 442376 | tf_op jit(solution)/shard_map/ppermute | solution.py:978
  298.3 6.7 %collective-permute-start.15 = (bf16[64,1152]{1,0:T(8,128)(2,1)S(1)}, bf16[64,1152]{1,0:T(8,128)(2,1)S(1)}, u32[]{:S(2)}, u32[]{:S(2)}) collective-permute-start(bf16[64,1152]{1,0:T(8,128)(2,1)S(1)} %broadcast_select_fusion.5), channel_id=1, source_target_pairs={{0,16},{8,24},{16,0},{24,8},{1,17},{9,25},{17,1},{25,9},{2,18},{10... | collective-permute-start | bytes 442376 | tf_op jit(solution)/shard_map/ppermute | solution.py:978
  298.4 8.3 %collective-permute-start.16 = (bf16[64,1152]{1,0:T(8,128)(2,1)S(1)}, bf16[64,1152]{1,0:T(8,128)(2,1)S(1)}, u32[]{:S(2)}, u32[]{:S(2)}) collective-permute-start(bf16[64,1152]{1,0:T(8,128)(2,1)S(1)} %broadcast_select_fusion.5), channel_id=1, source_target_pairs={{0,24},{8,16},{16,8},{24,0},{1,25},{9,17},{17,9},{25,1},{2,26},{10... | collective-permute-start | bytes 442376 | tf_op jit(solution)/shard_map/ppermute | solution.py:978
  341.0 219.8 %reduce-scatter.10.cloned.1.call-start = ((), (), s32[]{:S(2)}) async-start(), calls=%async_computation.8 | async-start | bytes 7372800
  341.0 36.4 %copy-start.34 = (s32[4]{0:T(128)S(1)}, s32[4]{0:T(128)}, u32[]{:S(2)}) copy-start(s32[4]{0:T(128)} %copy-done.33) | copy-start | bytes 52
  341.1 36.4 %copy-start.36 = (s32[4]{0:T(128)S(1)}, s32[4]{0:T(128)}, u32[]{:S(2)}) copy-start(s32[4]{0:T(128)} %copy-done.35) | copy-start | bytes 52
  372.2 48.8 %collective-permute-start.18 = (bf16[192,2304]{1,0:T(8,128)(2,1)}, bf16[192,2304]{1,0:T(8,128)(2,1)S(1)}, u32[]{:S(2)}, u32[]{:S(2)}) collective-permute-start(bf16[192,2304]{1,0:T(8,128)(2,1)} %get-tuple-element.78), channel_id=1, source_target_pairs={{0,1},{1,2},{2,3},{3,4},{4,5},{5,6},{6,7},{8,9},{9,10},{10,11},{11... | collective-permute-start | bytes 2654216 | tf_op jit(solution)/shard_map/ppermute | solution.py:1009
  376.2 44.9 %collective-permute-start.19 = (bf16[192,2304]{1,0:T(8,128)(2,1)}, bf16[192,2304]{1,0:T(8,128)(2,1)S(1)}, u32[]{:S(2)}, u32[]{:S(2)}) collective-permute-start(bf16[192,2304]{1,0:T(8,128)(2,1)} %get-tuple-element.79), channel_id=1, source_target_pairs={{1,0},{2,1},{3,2},{4,3},{5,4},{6,5},{7,6},{9,8},{10,9},{11,10},{12... | collective-permute-start | bytes 2654216 | tf_op jit(solution)/shard_map/ppermute | solution.py:1008
  380.1 47.5 %collective-permute-start.20 = (bf16[2,144,1152]{2,1,0:T(8,128)(2,1)}, bf16[2,144,1152]{2,1,0:T(8,128)(2,1)}, u32[]{:S(2)}, u32[]{:S(2)}) collective-permute-start(bf16[2,144,1152]{2,1,0:T(8,128)(2,1)} %dynamic-slice_bitcast_fusion.2), channel_id=1, source_target_pairs={{0,2},{1,3},{2,0},{3,1},{4,6},{5,7},{6,4},{7,5},{8,10},{9,11},{10,... | collective-permute-start | bytes 1990664 | tf_op jit(solution)/shard_map/ppermute | solution.py:864
  421.1 6.5 %copy-start.4 = (bf16[1,4,144,1152]{3,2,1,0:T(8,128)(2,1)S(1)}, bf16[1,4,144,1152]{3,2,1,0:T(8,128)(2,1)}, u32[]{:S(2)}) copy-start(bf16[1,4,144,1152]{3,2,1,0:T(8,128)(2,1)} %reduce-scatter.8.cloned.1.call-done) | copy-start | bytes 3981316
  455.0 9.9 %collective-permute-start.21 = (bf16[2,2,4,288,576]{4,3,2,1,0:T(8,128)(2,1)}, bf16[2,2,4,288,576]{4,3,2,1,0:T(8,128)(2,1)S(1)}, u32[]{:S(2)}, u32[]{:S(2)}) collective-permute-start(bf16[2,2,4,288,576]{4,3,2,1,0:T(8,128)(2,1)} %get-tuple-element.83.refs_9_), channel_id=1, source_target_pairs={{0,8},{8,0},{16,24},{24,16},{1,9},{9,1},{17,25},{25,17},{2,10},{10... | collective-permute-start | bytes 15925256 | tf_op jit(solution)/shard_map/ppermute | solution.py:864
  477.9 46.4 %collective-permute-start.32 = (bf16[2,288,576]{2,1,0:T(8,128)(2,1)}, bf16[2,288,576]{2,1,0:T(8,128)(2,1)}, u32[]{:S(2)}, u32[]{:S(2)}) collective-permute-start(bf16[2,288,576]{2,1,0:T(8,128)(2,1)} %dynamic-slice_bitcast_fusion), channel_id=1, source_target_pairs={{0,2},{1,3},{2,0},{3,1},{4,6},{5,7},{6,4},{7,5},{8,10},{9,11},{10,... | collective-permute-start | bytes 1990664 | tf_op jit(solution)/shard_map/ppermute | solution.py:864
  500.7 6.0 copy-start.3
  503.4 18.6 %collective-permute-start.23 = (bf16[134,864]{1,0:T(8,128)(2,1)S(1)}, bf16[134,864]{1,0:T(8,128)(2,1)S(1)}, u32[]{:S(2)}, u32[]{:S(2)}) collective-permute-start(bf16[134,864]{1,0:T(8,128)(2,1)S(1)} %pad_maximum_fusion.8), channel_id=1, source_target_pairs={{0,1},{1,0},{2,3},{3,2},{4,5},{5,4},{6,7},{7,6},{8,9},{9,8},{10,11... | collective-permute-start | bytes 694664 | tf_op jit(solution)/shard_map/ppermute | solution.py:864
  507.4 37.6 %collective-permute-start.34 = (bf16[1,144,1152]{2,1,0:T(8,128)(2,1)}, bf16[1,144,1152]{2,1,0:T(8,128)(2,1)}, u32[]{:S(2)}, u32[]{:S(2)}) collective-permute-start(bf16[1,144,1152]{2,1,0:T(8,128)(2,1)} %dynamic-slice_convert_fusion.2), channel_id=1, source_target_pairs={{0,4},{1,5},{2,6},{3,7},{4,0},{5,1},{6,2},{7,3},{8,12},{9,13},{10,... | collective-permute-start | bytes 995336 | tf_op jit(solution)/shard_map/ppermute | solution.py:864
  523.4 21.0 %collective-permute-start.24 = (bf16[166,864]{1,0:T(8,128)(2,1)S(1)}, bf16[166,864]{1,0:T(8,128)(2,1)S(1)}, u32[]{:S(2)}, u32[]{:S(2)}) collective-permute-start(bf16[166,864]{1,0:T(8,128)(2,1)S(1)} %pad_maximum_fusion.6), channel_id=1, source_target_pairs={{0,2},{1,3},{2,0},{3,1},{4,6},{5,7},{6,4},{7,5},{8,10},{9,11},{10,... | collective-permute-start | bytes 860552 | tf_op jit(solution)/shard_map/ppermute | solution.py:864
  525.9 21.0 %copy-start.5 = (f32[2,288,576]{2,1,0:T(8,128)}, f32[2,288,576]{2,1,0:T(8,128)S(1)}, u32[]{:S(2)}) copy-start(f32[2,288,576]{2,1,0:T(8,128)S(1)} %convert_add_fusion) | copy-start | bytes 3981316
  525.9 37.7 %collective-permute-start.33 = (bf16[1,288,576]{2,1,0:T(8,128)(2,1)S(1)}, bf16[1,288,576]{2,1,0:T(8,128)(2,1)}, u32[]{:S(2)}, u32[]{:S(2)}) collective-permute-start(bf16[1,288,576]{2,1,0:T(8,128)(2,1)S(1)} %dynamic-slice_convert_fusion), channel_id=1, source_target_pairs={{0,4},{1,5},{2,6},{3,7},{4,0},{5,1},{6,2},{7,3},{8,12},{9,13},{10,... | collective-permute-start | bytes 995336 | tf_op jit(solution)/shard_map/ppermute | solution.py:864
  544.6 16.1 %collective-permute-start.25 = (bf16[102,864]{1,0:T(8,128)(2,1)S(1)}, bf16[102,864]{1,0:T(8,128)(2,1)S(1)}, u32[]{:S(2)}, u32[]{:S(2)}) collective-permute-start(bf16[102,864]{1,0:T(8,128)(2,1)S(1)} %pad_maximum_fusion.11), channel_id=1, source_target_pairs={{0,4},{1,5},{2,6},{3,7},{4,0},{5,1},{6,2},{7,3},{8,12},{9,13},{10,... | collective-permute-start | bytes 528776 | tf_op jit(solution)/shard_map/ppermute | solution.py:864
  563.5 6.5 %copy-start.7 = (bf16[1152,864]{1,0:T(8,128)(2,1)S(1)}, bf16[1152,864]{1,0:T(8,128)(2,1)}, u32[]{:S(2)}) copy-start(bf16[1152,864]{1,0:T(8,128)(2,1)} %all-gather.11.cloned.1.call-done.refs_17_) | copy-start | bytes 5971972
  563.5 6.5 %copy-start.13 = (bf16[1,64,1152]{2,1,0:T(8,128)(2,1)S(1)}, bf16[1,64,1152]{2,1,0:T(8,128)(2,1)}, u32[]{:S(2)}) copy-start(bf16[1,64,1152]{2,1,0:T(8,128)(2,1)} %param.16) | copy-start | bytes 442372
  563.5 6.5 %copy-start.24 = (bf16[102,864]{1,0:T(8,128)(2,1)S(1)}, bf16[102,864]{1,0:T(8,128)(2,1)}, u32[]{:S(2)}) copy-start(bf16[102,864]{1,0:T(8,128)(2,1)} %copy-done.23) | copy-start | bytes 528772
  563.5 3.9 collective-permute-start.29
  566.8 19.1 %collective-permute-start.22 = (bf16[2,288,576]{2,1,0:T(8,128)(2,1)}, bf16[2,288,576]{2,1,0:T(8,128)(2,1)}, u32[]{:S(2)}, u32[]{:S(2)}) collective-permute-start(bf16[2,288,576]{2,1,0:T(8,128)(2,1)} %dynamic-slice_bitcast_fusion.1), channel_id=1, source_target_pairs={{0,2},{1,3},{2,0},{3,1},{4,6},{5,7},{6,4},{7,5},{8,10},{9,11},{10,... | collective-permute-start | bytes 1990664 | tf_op jit(solution)/shard_map/ppermute | solution.py:864
  567.6 10.4 %copy-start.25 = (bf16[64,288]{1,0:T(8,128)(2,1)S(1)}, bf16[64,288]{1,0:T(8,128)(2,1)}, u32[]{:S(2)}) copy-start(bf16[64,288]{1,0:T(8,128)(2,1)} %get-tuple-element.161) | copy-start | bytes 110596
  567.6 10.0 %collective-permute-start.30 = (bf16[166,864]{1,0:T(8,128)(2,1)S(1)}, bf16[166,864]{1,0:T(8,128)(2,1)S(1)}, u32[]{:S(2)}, u32[]{:S(2)}) collective-permute-start(bf16[166,864]{1,0:T(8,128)(2,1)S(1)} %pad_maximum_fusion.7), channel_id=1, source_target_pairs={{0,16},{8,24},{16,0},{24,8},{1,17},{9,25},{17,1},{25,9},{2,18},{10... | collective-permute-start | bytes 860552 | tf_op jit(solution)/shard_map/ppermute | solution.py:864
  572.0 18.3 %collective-permute-start.26 = (f32[4,8,1152]{2,1,0:T(8,128)S(1)}, f32[4,8,1152]{2,1,0:T(8,128)S(1)}, u32[]{:S(2)}, u32[]{:S(2)}) collective-permute-start(f32[4,8,1152]{2,1,0:T(8,128)S(1)} %dynamic-slice_bitcast_fusion.3), channel_id=1, source_target_pairs={{0,1},{1,0},{2,3},{3,2},{4,5},{5,4},{6,7},{7,6},{8,9},{9,8},{10,11... | collective-permute-start | bytes 442376 | tf_op jit(solution)/shard_map/ppermute | solution.py:864
  577.9 12.4 %copy-start.17 = (f32[64,1152]{1,0:T(8,128)S(1)}, f32[64,1152]{1,0:T(8,128)}, u32[]{:S(2)}) copy-start(f32[64,1152]{1,0:T(8,128)} %copy-done.16) | copy-start | bytes 884740
  590.4 4.4 collective-permute-start.27
  592.9 26.7 %copy-start.1 = (bf16[288,4608]{1,0:T(8,128)(2,1)S(1)}, bf16[288,4608]{1,0:T(8,128)(2,1)}, u32[]{:S(2)}) copy-start(bf16[288,4608]{1,0:T(8,128)(2,1)} %param.24) | copy-start | bytes 7962628
  594.9 4.9 collective-permute-start.28
  598.3 18.3 %collective-permute-start.31 = (bf16[1,288,576]{2,1,0:T(8,128)(2,1)S(1)}, bf16[1,288,576]{2,1,0:T(8,128)(2,1)S(1)}, u32[]{:S(2)}, u32[]{:S(2)}) collective-permute-start(bf16[1,288,576]{2,1,0:T(8,128)(2,1)S(1)} %dynamic-slice_convert_fusion.1), channel_id=1, source_target_pairs={{0,4},{1,5},{2,6},{3,7},{4,0},{5,1},{6,2},{7,3},{8,12},{9,13},{10,... | collective-permute-start | bytes 995336 | tf_op jit(solution)/shard_map/ppermute | solution.py:864
  (17 other events, 48.9 us)
Sparse Core Ops, SparseCore 0:
  10.5 79.3 all-gather.4
  91.8 63.5 all-gather.6
  157.3 63.8 all-gather.8
  222.6 22.3 all-gather.10
  294.3 83.6 reduce-scatter.7
  380.8 91.5 reduce-scatter.11
  475.4 82.0 reduce-scatter.9
